TPU v7x, 32 devices: a whole 2x2x4 slice. The times are simulated.
32 devices in a mesh: section: 4 (over y, x), expert: 8 (over z, core).
Axes of the slice: x: 2, y: 2, z: 4, core: 2. Of those that a mesh axis runs over, the one named last changes fastest.
Arguments:
- fwd_act: bfloat16 [4, 32, 3584], P('section', 'expert'), may hold values from -6 to 6
- fwd_enter: bfloat16 [32, 3584], P('expert'), may hold values from -6 to 6
- bwd_grad: bfloat16 [4, 32, 3584], P('section', 'expert'), may hold values from -6 to 6
- bwd_enter: bfloat16 [32, 3584], P('expert'), may hold values from -6 to 6
- w_in: bfloat16 [4, 8, 3584, 2048], P('section', 'expert'), may hold values from -0.09375 to 0.09375
- w_out: bfloat16 [4, 8, 1024, 3584], P('section', 'expert'), may hold values from -0.1875 to 0.1875
- fwd_route: int32 [2, 4, 32, 2], P(None, 'section', 'expert'), may hold values from 0 to 7, all different within a row; in each aligned block of 4 rows (0 to 3, 4 to 7, ..., all dimensions but the last counted through in order) at most 2 rows name the same one
- fwd_gate: float32 [2, 4, 32, 2], P(None, 'section', 'expert'), may hold values from 0.2 to 2
- bwd_route: int32 [2, 4, 32, 2], P(None, 'section', 'expert'), may hold values from 0 to 7, all different within a row; in each aligned block of 4 rows (0 to 3, 4 to 7, ..., all dimensions but the last counted through in order) at most 2 rows name the same one
- bwd_gate: float32 [2, 4, 32, 2], P(None, 'section', 'expert'), may hold values from 0.2 to 2
- saved_pre: float32 [2, 4, 8, 16, 2048], P(None, 'section', 'expert'), may hold values from -6 to 6
Outputs:
- fwd_out: bfloat16 [2, 4, 32, 3584], P(None, 'section', 'expert')
- bwd_out: bfloat16 [2, 4, 32, 3584], P(None, 'section', 'expert')
Inputs may be any that keep to these rules, and one draw needn't show every extreme that they name: `fwd_route`: each token names 2 different experts. Within the 4 tokens of one index of expert at one tick and section, no expert is named by more than 2 routes, and some such block reaches 2. `bwd_route`: as for fwd_route.
All inputs are finite; a program needn't handle non-finite values.
Results may differ from a plain program's by a relative error of at most 0.019.
Values may be sent and summed in bfloat16 or wider, within the bound.
No kernel may reach another device: no remote copies, remote signals or barrier semaphores. Data moves between devices by JAX's collectives and lax.ppermute only.
A program may use at most 64 MiB of HBM per device.

v0:
```python
import jax
import jax.numpy as jnp
from jax import lax
from jax.sharding import PartitionSpec as P

FF = 1024
TICKS = 2


def padded_2(array, sides, width):
    for axis, dim in sides:
        devices, length = (lax.axis_size(axis), array.shape[dim])
        up = [(i, (i + 1) % devices) for i in range(devices - 1)]
        down = [(j, i) for i, j in up]
        last = lax.slice_in_dim(array, length - width, length, axis=dim)
        first = lax.slice_in_dim(array, 0, width, axis=dim)
        before = lax.ppermute(last, axis, up)
        after = lax.ppermute(first, axis, down)
        array = jnp.concatenate([before, array, after], axis=dim)
    return array


def route_tables(routing, weights, per_expert, experts):
    token_total, top_total = routing.shape
    route_total = token_total * top_total
    flat_route = routing.reshape(route_total)
    positions = jnp.arange(route_total, dtype=jnp.int32)
    same_expert = flat_route[:, None] == flat_route[None, :]
    earlier = positions[None, :] < positions[:, None]
    route_rank = jnp.sum((same_expert & earlier).astype(jnp.int32), axis=1)
    slot_index = flat_route * per_expert + route_rank
    slot_onehot = (
        slot_index[:, None] == jnp.arange(experts * per_expert, dtype=jnp.int32)[None, :]
    ).astype(jnp.float32)
    token_onehot = (
        (positions // top_total)[:, None] == jnp.arange(token_total, dtype=jnp.int32)[None, :]
    ).astype(jnp.float32)
    select = jnp.dot(slot_onehot.T, token_onehot, precision=lax.Precision.HIGHEST)
    weighted = token_onehot * weights.reshape(route_total)[:, None]
    combine = jnp.dot(weighted.T, slot_onehot, precision=lax.Precision.HIGHEST)
    return (select, combine)


def spread(tokens, select, per_expert, experts, slice_count):
    model_width = tokens.shape[1]
    placed = jnp.dot(
        select.astype(jnp.bfloat16), tokens, preferred_element_type=jnp.float32
    ).astype(jnp.bfloat16)
    placed = jnp.broadcast_to(
        placed.reshape(experts, 1, per_expert, model_width),
        (experts, slice_count, per_expert, model_width),
    )
    return placed.reshape(experts * slice_count, per_expert, model_width)


def forward_expert(received, weight_in, weight_out):
    hidden_units = weight_out.shape[0]
    slot_rows = received.reshape(-1, received.shape[2])
    gate_up = jnp.dot(slot_rows, weight_in, preferred_element_type=jnp.float32)
    hidden = (jax.nn.silu(gate_up[:, :hidden_units]) * gate_up[:, hidden_units:]).astype(
        jnp.bfloat16
    )
    partial_value = jnp.dot(hidden, weight_out, preferred_element_type=jnp.float32).astype(
        jnp.bfloat16
    )
    return partial_value.reshape(received.shape)


def backward_expert(received, saved_slots, weight_in, weight_out):
    hidden_units = weight_out.shape[0]
    slot_rows = received.reshape(-1, received.shape[2])
    hidden_grad = lax.dot_general(
        slot_rows, weight_out, (((1,), (1,)), ((), ())), preferred_element_type=jnp.float32
    )
    gate_pre = saved_slots[:, :hidden_units]
    up_pre = saved_slots[:, hidden_units:]
    sigmoid_gate = jax.nn.sigmoid(gate_pre)
    activated = gate_pre * sigmoid_gate
    silu_slope = sigmoid_gate * (1.0 + gate_pre * (1.0 - sigmoid_gate))
    joined = jnp.concatenate(
        [hidden_grad * up_pre * silu_slope, hidden_grad * activated], axis=1
    ).astype(jnp.bfloat16)
    partial_value = lax.dot_general(
        joined, weight_in, (((1,), (1,)), ((), ())), preferred_element_type=jnp.float32
    ).astype(jnp.bfloat16)
    return partial_value.reshape(received.shape)


def collect(returned, tokens, combine, experts):
    summed = (
        returned.reshape(experts, -1, returned.shape[1], returned.shape[2])
        .astype(jnp.float32)
        .sum(axis=1)
    )
    summed = summed.reshape(-1, returned.shape[2])
    mixed = tokens.astype(jnp.float32) + jnp.dot(combine, summed, precision=lax.Precision.HIGHEST)
    return mixed.astype(jnp.bfloat16)


def shards(
    fwd_act,
    fwd_enter,
    bwd_grad,
    bwd_enter,
    w_in,
    w_out,
    fwd_route,
    fwd_gate,
    bwd_route,
    bwd_gate,
    saved_pre,
):
    device_total = lax.axis_size("expert")
    slice_count = FF // w_out.shape[2]
    experts = device_total // slice_count
    per_expert = saved_pre.shape[3] // device_total
    weight_in = w_in[0, 0]
    weight_out = w_out[0, 0]
    section_index = lax.axis_index("section")
    section_total = lax.axis_size("section")
    fwd_now = fwd_act[0]
    bwd_now = bwd_grad[0]
    fwd_list = []
    bwd_list = []
    for tick_index in range(TICKS):
        fwd_select, fwd_combine = route_tables(
            fwd_route[tick_index, 0], fwd_gate[tick_index, 0], per_expert, experts
        )
        bwd_select, bwd_combine = route_tables(
            bwd_route[tick_index, 0], bwd_gate[tick_index, 0], per_expert, experts
        )
        fwd_slots = spread(fwd_now, fwd_select, per_expert, experts, slice_count)
        bwd_slots = spread(bwd_now, bwd_select, per_expert, experts, slice_count)
        saved_slots = saved_pre[tick_index, 0, 0]
        fwd_recv, bwd_recv = (
            lax.all_to_all(fwd_slots, "expert", split_axis=0, concat_axis=0, tiled=True),
            lax.all_to_all(bwd_slots, "expert", split_axis=0, concat_axis=0, tiled=True),
        )
        fwd_part = forward_expert(fwd_recv, weight_in, weight_out)
        bwd_part = backward_expert(bwd_recv, saved_slots, weight_in, weight_out)
        fwd_back, bwd_back = (
            lax.all_to_all(fwd_part, "expert", split_axis=0, concat_axis=0, tiled=True),
            lax.all_to_all(bwd_part, "expert", split_axis=0, concat_axis=0, tiled=True),
        )
        fwd_next = collect(fwd_back, fwd_now, fwd_combine, experts)
        bwd_next = collect(bwd_back, bwd_now, bwd_combine, experts)
        fwd_list.append(fwd_next)
        bwd_list.append(bwd_next)
        if tick_index + 1 < TICKS:
            padded = padded_2(jnp.stack([bwd_next, fwd_next]), (("section", 0),), 1)
            from_below = padded[0]
            from_above = padded[3]
            fwd_now = jnp.where(section_index == 0, fwd_enter, from_below)
            bwd_now = jnp.where(section_index == section_total - 1, bwd_enter, from_above)
    return (jnp.stack(fwd_list)[:, None], jnp.stack(bwd_list)[:, None])


def solution(mesh):
    placed = (
        P("section", "expert", None),
        P("expert", None),
        P("section", "expert", None),
        P("expert", None),
        P("section", "expert", None, None),
        P("section", "expert", None, None),
        P(None, "section", "expert", None),
        P(None, "section", "expert", None),
        P(None, "section", "expert", None),
        P(None, "section", "expert", None),
        P(None, "section", "expert", None, None),
    )
    return jax.shard_map(
        shards,
        mesh=mesh,
        in_specs=placed,
        out_specs=(P(None, "section", "expert", None), P(None, "section", "expert", None)),
        check_vma=False,
    )
```

profile of v0, /device:TPU:0, one launch (start us, length us, event | category | flops | bytes accessed | tf_op | source)
XLA Modules:
  0.0 127.4 jit_solution(2900031922516332375)
XLA Ops:
  4.7 6.3 %all-to-all-start.4 = ((bf16[8,2,3584]{2,1,0:T(2,128)(2,1)}), bf16[8,2,3584]{2,1,0:T(2,128)(2,1)S(1)}, u32[]{:S(2)}, u32[]{:S(2)}) async-start(bf16[8,2,3584]{2,1,0:T(2,128)(2,1)} %reshape_reshape.14), calls=%async_computation.4 | async-start | bytes 229376 | tf_op jit(solution)/shard_map/all_to_all | solution.py:137
  11.0 1.6 %slice_bitcast_fusion = (f32[16,2048]{1,0:T(8,128)}, f32[16,2048]{1,0:T(8,128)S(1)}) fusion(f32[2,1,1,16,2048]{4,3,2,1,0:T(8,128)} %param.21), kind=kLoop, calls=%fused_computation.34 | loop fusion | bytes 524288 | tf_op jit(solution)/shard_map/squeeze | solution.py:134
  15.8 1.0 convolution_convert_fusion.3
  20.0 5.1 %all-to-all-start = ((bf16[8,2,3584]{2,1,0:T(2,128)(2,1)}), bf16[8,2,3584]{2,1,0:T(2,128)(2,1)S(1)}, u32[]{:S(2)}, u32[]{:S(2)}) async-start(bf16[8,2,3584]{2,1,0:T(2,128)(2,1)} %reshape_reshape.12), calls=%async_computation | async-start | bytes 229376 | tf_op jit(solution)/shard_map/all_to_all | solution.py:136
  25.2 5.1 %fusion.35 = (bf16[16,1024]{1,0:T(8,128)(2,1)S(1)}, bf16[16,1024]{1,0:T(8,128)(2,1)S(1)}) fusion(f32[16,2048]{1,0:T(8,128)S(1)} %get-tuple-element.9, bf16[16,3584]{1,0:T(8,128)(2,1)S(1)} %reshape.119, bf16[1,1,1024,3584]{3,2,1,0:T(8,128)(2,1)} %param.16), kind=kOutput, calls=%fused_computation.41 | convolution fusion | flops 117653504 | bytes 7651328 | tf_op jit(solution)/shard_map/dot_general | solution.py:72
  30.2 9.1 %fusion.22 = bf16[16,3584]{1,0:T(8,128)(2,1)S(1)} fusion(bf16[1,1,3584,2048]{3,2,1,0:T(8,128)(2,1)} %param.15, bf16[16,1024]{1,0:T(8,128)(2,1)S(1)} %get-tuple-element.13, bf16[16,1024]{1,0:T(8,128)(2,1)S(1)} %get-tuple-element.12), kind=kOutput, calls=%fused_computation.18 | convolution fusion | flops 235069440 | bytes 14860288 | tf_op jit(solution)/shard_map/dot_general | solution.py:83
  40.0 5.2 %all-to-all-start.5 = ((bf16[8,2,3584]{2,1,0:T(2,128)(2,1)}), bf16[8,2,3584]{2,1,0:T(2,128)(2,1)S(1)}, u32[]{:S(2)}, u32[]{:S(2)}) async-start(bf16[8,2,3584]{2,1,0:T(2,128)(2,1)} %reshape.120), calls=%async_computation.5 | async-start | bytes 229376 | tf_op jit(solution)/shard_map/all_to_all | solution.py:143
  45.3 7.3 %fusion.6 = f32[16,2048]{1,0:T(8,128)S(1)} fusion(bf16[16,3584]{1,0:T(8,128)(2,1)S(1)} %reshape.113, bf16[1,1,3584,2048]{3,2,1,0:T(8,128)(2,1)} %param.15), kind=kOutput, calls=%fused_computation.6 | convolution fusion | flops 234881024 | bytes 14925824 | tf_op jit(solution)/shard_map/dot_general | solution.py:59
  52.7 1.1 fusion.16
  54.4 5.1 %all-to-all-start.1 = ((bf16[8,2,3584]{2,1,0:T(2,128)(2,1)}), bf16[8,2,3584]{2,1,0:T(2,128)(2,1)S(1)}, u32[]{:S(2)}, u32[]{:S(2)}) async-start(bf16[8,2,3584]{2,1,0:T(2,128)(2,1)} %reshape.114), calls=%async_computation.1 | async-start | bytes 229376 | tf_op jit(solution)/shard_map/all_to_all | solution.py:142
  60.1 1.3 %collective-permute-start.1 = (bf16[1,4,3584]{2,1,0:T(4,128)(2,1)S(1)}, bf16[1,4,3584]{2,1,0:T(4,128)(2,1)S(1)}, u32[]{:S(2)}, u32[]{:S(2)}) collective-permute-start(bf16[1,4,3584]{2,1,0:T(4,128)(2,1)S(1)} %fusion.30), channel_id=1, source_target_pairs={{8,0},{16,8},{24,16},{9,1},{17,9},{25,17},{10,2},{18,10},{26,18},{... | collective-permute-start | bytes 86024 | tf_op jit(solution)/shard_map/ppermute | solution.py:18
  61.4 4.7 %all-to-all-done.1 = bf16[8,2,3584]{2,1,0:T(2,128)(2,1)S(1)} async-done(((bf16[8,2,3584]{2,1,0:T(2,128)(2,1)}), bf16[8,2,3584]{2,1,0:T(2,128)(2,1)S(1)}, u32[]{:S(2)}, u32[]{:S(2)}) %all-to-all-start.1) | async-done | bytes 114720 | tf_op jit(solution)/shard_map/all_to_all | solution.py:142
  67.1 3.4 %collective-permute-start = (bf16[1,4,3584]{2,1,0:T(4,128)(2,1)S(1)}, bf16[1,4,3584]{2,1,0:T(4,128)(2,1)S(1)}, u32[]{:S(2)}, u32[]{:S(2)}) collective-permute-start(bf16[1,4,3584]{2,1,0:T(4,128)(2,1)S(1)} %fusion.31), channel_id=1, source_target_pairs={{0,8},{8,16},{16,24},{1,9},{9,17},{17,25},{2,10},{10,18},{18,26},{... | collective-permute-start | bytes 86024 | tf_op jit(solution)/shard_map/ppermute | solution.py:17
  71.5 3.4 %all-to-all-start.6 = ((bf16[8,2,3584]{2,1,0:T(2,128)(2,1)}), bf16[8,2,3584]{2,1,0:T(2,128)(2,1)S(1)}, u32[]{:S(2)}, u32[]{:S(2)}) async-start(bf16[8,2,3584]{2,1,0:T(2,128)(2,1)} %reshape_reshape.15), calls=%async_computation.6 | async-start | bytes 229376 | tf_op jit(solution)/shard_map/all_to_all | solution.py:137
  74.9 1.0 convolution_convert_fusion.2
  76.5 4.8 %all-to-all-done.6 = bf16[8,2,3584]{2,1,0:T(2,128)(2,1)S(1)} async-done(((bf16[8,2,3584]{2,1,0:T(2,128)(2,1)}), bf16[8,2,3584]{2,1,0:T(2,128)(2,1)S(1)}, u32[]{:S(2)}, u32[]{:S(2)}) %all-to-all-start.6) | async-done | bytes 114720 | tf_op jit(solution)/shard_map/all_to_all | solution.py:137
  81.3 3.5 %all-to-all-start.2 = ((bf16[8,2,3584]{2,1,0:T(2,128)(2,1)}), bf16[8,2,3584]{2,1,0:T(2,128)(2,1)S(1)}, u32[]{:S(2)}, u32[]{:S(2)}) async-start(bf16[8,2,3584]{2,1,0:T(2,128)(2,1)} %reshape_reshape.13), calls=%async_computation.2 | async-start | bytes 229376 | tf_op jit(solution)/shard_map/all_to_all | solution.py:136
  85.0 5.1 %fusion.33 = (bf16[16,1024]{1,0:T(8,128)(2,1)S(1)}, bf16[16,1024]{1,0:T(8,128)(2,1)S(1)}) fusion(f32[16,2048]{1,0:T(8,128)S(1)} %copy-done, bf16[16,3584]{1,0:T(8,128)(2,1)S(1)} %reshape.122, bf16[1,1,1024,3584]{3,2,1,0:T(8,128)(2,1)} %param.16), kind=kOutput, calls=%fused_computation.38 | convolution fusion | flops 117653504 | bytes 7651328 | tf_op jit(solution)/shard_map/dot_general | solution.py:72
  90.1 9.1 %fusion.25 = bf16[16,3584]{1,0:T(8,128)(2,1)S(1)} fusion(bf16[1,1,3584,2048]{3,2,1,0:T(8,128)(2,1)} %param.15, bf16[16,1024]{1,0:T(8,128)(2,1)S(1)} %get-tuple-element.11, bf16[16,1024]{1,0:T(8,128)(2,1)S(1)} %get-tuple-element.10), kind=kOutput, calls=%fused_computation.19 | convolution fusion | flops 235069440 | bytes 14860288 | tf_op jit(solution)/shard_map/dot_general | solution.py:83
  99.8 5.0 %all-to-all-start.7 = ((bf16[8,2,3584]{2,1,0:T(2,128)(2,1)}), bf16[8,2,3584]{2,1,0:T(2,128)(2,1)S(1)}, u32[]{:S(2)}, u32[]{:S(2)}) async-start(bf16[8,2,3584]{2,1,0:T(2,128)(2,1)} %reshape.123), calls=%async_computation.7 | async-start | bytes 229376 | tf_op jit(solution)/shard_map/all_to_all | solution.py:143
  104.9 7.3 %fusion.4 = f32[16,2048]{1,0:T(8,128)S(1)} fusion(bf16[16,3584]{1,0:T(8,128)(2,1)S(1)} %reshape.116, bf16[1,1,3584,2048]{3,2,1,0:T(8,128)(2,1)} %param.15), kind=kOutput, calls=%fused_computation.4 | convolution fusion | flops 234881024 | bytes 14925824 | tf_op jit(solution)/shard_map/dot_general | solution.py:59
  112.3 1.1 fusion.19
  114.0 5.1 %all-to-all-start.3 = ((bf16[8,2,3584]{2,1,0:T(2,128)(2,1)}), bf16[8,2,3584]{2,1,0:T(2,128)(2,1)S(1)}, u32[]{:S(2)}, u32[]{:S(2)}) async-start(bf16[8,2,3584]{2,1,0:T(2,128)(2,1)} %reshape.117), calls=%async_computation.3 | async-start | bytes 229376 | tf_op jit(solution)/shard_map/all_to_all | solution.py:142
  120.8 4.9 %all-to-all-done.3 = bf16[8,2,3584]{2,1,0:T(2,128)(2,1)S(1)} async-done(((bf16[8,2,3584]{2,1,0:T(2,128)(2,1)}), bf16[8,2,3584]{2,1,0:T(2,128)(2,1)S(1)}, u32[]{:S(2)}, u32[]{:S(2)}) %all-to-all-start.3) | async-done | bytes 114720 | tf_op jit(solution)/shard_map/all_to_all | solution.py:142
  (97 shorter events, 19.8 us)
Async XLA Ops:
  4.7 15.3 %all-to-all-start.4 = ((bf16[8,2,3584]{2,1,0:T(2,128)(2,1)}), bf16[8,2,3584]{2,1,0:T(2,128)(2,1)S(1)}, u32[]{:S(2)}, u32[]{:S(2)}) async-start(bf16[8,2,3584]{2,1,0:T(2,128)(2,1)} %reshape_reshape.14), calls=%async_computation.4 | async-start | bytes 229376 | tf_op jit(solution)/shard_map/all_to_all | solution.py:137
  20.0 20.0 %all-to-all-start = ((bf16[8,2,3584]{2,1,0:T(2,128)(2,1)}), bf16[8,2,3584]{2,1,0:T(2,128)(2,1)S(1)}, u32[]{:S(2)}, u32[]{:S(2)}) async-start(bf16[8,2,3584]{2,1,0:T(2,128)(2,1)} %reshape_reshape.12), calls=%async_computation | async-start | bytes 229376 | tf_op jit(solution)/shard_map/all_to_all | solution.py:136
  39.3 13.4 %slice-start = ((s8[7340032]{0:T(1024)(128)(4,1)}), s8[3145728]{0:T(1024)(128)(4,1)S(1)}, s32[]{:S(2)}) async-start(s8[7340032]{0:T(1024)(128)(4,1)} %bitcast.84), calls=%async_computation.8 | async-start | bytes 6291456
  40.0 14.4 %all-to-all-start.5 = ((bf16[8,2,3584]{2,1,0:T(2,128)(2,1)}), bf16[8,2,3584]{2,1,0:T(2,128)(2,1)S(1)}, u32[]{:S(2)}, u32[]{:S(2)}) async-start(bf16[8,2,3584]{2,1,0:T(2,128)(2,1)} %reshape.120), calls=%async_computation.5 | async-start | bytes 229376 | tf_op jit(solution)/shard_map/all_to_all | solution.py:143
  45.3 7.4 %slice-start.1 = ((s8[7340032]{0:T(1024)(128)(4,1)}), s8[4194304]{0:T(1024)(128)(4,1)S(1)}, s32[]{:S(2)}) async-start(s8[7340032]{0:T(1024)(128)(4,1)} %bitcast.84), calls=%async_computation.9 | async-start | bytes 8388608
  45.3 14.5 %copy-start.3 = (bf16[1,4,3584]{2,1,0:T(4,128)(2,1)S(1)}, bf16[1,4,3584]{2,1,0:T(4,128)(2,1)}, u32[]{:S(2)}) copy-start(bf16[1,4,3584]{2,1,0:T(4,128)(2,1)} %param.13) | copy-start | bytes 86020
  45.3 39.6 %copy-start = (f32[16,2048]{1,0:T(8,128)S(1)}, f32[16,2048]{1,0:T(8,128)}, u32[]{:S(2)}) copy-start(f32[16,2048]{1,0:T(8,128)} %get-tuple-element.8) | copy-start | bytes 393220
  54.4 11.7 %all-to-all-start.1 = ((bf16[8,2,3584]{2,1,0:T(2,128)(2,1)}), bf16[8,2,3584]{2,1,0:T(2,128)(2,1)S(1)}, u32[]{:S(2)}, u32[]{:S(2)}) async-start(bf16[8,2,3584]{2,1,0:T(2,128)(2,1)} %reshape.114), calls=%async_computation.1 | async-start | bytes 229376 | tf_op jit(solution)/shard_map/all_to_all | solution.py:142
  60.1 24.9 %copy-start.1 = (bf16[1,4,3584]{2,1,0:T(4,128)(2,1)}, bf16[1,4,3584]{2,1,0:T(4,128)(2,1)S(1)}, u32[]{:S(2)}) copy-start(bf16[1,4,3584]{2,1,0:T(4,128)(2,1)S(1)} %fusion.30) | copy-start | bytes 86020
  60.1 10.4 %collective-permute-start.1 = (bf16[1,4,3584]{2,1,0:T(4,128)(2,1)S(1)}, bf16[1,4,3584]{2,1,0:T(4,128)(2,1)S(1)}, u32[]{:S(2)}, u32[]{:S(2)}) collective-permute-start(bf16[1,4,3584]{2,1,0:T(4,128)(2,1)S(1)} %fusion.30), channel_id=1, source_target_pairs={{8,0},{16,8},{24,16},{9,1},{17,9},{25,17},{10,2},{18,10},{26,18},{... | collective-permute-start | bytes 86024 | tf_op jit(solution)/shard_map/ppermute | solution.py:18
  67.1 7.7 %collective-permute-start = (bf16[1,4,3584]{2,1,0:T(4,128)(2,1)S(1)}, bf16[1,4,3584]{2,1,0:T(4,128)(2,1)S(1)}, u32[]{:S(2)}, u32[]{:S(2)}) collective-permute-start(bf16[1,4,3584]{2,1,0:T(4,128)(2,1)S(1)} %fusion.31), channel_id=1, source_target_pairs={{0,8},{8,16},{16,24},{1,9},{9,17},{17,25},{2,10},{10,18},{18,26},{... | collective-permute-start | bytes 86024 | tf_op jit(solution)/shard_map/ppermute | solution.py:17
  70.5 14.4 %copy-start.7 = (bf16[1,4,3584]{2,1,0:T(4,128)(2,1)}, bf16[1,4,3584]{2,1,0:T(4,128)(2,1)S(1)}, u32[]{:S(2)}) copy-start(bf16[1,4,3584]{2,1,0:T(4,128)(2,1)S(1)} %collective-permute-done.1) | copy-start | bytes 86020
  71.5 9.9 %all-to-all-start.6 = ((bf16[8,2,3584]{2,1,0:T(2,128)(2,1)}), bf16[8,2,3584]{2,1,0:T(2,128)(2,1)S(1)}, u32[]{:S(2)}, u32[]{:S(2)}) async-start(bf16[8,2,3584]{2,1,0:T(2,128)(2,1)} %reshape_reshape.15), calls=%async_computation.6 | async-start | bytes 229376 | tf_op jit(solution)/shard_map/all_to_all | solution.py:137
  74.8 10.1 %copy-start.6 = (bf16[1,4,3584]{2,1,0:T(4,128)(2,1)}, bf16[1,4,3584]{2,1,0:T(4,128)(2,1)S(1)}, u32[]{:S(2)}) copy-start(bf16[1,4,3584]{2,1,0:T(4,128)(2,1)S(1)} %collective-permute-done) | copy-start | bytes 86020
  81.3 18.5 %all-to-all-start.2 = ((bf16[8,2,3584]{2,1,0:T(2,128)(2,1)}), bf16[8,2,3584]{2,1,0:T(2,128)(2,1)S(1)}, u32[]{:S(2)}, u32[]{:S(2)}) async-start(bf16[8,2,3584]{2,1,0:T(2,128)(2,1)} %reshape_reshape.13), calls=%async_computation.2 | async-start | bytes 229376 | tf_op jit(solution)/shard_map/all_to_all | solution.py:136
  99.1 13.1 %slice-start.2 = ((s8[7340032]{0:T(1024)(128)(4,1)}), s8[3145728]{0:T(1024)(128)(4,1)S(1)}, s32[]{:S(2)}) async-start(s8[7340032]{0:T(1024)(128)(4,1)} %bitcast.86), calls=%async_computation.10 | async-start | bytes 6291456
  99.8 14.2 %all-to-all-start.7 = ((bf16[8,2,3584]{2,1,0:T(2,128)(2,1)}), bf16[8,2,3584]{2,1,0:T(2,128)(2,1)S(1)}, u32[]{:S(2)}, u32[]{:S(2)}) async-start(bf16[8,2,3584]{2,1,0:T(2,128)(2,1)} %reshape.123), calls=%async_computation.7 | async-start | bytes 229376 | tf_op jit(solution)/shard_map/all_to_all | solution.py:143
  104.9 7.4 %slice-start.3 = ((s8[7340032]{0:T(1024)(128)(4,1)}), s8[4194304]{0:T(1024)(128)(4,1)S(1)}, s32[]{:S(2)}) async-start(s8[7340032]{0:T(1024)(128)(4,1)} %bitcast.86), calls=%async_computation.11 | async-start | bytes 8388608
  104.9 14.3 %copy-start.4 = (bf16[4,3584]{1,0:T(4,128)(2,1)S(1)}, bf16[4,3584]{1,0:T(4,128)(2,1)}, u32[]{:S(2)}) copy-start(bf16[4,3584]{1,0:T(4,128)(2,1)} %param.14) | copy-start | bytes 86020
  104.9 14.3 %copy-start.9 = (f32[4,16]{1,0:T(4,128)S(1)}, f32[4,16]{1,0:T(4,128)}, u32[]{:S(2)}) copy-start(f32[4,16]{1,0:T(4,128)} %fusion.52) | copy-start | bytes 772
  104.9 15.3 %copy-start.2 = (bf16[1,4,3584]{2,1,0:T(4,128)(2,1)S(1)}, bf16[1,4,3584]{2,1,0:T(4,128)(2,1)}, u32[]{:S(2)}) copy-start(bf16[1,4,3584]{2,1,0:T(4,128)(2,1)} %copy-done.1) | copy-start | bytes 86020
  104.9 20.8 %copy-start.5 = (bf16[4,3584]{1,0:T(4,128)(2,1)S(1)}, bf16[4,3584]{1,0:T(4,128)(2,1)}, u32[]{:S(2)}) copy-start(bf16[4,3584]{1,0:T(4,128)(2,1)} %param.12) | copy-start | bytes 86020
  104.9 20.8 %copy-start.8 = (f32[4,16]{1,0:T(4,128)S(1)}, f32[4,16]{1,0:T(4,128)}, u32[]{:S(2)}) copy-start(f32[4,16]{1,0:T(4,128)} %fusion.56) | copy-start | bytes 772
  114.0 11.7 %all-to-all-start.3 = ((bf16[8,2,3584]{2,1,0:T(2,128)(2,1)}), bf16[8,2,3584]{2,1,0:T(2,128)(2,1)S(1)}, u32[]{:S(2)}, u32[]{:S(2)}) async-start(bf16[8,2,3584]{2,1,0:T(2,128)(2,1)} %reshape.117), calls=%async_computation.3 | async-start | bytes 229376 | tf_op jit(solution)/shard_map/all_to_all | solution.py:142
where the time goes:
time: 129 us; the launch traced here: 127 us
  matrix products  54.5 us (42%)
  starting transfers between devices  43.4 us (34%)
  waiting for transfers between devices  14.4 us (11%)
  local copies, waits for them, and re-layouts  11.9 us (9%)
  other arithmetic  2.13 us (2%)
    dot_general x2, matrix products, backward_expert(): lax.dot_general(joined, weight_in, (((1,), (1,)), ((), ())), preferred_el...  18.1 us
    dot_general x2, matrix products, forward_expert(): gate_up = jnp.dot(slot_rows, weight_in, preferred_element_type=jnp.float32)  14.7 us
    all_to_all x2, starting transfers between devices, shards(): lax.all_to_all(bwd_part, 'expert', split_axis=0, concat_axis=0, tiled=True)  10.2 us
    all_to_all x2, starting transfers between devices, shards(): lax.all_to_all(fwd_part, 'expert', split_axis=0, concat_axis=0, tiled=True)  10.2 us
    dot_general x2, matrix products, backward_expert(): lax.dot_general(slot_rows, weight_out, (((1,), (1,)), ((), ())), preferre...  10.2 us
    all_to_all x2, starting transfers between devices, shards(): lax.all_to_all(bwd_slots, 'expert', split_axis=0, concat_axis=0, tiled=True)  9.69 us
    all_to_all x2, waiting for transfers between devices, shards(): lax.all_to_all(fwd_part, 'expert', split_axis=0, concat_axis=0, tiled=True)  9.62 us
    all_to_all x2, starting transfers between devices, shards(): lax.all_to_all(fwd_slots, 'expert', split_axis=0, concat_axis=0, tiled=True)  8.65 us
  transfers between devices with their start and end apart: 10, of which 3 were waited for; matrix products, arithmetic and copies ran while one was open for 49% of the time, Pallas kernels for 0%

commit v1 on v0

v1 whole, which is shorter than its diff:
```python
import functools

import jax
import jax.numpy as jnp
from jax import lax
from jax.experimental import pallas as pl
from jax.experimental.pallas import tpu as pltpu
from jax.sharding import PartitionSpec as P

FF = 1024
TICKS = 2
LANES = 128
VMEM_LIMIT = 48 * 1024 * 1024


def pack_kernel(fwd_ref, bwd_ref, fwd_route_ref, fwd_gate_ref, bwd_route_ref, bwd_gate_ref, out_ref):
    tokens, width = fwd_ref.shape[1:]
    out_ref[:tokens, :width] = fwd_ref[0]
    out_ref[tokens:, :width] = bwd_ref[0]
    lane = lax.broadcasted_iota(jnp.int32, (tokens, LANES), 1)
    for row, (route_ref, gate_ref) in enumerate(
        ((fwd_route_ref, fwd_gate_ref), (bwd_route_ref, bwd_gate_ref))
    ):
        meta = jnp.zeros((tokens, LANES), jnp.float32)
        position = 0
        for tick in range(TICKS):
            route = route_ref[tick, 0].astype(jnp.float32)
            gate = gate_ref[tick, 0]
            high = gate.astype(jnp.bfloat16).astype(jnp.float32)
            for column in range(route.shape[1]):
                for field in (route, high, gate - high):
                    meta = jnp.where(lane == position, field[:, column : column + 1], meta)
                    position += 1
        out_ref[row * tokens : (row + 1) * tokens, width:] = meta.astype(jnp.bfloat16)


def pack(fwd_now, bwd_now, fwd_route, fwd_gate, bwd_route, bwd_gate):
    tokens, width = fwd_now.shape[1:]
    return pl.pallas_call(
        pack_kernel,
        out_shape=jax.ShapeDtypeStruct((2 * tokens, width + LANES), jnp.bfloat16),
    )(fwd_now, bwd_now, fwd_route, fwd_gate, bwd_route, bwd_gate)


def expert_kernel(
    tick, tokens, top, slots, slices, chunk,
    meta_ref, rows_ref, saved_ref, w_in_ref, w_out_ref, out_ref,
    gate_w, up_w, down_w, slot_rows, weighted, sem,
):
    total, width = out_ref.shape
    hidden_units = w_out_ref.shape[2]
    chunks = hidden_units // chunk

    def copies(index):
        at = index * chunk
        return (
            pltpu.make_async_copy(
                w_in_ref.at[0, 0, :, pl.ds(at, chunk)], gate_w.at[index], sem.at[index, 0]
            ),
            pltpu.make_async_copy(
                w_in_ref.at[0, 0, :, pl.ds(hidden_units + at, chunk)], up_w.at[index], sem.at[index, 1]
            ),
            pltpu.make_async_copy(
                w_out_ref.at[0, 0, pl.ds(at, chunk), :], down_w.at[index], sem.at[index, 2]
            ),
        )

    for index in range(chunks):
        for copy in copies(index):
            copy.start()

    expert = (lax.axis_index("expert") // slices).astype(jnp.float32)
    meta = meta_ref[...].astype(jnp.float32)
    hit = jnp.zeros((total, 1), jnp.float32)
    gate_of = jnp.zeros((total, 1), jnp.float32)
    for column in range(top):
        at = (tick * top + column) * 3
        named = meta[:, at : at + 1] == expert
        hit = jnp.where(named, 1.0, hit)
        gate_of = jnp.where(named, meta[:, at + 1 : at + 2] + meta[:, at + 2 : at + 3], gate_of)
    row = lax.broadcasted_iota(jnp.int32, (total, total), 0)
    other = lax.broadcasted_iota(jnp.int32, (total, total), 1)
    earlier = (row // tokens == other // tokens) & (other < row)
    rank = jnp.dot(
        earlier.astype(jnp.bfloat16),
        jnp.broadcast_to(hit, (total, 2 * slots)).astype(jnp.bfloat16),
        preferred_element_type=jnp.float32,
    )
    row = lax.broadcasted_iota(jnp.int32, (total, 2 * slots), 0)
    slot = lax.broadcasted_iota(jnp.int32, (total, 2 * slots), 1)
    blocks = total // (2 * tokens)
    per_block = slots // blocks
    first = (row // tokens) % 2 * slots + row // (2 * tokens) * per_block
    place = jnp.where(
        (slot == first + rank.astype(jnp.int32)) & (hit > 0.0), 1.0, 0.0
    ).astype(jnp.bfloat16)
    slot_rows[...] = lax.dot_general(
        place, rows_ref[:, :width], (((0,), (0,)), ((), ())), preferred_element_type=jnp.float32
    ).astype(jnp.bfloat16)

    forward = slot_rows[:slots]
    backward = slot_rows[slots:]
    for index in range(chunks):
        for copy in copies(index):
            copy.wait()
        gate_mat, up_mat, down_mat = gate_w[index], up_w[index], down_w[index]
        gate = jnp.dot(forward, gate_mat, preferred_element_type=jnp.float32)
        up = jnp.dot(forward, up_mat, preferred_element_type=jnp.float32)
        hidden = (gate * jax.nn.sigmoid(gate) * up).astype(jnp.bfloat16)
        grad = lax.dot_general(
            backward, down_mat, (((1,), (1,)), ((), ())), preferred_element_type=jnp.float32
        )
        gate_pre = saved_ref[tick, 0, 0, :, index * chunk : (index + 1) * chunk]
        up_pre = saved_ref[
            tick, 0, 0, :, hidden_units + index * chunk : hidden_units + (index + 1) * chunk
        ]
        sigma = jax.nn.sigmoid(gate_pre)
        slope = sigma * (1.0 + gate_pre * (1.0 - sigma))
        joined_gate = (grad * up_pre * slope).astype(jnp.bfloat16)
        joined_up = (grad * (gate_pre * sigma)).astype(jnp.bfloat16)
        forward_add = jnp.dot(hidden, down_mat, preferred_element_type=jnp.float32)
        backward_add = lax.dot_general(
            joined_gate, gate_mat, (((1,), (1,)), ((), ())), preferred_element_type=jnp.float32
        ) + lax.dot_general(
            joined_up, up_mat, (((1,), (1,)), ((), ())), preferred_element_type=jnp.float32
        )
        if index == 0:
            weighted[:slots] = forward_add
            weighted[slots:] = backward_add
        else:
            weighted[:slots] += forward_add
            weighted[slots:] += backward_add
    parts = weighted[...].astype(jnp.bfloat16)
    out_ref[...] = (
        jnp.dot(place, parts, preferred_element_type=jnp.float32) * gate_of
    ).astype(jnp.bfloat16)


def expert_step(tick, tokens, top, meta, rows, saved_pre, w_in, w_out):
    width, hidden_units = w_in.shape[2], w_out.shape[2]
    slots = saved_pre.shape[3]
    total = rows.shape[0]
    chunk = min(hidden_units, 256)
    chunks = hidden_units // chunk
    whole = pl.BlockSpec(memory_space=pltpu.VMEM)
    meta_spec = pl.BlockSpec((total, LANES), lambda i: (0, width // LANES))
    rows_spec = pl.BlockSpec((total, width), lambda i: (0, 0))
    return pl.pallas_call(
        functools.partial(expert_kernel, tick, tokens, top, slots, FF // hidden_units, chunk),
        grid=(1,),
        out_shape=jax.ShapeDtypeStruct((total, width), jnp.bfloat16),
        in_specs=[
            meta_spec,
            rows_spec,
            whole,
            pl.BlockSpec(memory_space=pl.ANY),
            pl.BlockSpec(memory_space=pl.ANY),
        ],
        out_specs=whole,
        scratch_shapes=[
            pltpu.VMEM((chunks, width, chunk), jnp.bfloat16),
            pltpu.VMEM((chunks, width, chunk), jnp.bfloat16),
            pltpu.VMEM((chunks, chunk, width), jnp.bfloat16),
            pltpu.VMEM((2 * slots, width), jnp.bfloat16),
            pltpu.VMEM((2 * slots, width), jnp.float32),
            pltpu.SemaphoreType.DMA((chunks, 3)),
        ],
        compiler_params=pltpu.CompilerParams(vmem_limit_bytes=VMEM_LIMIT),
        cost_estimate=pl.CostEstimate(
            flops=12 * slots * width * hidden_units,
            bytes_accessed=6 * width * hidden_units,
            transcendentals=0,
        ),
    )(meta, rows, saved_pre, w_in, w_out)


def shards(
    fwd_act,
    fwd_enter,
    bwd_grad,
    bwd_enter,
    w_in,
    w_out,
    fwd_route,
    fwd_gate,
    bwd_route,
    bwd_gate,
    saved_pre,
):
    tokens = fwd_enter.shape[0]
    top = fwd_route.shape[3]
    section_index = lax.axis_index("section")
    section_total = lax.axis_size("section")
    up = [(i, i + 1) for i in range(section_total - 1)]
    down = [(j, i) for i, j in up]
    packed = pack(fwd_act, bwd_grad, fwd_route, fwd_gate, bwd_route, bwd_gate)
    meta = lax.all_gather(packed, "expert", axis=0, tiled=True)
    rows = meta
    own = jnp.concatenate([fwd_act[0], bwd_grad[0]], axis=0)
    fwd_list = []
    bwd_list = []
    for tick in range(TICKS):
        partial = expert_step(tick, tokens, top, meta, rows, saved_pre, w_in, w_out)
        summed = lax.psum_scatter(partial, "expert", scatter_dimension=0, tiled=True)
        following = (own.astype(jnp.float32) + summed.astype(jnp.float32)).astype(jnp.bfloat16)
        fwd_next, bwd_next = following[:tokens], following[tokens:]
        fwd_list.append(fwd_next)
        bwd_list.append(bwd_next)
        if tick + 1 < TICKS:
            from_below = lax.ppermute(fwd_next, "section", up)
            from_above = lax.ppermute(bwd_next, "section", down)
            fwd_now = jnp.where(section_index == 0, fwd_enter, from_below)
            bwd_now = jnp.where(section_index == section_total - 1, bwd_enter, from_above)
            own = jnp.concatenate([fwd_now, bwd_now], axis=0)
            rows = lax.all_gather(own, "expert", axis=0, tiled=True)
    return (jnp.stack(fwd_list)[:, None], jnp.stack(bwd_list)[:, None])


def solution(mesh):
    placed = (
        P("section", "expert", None),
        P("expert", None),
        P("section", "expert", None),
        P("expert", None),
        P("section", "expert", None, None),
        P("section", "expert", None, None),
        P(None, "section", "expert", None),
        P(None, "section", "expert", None),
        P(None, "section", "expert", None),
        P(None, "section", "expert", None),
        P(None, "section", "expert", None, None),
    )
    return jax.shard_map(
        shards,
        mesh=mesh,
        in_specs=placed,
        out_specs=(P(None, "section", "expert", None), P(None, "section", "expert", None)),
        check_vma=False,
    )
```

time: 129 us -> 158 us (1.22)
  matrix products: 54.5 us -> 0 us
  waiting for transfers between devices: 14.4 us -> 64.5 us
  starting transfers between devices: 43.4 us -> 5.92 us
  Pallas kernels: 0 us -> 32.9 us
  blocking collectives: 0 us -> 31.4 us
  between operations: 1.01 us -> 14.2 us
  local copies, waits for them, and re-layouts: 11.9 us -> 6.5 us
    reduce_scatter x0 -> x2, waiting for transfers between devices: none -> 63 us  [shards(): lax.psum_scatter(partial, 'expert', scatter_dimension=0, tiled=True)]
    dot_general x24 -> x0, matrix products: 54.5 us -> none  [the longest x2 18.1 us: backward_expert(): lax.dot_general(joined, weight_in, (((1,), (1,)), ((), ())), preferred_el...]
    all_to_all x8 -> x0, starting transfers between devices: 38.7 us -> none  [the longest x2 10.2 us: shards(): lax.all_to_all(bwd_part, 'expert', split_axis=0, concat_axis=0, tiled=True)]
    pallas_call x0 -> x3, Pallas kernels: none -> 32.9 us  [the longest x2 31.4 us: expert_step(): pl.pallas_call(functools.partial(expert_kernel, tick, tokens, top, slots,...]
    all_gather x0 -> x2, blocking collectives: none -> 31.4 us  [the longest x1 16.6 us: shards(): meta = lax.all_gather(packed, 'expert', axis=0, tiled=True)]
    all_to_all x8 -> x0, waiting for transfers between devices: 14.4 us -> none  [the longest x2 9.62 us: shards(): lax.all_to_all(fwd_part, 'expert', split_axis=0, concat_axis=0, tiled=True)]
    unnamed x28 -> x16, local copies, waits for them, and re-layouts: 0.07 us -> 6.44 us
    slice x12 -> x0, local copies, waits for them, and re-layouts: 3.55 us -> none  [the longest x3 0.89 us: shards(): fwd_gate[tick_index, 0]]
  transfers between devices with their start and end apart: 10 -> 4, of which waited for: 3 -> 3; matrix products, arithmetic and copies ran while one was open for 49% -> 0% of each run, Pallas kernels for 0% -> 0%
where the time goes in v1:
time: 158 us
  waiting for transfers between devices  64.5 us (41%)
  Pallas kernels  32.9 us (21%)
  blocking collectives  31.4 us (20%)
  between operations  14.2 us (9%)
  local copies, waits for them, and re-layouts  6.5 us (4%)
  starting transfers between devices  5.92 us (4%)
  other arithmetic  2.52 us (2%)
    reduce_scatter x2, waiting for transfers between devices, shards(): lax.psum_scatter(partial, 'expert', scatter_dimension=0, tiled=True)  63 us
    pallas_call x2, Pallas kernels, expert_step(): pl.pallas_call(functools.partial(expert_kernel, tick, tokens, top, slots,...  31.4 us
    all_gather x1, blocking collectives, shards(): meta = lax.all_gather(packed, 'expert', axis=0, tiled=True)  16.6 us
    all_gather x1, blocking collectives, shards(): rows = lax.all_gather(own, 'expert', axis=0, tiled=True)  14.8 us
    unnamed x16, local copies, waits for them, and re-layouts  6.44 us
    ppermute x1, starting transfers between devices, shards(): from_below = lax.ppermute(fwd_next, 'section', up)  4.55 us
  transfers between devices with their start and end apart: 4, of which 3 were waited for; matrix products, arithmetic and copies ran while one was open for 0% of the time, Pallas kernels for 0%

profile of v1, /device:TPU:0, one launch (start us, length us, event | category | flops | bytes accessed | tf_op | source)
XLA Modules:
  0.0 158.0 jit_solution(7488129338396568096)
XLA Ops:
  7.2 0.0 copy-start.3
  7.2 0.0 copy-start.1
  7.2 0.0 reduce-scatter.3.cloned.1.call-start
  7.3 1.4 copy.13.fwd_route_ref
  8.7 1.4 copy.14.fwd_gate_ref
  10.0 1.4 copy.15.bwd_route_ref
  11.4 1.4 copy.16.bwd_gate_ref
  12.7 1.5 shard_map.122
  14.2 16.6 %all_gather.6.meta_ref.rows_ref = bf16[64,3712]{1,0:T(8,128)(2,1)S(1)} all-gather(bf16[8,3712]{1,0:T(8,128)(2,1)} %shard_map.122), channel_id=1, replica_groups=mesh['section'=4,'expert'=8] {'expert'}, dimensions={0}, use_global_device_ids=true | all-gather | bytes 534528 | tf_op jit(solution)/shard_map/all_gather | solution.py:197
  30.8 0.9 copy-done
  31.8 15.7 %shard_map.123 = bf16[64,3584]{1,0:T(8,128)(2,1)} custom-call(bf16[64,3712]{1,0:T(8,128)(2,1)S(1)} %all_gather.6.meta_ref.rows_ref, bf16[64,3712]{1,0:T(8,128)(2,1)S(1)} %all_gather.6.meta_ref.rows_ref, f32[2,1,1,16,2048]{4,3,2,1,0:T(8,128)S(1)} %copy-done, bf16[1,1,3584,2048]{3,2,1,0:T(8,128)(2,1)} %w_in_ref.3, bf16[1,1,1024,3584]{3,2,1,0:T(8,128)(2,1)} %w_out_ref.3), custom_call_target="tpu_custom_call" | custom-call | flops 704643072 | bytes 22020096 | tf_op jit(solution)/shard_map/pallas_call | solution.py:148
  47.5 0.0 reduce-scatter.3.cloned.1.call-update
  47.5 0.0 reduce-scatter.5.cloned.1.call-start
  47.6 32.0 %reduce-scatter.3.cloned.1.call-done = bf16[8,3584]{1,0:T(8,128)(2,1)} async-done(((bf16[64,3584]{1,0:T(8,128)(2,1)}), bf16[8,3584]{1,0:T(8,128)(2,1)}) %reduce-scatter.3.cloned.1.call-update) | async-done | bytes 57360 | tf_op jit(solution)/shard_map/reduce_scatter | solution.py:204
  79.6 0.9 add_convert_fusion.1
  80.5 1.3 collective-permute-start.1
  81.8 4.5 %collective-permute-start = (bf16[4,3584]{1,0:T(4,128)(2,1)S(1)}, bf16[4,3584]{1,0:T(4,128)(2,1)S(1)}, u32[]{:S(2)}, u32[]{:S(2)}) collective-permute-start(bf16[4,3584]{1,0:T(4,128)(2,1)S(1)} %get-tuple-element.7), channel_id=1, source_target_pairs={{0,8},{8,16},{16,24},{1,9},{9,17},{17,25},{2,10},{10,18},{18,26},{... | collective-permute-start | bytes 86024 | tf_op jit(solution)/shard_map/ppermute | solution.py:210
  86.4 1.5 collective-permute-done
  88.0 14.8 %all_gather.7.rows_ref = bf16[64,3584]{1,0:T(8,128)(2,1)S(1)} all-gather(bf16[8,3584]{1,0:T(8,128)(2,1)S(1)} %pad_maximum_fusion), channel_id=1, replica_groups=mesh['section'=4,'expert'=8] {'expert'}, dimensions={0}, use_global_device_ids=true | all-gather | bytes 516096 | tf_op jit(solution)/shard_map/all_gather | solution.py:215
  102.8 15.7 %shard_map.124 = bf16[64,3584]{1,0:T(8,128)(2,1)} custom-call(bf16[64,3712]{1,0:T(8,128)(2,1)S(1)} %all_gather.6.meta_ref.rows_ref, bf16[64,3584]{1,0:T(8,128)(2,1)S(1)} %all_gather.7.rows_ref, f32[2,1,1,16,2048]{4,3,2,1,0:T(8,128)S(1)} %copy-done.1, bf16[1,1,3584,2048]{3,2,1,0:T(8,128)(2,1)} %w_in_ref.3, bf16[1,1,1024,3584]{3,2,1,0:T(8,128)(2,1)} %w_out_ref.3), custom_call_target="tpu_custom_call" | custom-call | flops 704643072 | bytes 22020096 | tf_op jit(solution)/shard_map/pallas_call | solution.py:148
  118.5 0.0 reduce-scatter.5.cloned.1.call-update
  118.6 31.0 %reduce-scatter.5.cloned.1.call-done = bf16[8,3584]{1,0:T(8,128)(2,1)} async-done(((bf16[64,3584]{1,0:T(8,128)(2,1)}), bf16[8,3584]{1,0:T(8,128)(2,1)}) %reduce-scatter.5.cloned.1.call-update) | async-done | bytes 57360 | tf_op jit(solution)/shard_map/reduce_scatter | solution.py:204
  149.5 0.9 add_convert_fusion
  150.4 0.7 maximum_bitcast_fusion
  (15 shorter events, 0.2 us)
Async XLA Ops:
  7.2 72.4 %copy-start.3 = (bf16[1,4,3584]{2,1,0:T(4,128)(2,1)S(1)}, bf16[1,4,3584]{2,1,0:T(4,128)(2,1)}, u32[]{:S(2)}) copy-start(bf16[1,4,3584]{2,1,0:T(4,128)(2,1)} %bwd_ref.1) | copy-start | bytes 86020
  7.2 72.4 %copy-start.2 = (bf16[1,4,3584]{2,1,0:T(4,128)(2,1)S(1)}, bf16[1,4,3584]{2,1,0:T(4,128)(2,1)}, u32[]{:S(2)}) copy-start(bf16[1,4,3584]{2,1,0:T(4,128)(2,1)} %fwd_ref.1) | copy-start | bytes 86020
  7.2 95.6 %copy-start.1 = (f32[2,1,1,16,2048]{4,3,2,1,0:T(8,128)S(1)}, f32[2,1,1,16,2048]{4,3,2,1,0:T(8,128)}, u32[]{:S(2)}) copy-start(f32[2,1,1,16,2048]{4,3,2,1,0:T(8,128)} %saved_ref.3) | copy-start | bytes 786436
  7.2 79.2 %copy-start.4 = (bf16[4,3584]{1,0:T(4,128)(2,1)S(1)}, bf16[4,3584]{1,0:T(4,128)(2,1)}, u32[]{:S(2)}) copy-start(bf16[4,3584]{1,0:T(4,128)(2,1)} %param.14) | copy-start | bytes 86020
  7.2 80.7 %copy-start.5 = (bf16[4,3584]{1,0:T(4,128)(2,1)S(1)}, bf16[4,3584]{1,0:T(4,128)(2,1)}, u32[]{:S(2)}) copy-start(bf16[4,3584]{1,0:T(4,128)(2,1)} %param.12) | copy-start | bytes 86020
  7.2 72.4 %reduce-scatter.3.cloned.1.call-start = ((), (), s32[]{:S(2)}) async-start(), calls=%async_computation.2 | async-start | bytes 516096 | tf_op jit(solution)/shard_map/reduce_scatter | solution.py:204
  30.8 1.0 copy-start
  47.5 102.0 %reduce-scatter.5.cloned.1.call-start = ((), (), s32[]{:S(2)}) async-start(), calls=%async_computation.3 | async-start | bytes 516096 | tf_op jit(solution)/shard_map/reduce_scatter | solution.py:204
  80.5 5.9 %collective-permute-start.1 = (bf16[4,3584]{1,0:T(4,128)(2,1)S(1)}, bf16[4,3584]{1,0:T(4,128)(2,1)S(1)}, u32[]{:S(2)}, u32[]{:S(2)}) collective-permute-start(bf16[4,3584]{1,0:T(4,128)(2,1)S(1)} %get-tuple-element.6), channel_id=1, source_target_pairs={{8,0},{16,8},{24,16},{9,1},{17,9},{25,17},{10,2},{18,10},{26,18},{... | collective-permute-start | bytes 86024 | tf_op jit(solution)/shard_map/ppermute | solution.py:211
  81.8 6.1 %collective-permute-start = (bf16[4,3584]{1,0:T(4,128)(2,1)S(1)}, bf16[4,3584]{1,0:T(4,128)(2,1)S(1)}, u32[]{:S(2)}, u32[]{:S(2)}) collective-permute-start(bf16[4,3584]{1,0:T(4,128)(2,1)S(1)} %get-tuple-element.7), channel_id=1, source_target_pairs={{0,8},{8,16},{16,24},{1,9},{9,17},{17,25},{2,10},{10,18},{18,26},{... | collective-permute-start | bytes 86024 | tf_op jit(solution)/shard_map/ppermute | solution.py:210
Sparse Core Ops, SparseCore 0:
  47.7 31.8 reduce-scatter.2
  118.7 30.7 reduce-scatter.4

commit v2 on v0

v2 whole, which is shorter than its diff:
```python
import functools

import jax
import jax.numpy as jnp
from jax import lax
from jax.experimental import pallas as pl
from jax.experimental.pallas import tpu as pltpu
from jax.sharding import PartitionSpec as P

FF = 1024
TICKS = 2
VMEM_LIMIT = 40 * 1024 * 1024
VMEM = pl.BlockSpec(memory_space=pltpu.VMEM)
ANY = pl.BlockSpec(memory_space=pl.ANY)


def exact_dot(one_hot, values):
    return jnp.dot(one_hot.astype(jnp.bfloat16), values, preferred_element_type=jnp.float32)


def placing(route_ref, gate_ref, tick, direction, rows, per_expert, slices):
    route = route_ref[tick, 0]
    gate = gate_ref[tick, 0]
    top, tokens = route.shape
    block = 4 * per_expert
    row = lax.broadcasted_iota(jnp.int32, (rows, tokens), 0)
    expert = row // (block * slices)
    mine = (row // per_expert) % 2 == direction
    hit = jnp.zeros((rows, tokens), jnp.float32)
    weight = jnp.zeros((rows, tokens), jnp.float32)
    for column in range(top):
        named = route[column : column + 1, :] == expert
        hit = jnp.where(named, 1.0, hit)
        weight = jnp.where(named, gate[column : column + 1, :], weight)
    lane = lax.broadcasted_iota(jnp.int32, (rows, tokens), 1)
    rank = jnp.zeros((rows, tokens), jnp.float32)
    for token in range(tokens - 1):
        rank = rank + jnp.where(lane > token, hit[:, token : token + 1], 0.0)
    place = jnp.where(
        mine & (hit > 0.0) & (rank.astype(jnp.int32) == row % per_expert), 1.0, 0.0
    )
    return place, weight * place


def half_of(rows, width, per_expert):
    row = lax.broadcasted_iota(jnp.int32, (rows, width), 0)
    return (row // (2 * per_expert)) % 2


def pack_kernel(
    tick, per_expert, slices,
    fwd_route_ref, fwd_gate_ref, bwd_route_ref, bwd_gate_ref, fwd_ref, bwd_ref, *rest,
):
    devices, block, half_width = rest[-1].shape
    out_ref = rest[-1]
    rows = devices * block
    fwd = fwd_ref[...].reshape(fwd_ref.shape[-2:])
    bwd = bwd_ref[...].reshape(bwd_ref.shape[-2:])
    if len(rest) == 3:
        section = lax.axis_index("section")
        fwd = jnp.where(section == 0, rest[0][...], fwd)
        bwd = jnp.where(section == lax.axis_size("section") - 1, rest[1][...], bwd)
    total = jnp.zeros((rows, half_width), jnp.float32)
    for direction, (route_ref, gate_ref, tokens) in enumerate(
        ((fwd_route_ref, fwd_gate_ref, fwd), (bwd_route_ref, bwd_gate_ref, bwd))
    ):
        place, _ = placing(route_ref, gate_ref, tick, direction, rows, per_expert, slices)
        side = half_of(rows, place.shape[1], per_expert)
        for half in range(2):
            total = total + exact_dot(
                jnp.where(side == half, place, 0.0),
                tokens[:, half * half_width : (half + 1) * half_width],
            )
    out_ref[...] = total.astype(jnp.bfloat16).reshape(out_ref.shape)


def pack(tick, devices, per_expert, slices, routing, fwd, bwd, *entering):
    width = fwd.shape[-1]
    return pl.pallas_call(
        functools.partial(pack_kernel, tick, per_expert, slices),
        out_shape=pltpu.VMEM((devices, 4 * per_expert, width // 2), jnp.bfloat16),
        in_specs=[VMEM] * (6 + len(entering)),
        out_specs=VMEM,
    )(*routing, fwd, bwd, *entering)


def combine_kernel(
    tick, per_expert, slices,
    fwd_route_ref, fwd_gate_ref, bwd_route_ref, bwd_gate_ref, back_ref, fwd_ref, bwd_ref, *rest,
):
    devices, block, half_width = back_ref.shape
    rows = devices * block
    fwd = fwd_ref[...].reshape(fwd_ref.shape[-2:])
    bwd = bwd_ref[...].reshape(bwd_ref.shape[-2:])
    last = len(rest) == 6
    if last:
        section = lax.axis_index("section")
        fwd = jnp.where(section == 0, rest[0][...], fwd)
        bwd = jnp.where(section == lax.axis_size("section") - 1, rest[1][...], bwd)
    back = back_ref[...].reshape(rows, half_width)
    for direction, (route_ref, gate_ref, tokens) in enumerate(
        ((fwd_route_ref, fwd_gate_ref, fwd), (bwd_route_ref, bwd_gate_ref, bwd))
    ):
        _, weight = placing(route_ref, gate_ref, tick, direction, rows, per_expert, slices)
        side = half_of(rows, weight.shape[1], per_expert)
        sides = jnp.concatenate(
            [jnp.where(side == half, weight, 0.0) for half in range(2)], axis=1
        )
        high = sides.astype(jnp.bfloat16)
        left = sides - high.astype(jnp.float32)
        middle = left.astype(jnp.bfloat16)
        low = (left - middle.astype(jnp.float32)).astype(jnp.bfloat16)
        mixed = jnp.zeros((sides.shape[1], half_width), jnp.float32)
        for term in (low, middle, high):
            mixed = mixed + lax.dot_general(
                term, back, (((0,), (0,)), ((), ())), preferred_element_type=jnp.float32
            )
        count = tokens.shape[0]
        for half in range(2):
            columns = slice(half * half_width, (half + 1) * half_width)
            value = tokens[:, columns].astype(jnp.float32) + mixed[half * count : (half + 1) * count]
            if last:
                rest[4 + direction][tick, 0, :, columns] = value.astype(jnp.bfloat16)
            else:
                rest[direction][:, columns] = value.astype(jnp.bfloat16)
        if last:
            for earlier in range(tick):
                rest[4 + direction][earlier, 0] = rest[2 + direction][...]


def combine(tick, per_expert, slices, routing, back, fwd, bwd, *others):
    tokens, width = fwd.shape[-2:]
    if others:
        out_shape = [jax.ShapeDtypeStruct((TICKS, 1, tokens, width), jnp.bfloat16)] * 2
    else:
        out_shape = [pltpu.VMEM((tokens, width), jnp.bfloat16)] * 2
    return pl.pallas_call(
        functools.partial(combine_kernel, tick, per_expert, slices),
        out_shape=out_shape,
        in_specs=[VMEM] * (7 + len(others)),
        out_specs=[VMEM] * 2,
    )(*routing, back, fwd, bwd, *others)


def expert_kernel(
    tick, in_chunk, out_chunk,
    rows_ref, saved_ref, w_in_ref, w_out_ref, out_ref,
    w_in, w_out, saved, fwd_rows, bwd_cols, joined, parts, in_sem, out_sem, saved_sem,
):
    devices, block, half_width = rows_ref.shape
    per_expert = block // 4
    slots = devices * per_expert
    width, both = w_in.shape
    hidden_units = both // 2
    rows = devices * block

    def in_copy(index):
        at = pl.ds(index * in_chunk, in_chunk)
        return pltpu.make_async_copy(w_in_ref.at[0, 0, at, :], w_in.at[at, :], in_sem.at[index])

    def out_copy(index):
        at = pl.ds(index * out_chunk, out_chunk)
        return pltpu.make_async_copy(w_out_ref.at[0, 0, at, :], w_out.at[at, :], out_sem.at[index])

    saved_copy = pltpu.make_async_copy(saved_ref.at[tick, 0, 0], saved, saved_sem)
    saved_copy.start()
    for index in range(hidden_units // out_chunk):
        out_copy(index).start()
    for index in range(width // in_chunk):
        in_copy(index).start()

    received = rows_ref[...].reshape(rows, half_width)
    slot = lax.broadcasted_iota(jnp.int32, (2 * slots, rows), 0)
    row = lax.broadcasted_iota(jnp.int32, (2 * slots, rows), 1)
    home = (slot % slots) // per_expert * block + slot // slots * per_expert + slot % per_expert
    for half in range(2):
        columns = slice(half * half_width, (half + 1) * half_width)
        pick = jnp.where(row == home + half * 2 * per_expert, 1.0, 0.0)
        picked = exact_dot(pick, received)
        fwd_rows[:, columns] = picked[:slots].astype(jnp.bfloat16)
        bwd_cols[columns, :] = picked[slots:].T.astype(jnp.bfloat16)

    saved_copy.wait()
    gate_pre = saved[:, :hidden_units]
    sigma = jax.nn.sigmoid(gate_pre)
    slope = sigma * (1.0 + gate_pre * (1.0 - sigma))
    gate_factor = (saved[:, hidden_units:] * slope).T
    up_factor = (gate_pre * sigma).T

    for index in range(hidden_units // out_chunk):
        out_copy(index).wait()
        at = slice(index * out_chunk, (index + 1) * out_chunk)
        grad = jnp.dot(w_out[at, :], bwd_cols[...], preferred_element_type=jnp.float32)
        joined[at, :] = (grad * gate_factor[at]).astype(jnp.bfloat16)
        joined[hidden_units + at.start : hidden_units + at.stop, :] = (
            grad * up_factor[at]
        ).astype(jnp.bfloat16)

    gate_up = jnp.zeros((slots, both), jnp.float32)
    for index in range(width // in_chunk):
        in_copy(index).wait()
        at = slice(index * in_chunk, (index + 1) * in_chunk)
        mat = w_in[at, :]
        gate_up = gate_up + jnp.dot(fwd_rows[:, at], mat, preferred_element_type=jnp.float32)
        part = jnp.dot(mat, joined[...], preferred_element_type=jnp.float32)
        parts[slots:, at] = part.T.astype(jnp.bfloat16)

    gate = gate_up[:, :hidden_units]
    hidden = (gate * jax.nn.sigmoid(gate) * gate_up[:, hidden_units:]).astype(jnp.bfloat16)
    for half in range(2):
        columns = slice(half * half_width, (half + 1) * half_width)
        parts[:slots, columns] = jnp.dot(
            hidden, w_out[:, columns], preferred_element_type=jnp.float32
        ).astype(jnp.bfloat16)

    row = lax.broadcasted_iota(jnp.int32, (rows, 2 * slots), 0)
    slot = lax.broadcasted_iota(jnp.int32, (rows, 2 * slots), 1)
    home = (slot % slots) // per_expert * block + slot // slots * per_expert + slot % per_expert
    total = jnp.zeros((rows, half_width), jnp.float32)
    for half in range(2):
        spread = jnp.where(row == home + half * 2 * per_expert, 1.0, 0.0)
        total = total + exact_dot(spread, parts[:, half * half_width : (half + 1) * half_width])
    out_ref[...] = total.astype(jnp.bfloat16).reshape(out_ref.shape)


def expert_step(tick, rows, saved_pre, w_in, w_out):
    width, hidden_units = w_in.shape[2], w_out.shape[2]
    slots = saved_pre.shape[3]
    in_chunk, out_chunk = width // 7, min(hidden_units, 256)
    return pl.pallas_call(
        functools.partial(expert_kernel, tick, in_chunk, out_chunk),
        out_shape=pltpu.VMEM(rows.shape, jnp.bfloat16),
        in_specs=[VMEM, ANY, ANY, ANY],
        out_specs=VMEM,
        scratch_shapes=[
            pltpu.VMEM((width, 2 * hidden_units), jnp.bfloat16),
            pltpu.VMEM((hidden_units, width), jnp.bfloat16),
            pltpu.VMEM((slots, 2 * hidden_units), jnp.float32),
            pltpu.VMEM((slots, width), jnp.bfloat16),
            pltpu.VMEM((width, slots), jnp.bfloat16),
            pltpu.VMEM((2 * hidden_units, slots), jnp.bfloat16),
            pltpu.VMEM((2 * slots, width), jnp.bfloat16),
            pltpu.SemaphoreType.DMA((width // in_chunk,)),
            pltpu.SemaphoreType.DMA((hidden_units // out_chunk,)),
            pltpu.SemaphoreType.DMA,
        ],
        compiler_params=pltpu.CompilerParams(vmem_limit_bytes=VMEM_LIMIT),
        cost_estimate=pl.CostEstimate(
            flops=12 * slots * width * hidden_units,
            bytes_accessed=6 * width * hidden_units,
            transcendentals=0,
        ),
    )(rows, saved_pre, w_in, w_out)


def exchange(array):
    return lax.all_to_all(array, "expert", split_axis=0, concat_axis=0, tiled=True)


def shards(
    fwd_act,
    fwd_enter,
    bwd_grad,
    bwd_enter,
    w_in,
    w_out,
    fwd_route,
    fwd_gate,
    bwd_route,
    bwd_gate,
    saved_pre,
):
    devices = lax.axis_size("expert")
    slices = FF // w_out.shape[2]
    per_expert = saved_pre.shape[3] // devices
    section_total = lax.axis_size("section")
    up = [(i, i + 1) for i in range(section_total - 1)]
    down = [(j, i) for i, j in up]
    routing = [
        jnp.swapaxes(table, 2, 3) for table in (fwd_route, fwd_gate, bwd_route, bwd_gate)
    ]
    fwd_now, bwd_now, entering, earlier = fwd_act, bwd_grad, (), ()
    for tick in range(TICKS):
        sent = pack(tick, devices, per_expert, slices, routing, fwd_now, bwd_now, *entering)
        parts = expert_step(tick, exchange(sent), saved_pre, w_in, w_out)
        fwd_next, bwd_next = combine(
            tick, per_expert, slices, routing, exchange(parts), fwd_now, bwd_now, *entering, *earlier
        )
        if tick + 1 < TICKS:
            earlier = (fwd_next, bwd_next)
            entering = (fwd_enter, bwd_enter)
            fwd_now = lax.ppermute(fwd_next, "section", up)
            bwd_now = lax.ppermute(bwd_next, "section", down)
    return fwd_next, bwd_next


def solution(mesh):
    placed = (
        P("section", "expert", None),
        P("expert", None),
        P("section", "expert", None),
        P("expert", None),
        P("section", "expert", None, None),
        P("section", "expert", None, None),
        P(None, "section", "expert", None),
        P(None, "section", "expert", None),
        P(None, "section", "expert", None),
        P(None, "section", "expert", None),
        P(None, "section", "expert", None, None),
    )
    return jax.shard_map(
        shards,
        mesh=mesh,
        in_specs=placed,
        out_specs=(P(None, "section", "expert", None), P(None, "section", "expert", None)),
        check_vma=False,
    )
```

time: 129 us -> 105 us (0.81)
  matrix products: 54.5 us -> 0 us
  blocking collectives: 0 us -> 50.8 us
  starting transfers between devices: 43.4 us -> 4.69 us
  Pallas kernels: 0 us -> 36.2 us
  waiting for transfers between devices: 14.4 us -> 4.46 us
  local copies, waits for them, and re-layouts: 11.9 us -> 7.75 us
  other arithmetic: 2.13 us -> 0 us
    dot_general x24 -> x0, matrix products: 54.5 us -> none  [the longest x2 18.1 us: backward_expert(): lax.dot_general(joined, weight_in, (((1,), (1,)), ((), ())), preferred_el...]
    all_to_all x0 -> x4, blocking collectives: none -> 50.8 us  [exchange(): lax.all_to_all(array, 'expert', split_axis=0, concat_axis=0, tiled=True)]
    all_to_all x8 -> x0, starting transfers between devices: 38.7 us -> none  [the longest x2 10.2 us: shards(): lax.all_to_all(bwd_part, 'expert', split_axis=0, concat_axis=0, tiled=True)]
    pallas_call x0 -> x6, Pallas kernels: none -> 36.2 us  [the longest x2 29.8 us: expert_step(): pl.pallas_call(functools.partial(expert_kernel, tick, in_chunk, out_chunk...]
    all_to_all x8 -> x0, waiting for transfers between devices: 14.4 us -> none  [the longest x2 9.62 us: shards(): lax.all_to_all(fwd_part, 'expert', split_axis=0, concat_axis=0, tiled=True)]
    unnamed x28 -> x16, local copies, waits for them, and re-layouts: 0.07 us -> 7.75 us
    ppermute x2, waiting for transfers between devices: 0.01 us -> 4.46 us  [the longest x1 4.22 us: shards(): bwd_now = lax.ppermute(bwd_next, 'section', down)]
    slice x12 -> x0, local copies, waits for them, and re-layouts: 3.55 us -> none  [the longest x3 0.89 us: shards(): fwd_gate[tick_index, 0]]
  transfers between devices with their start and end apart: 10 -> 2, of which waited for: 3 -> 2; matrix products, arithmetic and copies ran while one was open for 49% -> 0% of each run, Pallas kernels for 0% -> 0%
where the time goes in v2:
time: 105 us
  blocking collectives  50.8 us (48%)
  Pallas kernels  36.2 us (34%)
  local copies, waits for them, and re-layouts  7.75 us (7%)
  starting transfers between devices  4.69 us (4%)
  waiting for transfers between devices  4.46 us (4%)
    all_to_all x4, blocking collectives, exchange(): lax.all_to_all(array, 'expert', split_axis=0, concat_axis=0, tiled=True)  50.8 us
    pallas_call x2, Pallas kernels, expert_step(): pl.pallas_call(functools.partial(expert_kernel, tick, in_chunk, out_chunk...  29.8 us
    unnamed x16, local copies, waits for them, and re-layouts  7.75 us
    ppermute x1, waiting for transfers between devices, shards(): bwd_now = lax.ppermute(bwd_next, 'section', down)  4.22 us
    pallas_call x2, Pallas kernels, combine(): pl.pallas_call(functools.partial(combine_kernel, tick, per_expert, slices...  3.83 us
    ppermute x1, starting transfers between devices, shards(): fwd_now = lax.ppermute(fwd_next, 'section', up)  3.39 us
    pallas_call x2, Pallas kernels, pack(): pl.pallas_call(functools.partial(pack_kernel, tick, per_expert, slices),...  2.65 us
  transfers between devices with their start and end apart: 2, of which 2 were waited for; matrix products, arithmetic and copies ran while one was open for 0% of the time, Pallas kernels for 0%

profile of v2, /device:TPU:0, one launch (start us, length us, event | category | flops | bytes accessed | tf_op | source)
XLA Modules:
  0.0 104.7 jit_solution(8810461457122409423)
XLA Ops:
  0.6 0.0 copy-start.3
  0.6 1.3 %shard_map.122 = bf16[8,8,1792]{2,1,0:T(8,128)(2,1)S(1)} custom-call(s32[2,1,2,4]{3,2,1,0:T(2,128)} %bitcast.4, f32[2,1,2,4]{3,2,1,0:T(2,128)} %bitcast.8, s32[2,1,2,4]{3,2,1,0:T(2,128)} %bitcast.12, f32[2,1,2,4]{3,2,1,0:T(2,128)} %bitcast.16, bf16[1,4,3584]{2,1,0:T(4,128)(2,1)} %fwd_ref.3, bf16[1,4,3584]{2,1,0:T(4,128)(2,1)} %bwd_ref.3), custom_call_target="tpu_custom_call" | custom-call | tf_op jit(solution)/shard_map/pallas_call | solution.py:79
  2.0 15.2 %all_to_all.20.rows_ref = bf16[8,8,1792]{2,1,0:T(8,128)(2,1)S(1)} all-to-all(bf16[8,8,1792]{2,1,0:T(8,128)(2,1)S(1)} %shard_map.122), channel_id=1, replica_groups=mesh['section'=4,'expert'=8] {'expert'}, dimensions={0} | all-to-all | bytes 458752 | tf_op jit(solution)/shard_map/all_to_all | solution.py:257
  17.1 3.1 %copy-done = bf16[1,1,1024,3584]{3,2,1,0:T(8,128)(2,1)S(1)} copy-done((bf16[1,1,1024,3584]{3,2,1,0:T(8,128)(2,1)S(1)}, bf16[1,1,1024,3584]{3,2,1,0:T(8,128)(2,1)}, u32[]{:S(2)}) %copy-start) | copy-done | bytes 7340056
  20.2 0.9 copy-done.2
  21.2 14.9 %shard_map.123 = bf16[8,8,1792]{2,1,0:T(8,128)(2,1)S(1)} custom-call(bf16[8,8,1792]{2,1,0:T(8,128)(2,1)S(1)} %all_to_all.20.rows_ref, f32[2,1,1,16,2048]{4,3,2,1,0:T(8,128)S(1)} %copy-done.2, bf16[1,1,3584,2048]{3,2,1,0:T(8,128)(2,1)} %w_in_ref.3, bf16[1,1,1024,3584]{3,2,1,0:T(8,128)(2,1)S(1)} %copy-done), custom_call_target="tpu_custom_call" | custom-call | flops 704643072 | bytes 22020096 | tf_op jit(solution)/shard_map/pallas_call | solution.py:230
  36.1 12.1 %all_to_all.21.back_ref = bf16[8,8,1792]{2,1,0:T(8,128)(2,1)} all-to-all(bf16[8,8,1792]{2,1,0:T(8,128)(2,1)S(1)} %shard_map.123), channel_id=1, replica_groups=mesh['section'=4,'expert'=8] {'expert'}, dimensions={0} | all-to-all | bytes 458752 | tf_op jit(solution)/shard_map/all_to_all | solution.py:257
  48.2 1.6 %shard_map.124 = (bf16[4,3584]{1,0:T(4,128)(2,1)S(1)}, bf16[4,3584]{1,0:T(4,128)(2,1)S(1)}) custom-call(s32[2,1,2,4]{3,2,1,0:T(2,128)} %bitcast.5, f32[2,1,2,4]{3,2,1,0:T(2,128)} %bitcast.9, s32[2,1,2,4]{3,2,1,0:T(2,128)} %bitcast.13, f32[2,1,2,4]{3,2,1,0:T(2,128)} %bitcast.17, bf16[8,8,1792]{2,1,0:T(8,128)(2,1)} %all_to_all.21.back_ref, ...), custom_call_target="tpu_custom_call" | custom-call | tf_op jit(solution)/shard_map/pallas_call | solution.py:137
  49.8 0.0 copy-start.4
  49.8 0.0 copy-start.5
  49.8 3.4 %collective-permute-start = (bf16[4,3584]{1,0:T(4,128)(2,1)S(1)}, bf16[4,3584]{1,0:T(4,128)(2,1)S(1)}, u32[]{:S(2)}, u32[]{:S(2)}) collective-permute-start(bf16[4,3584]{1,0:T(4,128)(2,1)S(1)} %get-tuple-element.4.rest_2_), channel_id=1, source_target_pairs={{0,8},{8,16},{16,24},{1,9},{9,17},{17,25},{2,10},{10,18},{18,26},{... | collective-permute-start | bytes 86024 | tf_op jit(solution)/shard_map/ppermute | solution.py:292
  53.2 1.3 %collective-permute-start.1 = (bf16[4,3584]{1,0:T(4,128)(2,1)S(1)}, bf16[4,3584]{1,0:T(4,128)(2,1)S(1)}, u32[]{:S(2)}, u32[]{:S(2)}) collective-permute-start(bf16[4,3584]{1,0:T(4,128)(2,1)S(1)} %get-tuple-element.5.rest_3_), channel_id=1, source_target_pairs={{8,0},{16,8},{24,16},{9,1},{17,9},{25,17},{10,2},{18,10},{26,18},{... | collective-permute-start | bytes 86024 | tf_op jit(solution)/shard_map/ppermute | solution.py:293
  54.5 0.2 collective-permute-done.fwd_ref
  54.7 4.2 %collective-permute-done.1.bwd_ref = bf16[4,3584]{1,0:T(4,128)(2,1)S(1)} collective-permute-done((bf16[4,3584]{1,0:T(4,128)(2,1)S(1)}, bf16[4,3584]{1,0:T(4,128)(2,1)S(1)}, u32[]{:S(2)}, u32[]{:S(2)}) %collective-permute-start.1) | collective-permute-done | bytes 28704 | tf_op jit(solution)/shard_map/ppermute | solution.py:293
  58.9 0.0 copy-done.6
  58.9 0.6 copy-done.7
  59.6 1.3 %shard_map.125 = bf16[8,8,1792]{2,1,0:T(8,128)(2,1)S(1)} custom-call(s32[2,1,2,4]{3,2,1,0:T(2,128)} %bitcast.6, f32[2,1,2,4]{3,2,1,0:T(2,128)} %bitcast.10, s32[2,1,2,4]{3,2,1,0:T(2,128)} %bitcast.14, f32[2,1,2,4]{3,2,1,0:T(2,128)} %bitcast.18, bf16[4,3584]{1,0:T(4,128)(2,1)} %copy-done.6, bf16[4,3584]{1,0:T(4,128)(2,1)} %copy-done.7, ...), custom_call_target="tpu_custom_call" | custom-call | tf_op jit(solution)/shard_map/pallas_call | solution.py:79
  60.9 11.4 %all_to_all.22.rows_ref = bf16[8,8,1792]{2,1,0:T(8,128)(2,1)S(1)} all-to-all(bf16[8,8,1792]{2,1,0:T(8,128)(2,1)S(1)} %shard_map.125), channel_id=1, replica_groups=mesh['section'=4,'expert'=8] {'expert'}, dimensions={0} | all-to-all | bytes 458752 | tf_op jit(solution)/shard_map/all_to_all | solution.py:257
  72.3 0.0 copy-done.3
  72.3 3.1 %copy-done.1 = bf16[1,1,1024,3584]{3,2,1,0:T(8,128)(2,1)S(1)} copy-done((bf16[1,1,1024,3584]{3,2,1,0:T(8,128)(2,1)S(1)}, bf16[1,1,1024,3584]{3,2,1,0:T(8,128)(2,1)}, u32[]{:S(2)}) %copy-start.1) | copy-done | bytes 7340056
  75.4 14.9 %shard_map.126 = bf16[8,8,1792]{2,1,0:T(8,128)(2,1)S(1)} custom-call(bf16[8,8,1792]{2,1,0:T(8,128)(2,1)S(1)} %all_to_all.22.rows_ref, f32[2,1,1,16,2048]{4,3,2,1,0:T(8,128)S(1)} %copy-done.3, bf16[1,1,3584,2048]{3,2,1,0:T(8,128)(2,1)} %w_in_ref.3, bf16[1,1,1024,3584]{3,2,1,0:T(8,128)(2,1)S(1)} %copy-done.1), custom_call_target="tpu_custom_call" | custom-call | flops 704643072 | bytes 22020096 | tf_op jit(solution)/shard_map/pallas_call | solution.py:230
  90.3 12.1 %all_to_all.23.back_ref = bf16[8,8,1792]{2,1,0:T(8,128)(2,1)} all-to-all(bf16[8,8,1792]{2,1,0:T(8,128)(2,1)S(1)} %shard_map.126), channel_id=1, replica_groups=mesh['section'=4,'expert'=8] {'expert'}, dimensions={0} | all-to-all | bytes 458752 | tf_op jit(solution)/shard_map/all_to_all | solution.py:257
  102.4 0.0 copy-done.4
  102.4 2.3 %shard_map.127 = (bf16[2,1,4,3584]{3,2,1,0:T(4,128)(2,1)}, bf16[2,1,4,3584]{3,2,1,0:T(4,128)(2,1)}) custom-call(s32[2,1,2,4]{3,2,1,0:T(2,128)} %bitcast.7, f32[2,1,2,4]{3,2,1,0:T(2,128)} %bitcast.11, s32[2,1,2,4]{3,2,1,0:T(2,128)} %bitcast.15, f32[2,1,2,4]{3,2,1,0:T(2,128)} %bitcast.19, bf16[8,8,1792]{2,1,0:T(8,128)(2,1)} %all_to_all.23.back_ref, ...), custom_call_target="tpu_custom_call" | custom-call | tf_op jit(solution)/shard_map/pallas_call | solution.py:137
  (6 shorter events, 0.0 us)
Async XLA Ops:
  0.6 71.7 %copy-start.3 = (f32[2,1,1,16,2048]{4,3,2,1,0:T(8,128)S(1)}, f32[2,1,1,16,2048]{4,3,2,1,0:T(8,128)}, u32[]{:S(2)}) copy-start(f32[2,1,1,16,2048]{4,3,2,1,0:T(8,128)} %saved_ref.3) | copy-start | bytes 786436
  17.1 3.1 %copy-start = (bf16[1,1,1024,3584]{3,2,1,0:T(8,128)(2,1)S(1)}, bf16[1,1,1024,3584]{3,2,1,0:T(8,128)(2,1)}, u32[]{:S(2)}) copy-start(bf16[1,1,1024,3584]{3,2,1,0:T(8,128)(2,1)} %w_out_ref.3) | copy-start | bytes 22020100
  20.2 0.9 copy-start.2
  49.8 52.7 %copy-start.4 = (bf16[4,3584]{1,0:T(4,128)(2,1)}, bf16[4,3584]{1,0:T(4,128)(2,1)S(1)}, u32[]{:S(2)}) copy-start(bf16[4,3584]{1,0:T(4,128)(2,1)S(1)} %get-tuple-element.4.rest_2_) | copy-start | bytes 86020
  49.8 52.7 %copy-start.5 = (bf16[4,3584]{1,0:T(4,128)(2,1)}, bf16[4,3584]{1,0:T(4,128)(2,1)S(1)}, u32[]{:S(2)}) copy-start(bf16[4,3584]{1,0:T(4,128)(2,1)S(1)} %get-tuple-element.5.rest_3_) | copy-start | bytes 86020
  49.8 4.9 %collective-permute-start = (bf16[4,3584]{1,0:T(4,128)(2,1)S(1)}, bf16[4,3584]{1,0:T(4,128)(2,1)S(1)}, u32[]{:S(2)}, u32[]{:S(2)}) collective-permute-start(bf16[4,3584]{1,0:T(4,128)(2,1)S(1)} %get-tuple-element.4.rest_2_), channel_id=1, source_target_pairs={{0,8},{8,16},{16,24},{1,9},{9,17},{17,25},{2,10},{10,18},{18,26},{... | collective-permute-start | bytes 86024 | tf_op jit(solution)/shard_map/ppermute | solution.py:292
  53.2 5.8 %collective-permute-start.1 = (bf16[4,3584]{1,0:T(4,128)(2,1)S(1)}, bf16[4,3584]{1,0:T(4,128)(2,1)S(1)}, u32[]{:S(2)}, u32[]{:S(2)}) collective-permute-start(bf16[4,3584]{1,0:T(4,128)(2,1)S(1)} %get-tuple-element.5.rest_3_), channel_id=1, source_target_pairs={{8,0},{16,8},{24,16},{9,1},{17,9},{25,17},{10,2},{18,10},{26,18},{... | collective-permute-start | bytes 86024 | tf_op jit(solution)/shard_map/ppermute | solution.py:293
  54.7 4.2 %copy-start.6 = (bf16[4,3584]{1,0:T(4,128)(2,1)}, bf16[4,3584]{1,0:T(4,128)(2,1)S(1)}, u32[]{:S(2)}) copy-start(bf16[4,3584]{1,0:T(4,128)(2,1)S(1)} %collective-permute-done.fwd_ref) | copy-start | bytes 86020
  58.9 0.6 copy-start.7
  72.3 3.1 %copy-start.1 = (bf16[1,1,1024,3584]{3,2,1,0:T(8,128)(2,1)S(1)}, bf16[1,1,1024,3584]{3,2,1,0:T(8,128)(2,1)}, u32[]{:S(2)}) copy-start(bf16[1,1,1024,3584]{3,2,1,0:T(8,128)(2,1)} %w_out_ref.3) | copy-start | bytes 22020100

commit v3 on v2

--- a/solution.py
+++ b/solution.py
@@ -9,9 +9,10 @@
 
 FF = 1024
 TICKS = 2
-VMEM_LIMIT = 40 * 1024 * 1024
+EXPERT_VMEM = 16 * 1024 * 1024
+SMALL_VMEM = 8 * 1024 * 1024
 VMEM = pl.BlockSpec(memory_space=pltpu.VMEM)
-ANY = pl.BlockSpec(memory_space=pl.ANY)
+HBM = pl.BlockSpec(memory_space=pltpu.HBM)
 
 
 def exact_dot(one_hot, values):
@@ -81,6 +82,7 @@
         out_shape=pltpu.VMEM((devices, 4 * per_expert, width // 2), jnp.bfloat16),
         in_specs=[VMEM] * (6 + len(entering)),
         out_specs=VMEM,
+        compiler_params=pltpu.CompilerParams(vmem_limit_bytes=SMALL_VMEM),
     )(*routing, fwd, bwd, *entering)
 
 
@@ -139,14 +141,16 @@
         out_shape=out_shape,
         in_specs=[VMEM] * (7 + len(others)),
         out_specs=[VMEM] * 2,
+        compiler_params=pltpu.CompilerParams(vmem_limit_bytes=SMALL_VMEM),
     )(*routing, back, fwd, bwd, *others)
 
 
-def expert_kernel(
-    tick, in_chunk, out_chunk,
-    rows_ref, saved_ref, w_in_ref, w_out_ref, out_ref,
-    w_in, w_out, saved, fwd_rows, bwd_cols, joined, parts, in_sem, out_sem, saved_sem,
-):
+def expert_kernel(tick, loads, in_chunk, out_chunk, rows_ref, saved_ref, *rest):
+    if loads:
+        w_in_hbm, w_out_hbm, out_ref, w_in, w_out = rest[:5]
+    else:
+        w_in, w_out, out_ref = rest[:3]
+    saved, slot_rows, joined, parts, in_sem, out_sem, saved_sem = rest[-7:]
     devices, block, half_width = rows_ref.shape
     per_expert = block // 4
     slots = devices * per_expert
@@ -156,54 +160,64 @@
 
     def in_copy(index):
         at = pl.ds(index * in_chunk, in_chunk)
-        return pltpu.make_async_copy(w_in_ref.at[0, 0, at, :], w_in.at[at, :], in_sem.at[index])
+        return pltpu.make_async_copy(w_in_hbm.at[0, 0, at, :], w_in.at[at, :], in_sem.at[index])
 
     def out_copy(index):
         at = pl.ds(index * out_chunk, out_chunk)
-        return pltpu.make_async_copy(w_out_ref.at[0, 0, at, :], w_out.at[at, :], out_sem.at[index])
+        return pltpu.make_async_copy(w_out_hbm.at[0, 0, at, :], w_out.at[at, :], out_sem.at[index])
 
     saved_copy = pltpu.make_async_copy(saved_ref.at[tick, 0, 0], saved, saved_sem)
     saved_copy.start()
-    for index in range(hidden_units // out_chunk):
-        out_copy(index).start()
-    for index in range(width // in_chunk):
-        in_copy(index).start()
+    if loads:
+        for index in range(hidden_units // out_chunk):
+            out_copy(index).start()
+        for index in range(width // in_chunk):
+            in_copy(index).start()
 
     received = rows_ref[...].reshape(rows, half_width)
     slot = lax.broadcasted_iota(jnp.int32, (2 * slots, rows), 0)
     row = lax.broadcasted_iota(jnp.int32, (2 * slots, rows), 1)
     home = (slot % slots) // per_expert * block + slot // slots * per_expert + slot % per_expert
     for half in range(2):
-        columns = slice(half * half_width, (half + 1) * half_width)
         pick = jnp.where(row == home + half * 2 * per_expert, 1.0, 0.0)
-        picked = exact_dot(pick, received)
-        fwd_rows[:, columns] = picked[:slots].astype(jnp.bfloat16)
-        bwd_cols[columns, :] = picked[slots:].T.astype(jnp.bfloat16)
+        slot_rows[:, half * half_width : (half + 1) * half_width] = exact_dot(
+            pick, received
+        ).astype(jnp.bfloat16)
 
     saved_copy.wait()
-    gate_pre = saved[:, :hidden_units]
-    sigma = jax.nn.sigmoid(gate_pre)
-    slope = sigma * (1.0 + gate_pre * (1.0 - sigma))
-    gate_factor = (saved[:, hidden_units:] * slope).T
-    up_factor = (gate_pre * sigma).T
-
     for index in range(hidden_units // out_chunk):
-        out_copy(index).wait()
-        at = slice(index * out_chunk, (index + 1) * out_chunk)
-        grad = jnp.dot(w_out[at, :], bwd_cols[...], preferred_element_type=jnp.float32)
-        joined[at, :] = (grad * gate_factor[at]).astype(jnp.bfloat16)
-        joined[hidden_units + at.start : hidden_units + at.stop, :] = (
-            grad * up_factor[at]
+        if loads:
+            out_copy(index).wait()
+        start, stop = index * out_chunk, (index + 1) * out_chunk
+        grad = lax.dot_general(
+            slot_rows[slots:],
+            w_out[start:stop, :],
+            (((1,), (1,)), ((), ())),
+            preferred_element_type=jnp.float32,
+        )
+        gate_pre = saved[:, start:stop]
+        up_pre = saved[:, hidden_units + start : hidden_units + stop]
+        sigma = jax.nn.sigmoid(gate_pre)
+        slope = sigma * (1.0 + gate_pre * (1.0 - sigma))
+        joined[:, start:stop] = (grad * up_pre * slope).astype(jnp.bfloat16)
+        joined[:, hidden_units + start : hidden_units + stop] = (
+            grad * (gate_pre * sigma)
         ).astype(jnp.bfloat16)
 
     gate_up = jnp.zeros((slots, both), jnp.float32)
     for index in range(width // in_chunk):
-        in_copy(index).wait()
+        if loads:
+            in_copy(index).wait()
         at = slice(index * in_chunk, (index + 1) * in_chunk)
-        mat = w_in[at, :]
-        gate_up = gate_up + jnp.dot(fwd_rows[:, at], mat, preferred_element_type=jnp.float32)
-        part = jnp.dot(mat, joined[...], preferred_element_type=jnp.float32)
-        parts[slots:, at] = part.T.astype(jnp.bfloat16)
+        gate_up = gate_up + jnp.dot(
+            slot_rows[:slots, at], w_in[at, :], preferred_element_type=jnp.float32
+        )
+        parts[slots:, at] = lax.dot_general(
+            joined[...],
+            w_in[at, :],
+            (((1,), (1,)), ((), ())),
+            preferred_element_type=jnp.float32,
+        ).astype(jnp.bfloat16)
 
     gate = gate_up[:, :hidden_units]
     hidden = (gate * jax.nn.sigmoid(gate) * gate_up[:, hidden_units:]).astype(jnp.bfloat16)
@@ -224,33 +238,42 @@
 
 
 def expert_step(tick, rows, saved_pre, w_in, w_out):
-    width, hidden_units = w_in.shape[2], w_out.shape[2]
+    loads = w_in.ndim == 4
+    width, both = w_in.shape[-2:]
+    hidden_units = both // 2
     slots = saved_pre.shape[3]
     in_chunk, out_chunk = width // 7, min(hidden_units, 256)
+    out_shape = [pltpu.VMEM(rows.shape, jnp.bfloat16)]
+    if loads:
+        out_shape += [
+            pltpu.VMEM((width, both), jnp.bfloat16),
+            pltpu.VMEM((hidden_units, width), jnp.bfloat16),
+        ]
+    home = HBM if loads else VMEM
+    pinned = [pltpu.with_memory_space_constraint(saved_pre, pltpu.HBM), w_in, w_out]
+    if loads:
+        pinned[1:] = [pltpu.with_memory_space_constraint(w, pltpu.HBM) for w in (w_in, w_out)]
     return pl.pallas_call(
-        functools.partial(expert_kernel, tick, in_chunk, out_chunk),
-        out_shape=pltpu.VMEM(rows.shape, jnp.bfloat16),
-        in_specs=[VMEM, ANY, ANY, ANY],
-        out_specs=VMEM,
+        functools.partial(expert_kernel, tick, loads, in_chunk, out_chunk),
+        out_shape=out_shape,
+        in_specs=[VMEM, HBM, home, home],
+        out_specs=[VMEM] * len(out_shape),
         scratch_shapes=[
-            pltpu.VMEM((width, 2 * hidden_units), jnp.bfloat16),
-            pltpu.VMEM((hidden_units, width), jnp.bfloat16),
-            pltpu.VMEM((slots, 2 * hidden_units), jnp.float32),
-            pltpu.VMEM((slots, width), jnp.bfloat16),
-            pltpu.VMEM((width, slots), jnp.bfloat16),
-            pltpu.VMEM((2 * hidden_units, slots), jnp.bfloat16),
+            pltpu.VMEM((slots, both), jnp.float32),
+            pltpu.VMEM((2 * slots, width), jnp.bfloat16),
+            pltpu.VMEM((slots, both), jnp.bfloat16),
             pltpu.VMEM((2 * slots, width), jnp.bfloat16),
             pltpu.SemaphoreType.DMA((width // in_chunk,)),
             pltpu.SemaphoreType.DMA((hidden_units // out_chunk,)),
             pltpu.SemaphoreType.DMA,
         ],
-        compiler_params=pltpu.CompilerParams(vmem_limit_bytes=VMEM_LIMIT),
+        compiler_params=pltpu.CompilerParams(vmem_limit_bytes=EXPERT_VMEM),
         cost_estimate=pl.CostEstimate(
             flops=12 * slots * width * hidden_units,
             bytes_accessed=6 * width * hidden_units,
             transcendentals=0,
         ),
-    )(rows, saved_pre, w_in, w_out)
+    )(rows, *pinned)
 
 
 def exchange(array):
@@ -282,7 +305,8 @@
     fwd_now, bwd_now, entering, earlier = fwd_act, bwd_grad, (), ()
     for tick in range(TICKS):
         sent = pack(tick, devices, per_expert, slices, routing, fwd_now, bwd_now, *entering)
-        parts = expert_step(tick, exchange(sent), saved_pre, w_in, w_out)
+        parts, *kept = expert_step(tick, exchange(sent), saved_pre, w_in, w_out)
+        w_in, w_out = kept or (w_in, w_out)
         fwd_next, bwd_next = combine(
             tick, per_expert, slices, routing, exchange(parts), fwd_now, bwd_now, *entering, *earlier
         )

time: 105 us -> 94.6 us (0.901)
  Pallas kernels: 36.2 us -> 30.3 us
  local copies, waits for them, and re-layouts: 7.75 us -> 4.26 us
  blocking collectives: 50.8 us -> 49.5 us
    unnamed x16 -> x28, local copies, waits for them, and re-layouts: 7.75 us -> 4.26 us
    pallas_call x2, Pallas kernels: 3.83 us -> 1.73 us  [combine(): pl.pallas_call(functools.partial(combine_kernel, tick, per_expert, slices...]
    pallas_call x2, Pallas kernels: 29.8 us -> 27.7 us  [expert_step(): pl.pallas_call(functools.partial(expert_kernel, tick, loads, in_chunk, ou...]
    pallas_call x2, Pallas kernels: 2.65 us -> 0.93 us  [pack(): pl.pallas_call(functools.partial(pack_kernel, tick, per_expert, slices),...]
    all_to_all x4, blocking collectives: 50.8 us -> 49.5 us  [exchange(): lax.all_to_all(array, 'expert', split_axis=0, concat_axis=0, tiled=True)]
where the time goes in v3:
time: 94.6 us; the launch traced here: 94 us
  blocking collectives  49.5 us (52%)
  Pallas kernels  30.3 us (32%)
  starting transfers between devices  4.69 us (5%)
  waiting for transfers between devices  4.46 us (5%)
  local copies, waits for them, and re-layouts  4.26 us (5%)
    all_to_all x4, blocking collectives, exchange(): lax.all_to_all(array, 'expert', split_axis=0, concat_axis=0, tiled=True)  49.5 us
    pallas_call x2, Pallas kernels, expert_step(): pl.pallas_call(functools.partial(expert_kernel, tick, loads, in_chunk, ou...  27.7 us
    unnamed x28, local copies, waits for them, and re-layouts  4.26 us
    ppermute x1, waiting for transfers between devices, shards(): bwd_now = lax.ppermute(bwd_next, 'section', down)  4.22 us
    ppermute x1, starting transfers between devices, shards(): fwd_now = lax.ppermute(fwd_next, 'section', up)  3.4 us
  transfers between devices with their start and end apart: 2, of which 2 were waited for; matrix products, arithmetic and copies ran while one was open for 0% of the time, Pallas kernels for 0%

profile of v3, /device:TPU:0, one launch (start us, length us, event | category | flops | bytes accessed | tf_op | source)
XLA Modules:
  0.0 94.0 jit_solution(3978620305676799679)
XLA Ops:
  0.7 0.8 copy-done
  1.4 0.7 copy-done.2
  2.2 0.7 copy-done.6
  2.9 0.7 copy-done.8
  3.5 0.7 copy-done.10
  4.2 0.7 copy-done.12
  4.9 0.5 shard_map.122
  5.4 15.2 %all_to_all.20.rows_ref = bf16[8,8,1792]{2,1,0:T(8,128)(2,1)S(1)} all-to-all(bf16[8,8,1792]{2,1,0:T(8,128)(2,1)S(1)} %shard_map.122), channel_id=1, replica_groups=mesh['section'=4,'expert'=8] {'expert'}, dimensions={0} | all-to-all | bytes 458752 | tf_op jit(solution)/shard_map/all_to_all | solution.py:280
  20.6 17.7 %shard_map.123 = (bf16[8,8,1792]{2,1,0:T(8,128)(2,1)S(1)}, bf16[3584,2048]{1,0:T(8,128)(2,1)S(1)}, bf16[1024,3584]{1,0:T(8,128)(2,1)S(1)}) custom-call(bf16[8,8,1792]{2,1,0:T(8,128)(2,1)S(1)} %all_to_all.20.rows_ref, f32[2,1,1,16,2048]{4,3,2,1,0:T(8,128)} %saved_ref.3, bf16[1,1,3584,2048]{3,2,1,0:T(8,128)(2,1)} %rest_0_.3, bf16[1,1,1024,3584]{3,2,1,0:T(8,128)(2,1)} %rest_1_.3), custom_call_target="tpu_custom_call" | custom-call | flops 704643072 | bytes 22020096 | tf_op jit(solution)/shard_map/pallas_call | solution.py:256
  38.3 11.4 %all_to_all.21.back_ref = bf16[8,8,1792]{2,1,0:T(8,128)(2,1)S(1)} all-to-all(bf16[8,8,1792]{2,1,0:T(8,128)(2,1)S(1)} %get-tuple-element.7), channel_id=1, replica_groups=mesh['section'=4,'expert'=8] {'expert'}, dimensions={0} | all-to-all | bytes 458752 | tf_op jit(solution)/shard_map/all_to_all | solution.py:280
  49.8 0.0 copy-done.7
  49.8 0.0 copy-done.1
  49.8 0.0 copy-done.3
  49.8 0.0 copy-done.13
  49.8 0.6 shard_map.124
  50.4 3.4 %collective-permute-start = (bf16[4,3584]{1,0:T(4,128)(2,1)S(1)}, bf16[4,3584]{1,0:T(4,128)(2,1)S(1)}, u32[]{:S(2)}, u32[]{:S(2)}) collective-permute-start(bf16[4,3584]{1,0:T(4,128)(2,1)S(1)} %get-tuple-element.8.rest_2_), channel_id=1, source_target_pairs={{0,8},{8,16},{16,24},{1,9},{9,17},{17,25},{2,10},{10,18},{18,26},{... | collective-permute-start | bytes 86024 | tf_op jit(solution)/shard_map/ppermute | solution.py:316
  53.8 1.3 %collective-permute-start.1 = (bf16[4,3584]{1,0:T(4,128)(2,1)S(1)}, bf16[4,3584]{1,0:T(4,128)(2,1)S(1)}, u32[]{:S(2)}, u32[]{:S(2)}) collective-permute-start(bf16[4,3584]{1,0:T(4,128)(2,1)S(1)} %get-tuple-element.9.rest_3_), channel_id=1, source_target_pairs={{8,0},{16,8},{24,16},{9,1},{17,9},{25,17},{10,2},{18,10},{26,18},{... | collective-permute-start | bytes 86024 | tf_op jit(solution)/shard_map/ppermute | solution.py:317
  55.1 0.2 collective-permute-done.fwd_ref
  55.3 4.2 %collective-permute-done.1.bwd_ref = bf16[4,3584]{1,0:T(4,128)(2,1)S(1)} collective-permute-done((bf16[4,3584]{1,0:T(4,128)(2,1)S(1)}, bf16[4,3584]{1,0:T(4,128)(2,1)S(1)}, u32[]{:S(2)}, u32[]{:S(2)}) %collective-permute-start.1) | collective-permute-done | bytes 28704 | tf_op jit(solution)/shard_map/ppermute | solution.py:317
  59.5 0.5 shard_map.125
  60.0 11.4 %all_to_all.22.rows_ref = bf16[8,8,1792]{2,1,0:T(8,128)(2,1)S(1)} all-to-all(bf16[8,8,1792]{2,1,0:T(8,128)(2,1)S(1)} %shard_map.125), channel_id=1, replica_groups=mesh['section'=4,'expert'=8] {'expert'}, dimensions={0} | all-to-all | bytes 458752 | tf_op jit(solution)/shard_map/all_to_all | solution.py:280
  71.5 9.9 %shard_map.126 = bf16[8,8,1792]{2,1,0:T(8,128)(2,1)S(1)} custom-call(bf16[8,8,1792]{2,1,0:T(8,128)(2,1)S(1)} %all_to_all.22.rows_ref, f32[2,1,1,16,2048]{4,3,2,1,0:T(8,128)} %saved_ref.3, bf16[3584,2048]{1,0:T(8,128)(2,1)S(1)} %get-tuple-element.10.rest_0_, bf16[1024,3584]{1,0:T(8,128)(2,1)S(1)} %get-tuple-element.11.rest_1_), custom_call_target="tpu_custom_call" | custom-call | flops 704643072 | bytes 22020096 | tf_op jit(solution)/shard_map/pallas_call | solution.py:256
  81.4 11.4 %all_to_all.23.back_ref = bf16[8,8,1792]{2,1,0:T(8,128)(2,1)S(1)} all-to-all(bf16[8,8,1792]{2,1,0:T(8,128)(2,1)S(1)} %shard_map.126), channel_id=1, replica_groups=mesh['section'=4,'expert'=8] {'expert'}, dimensions={0} | all-to-all | bytes 458752 | tf_op jit(solution)/shard_map/all_to_all | solution.py:280
  92.8 1.2 %shard_map.127 = (bf16[2,1,4,3584]{3,2,1,0:T(4,128)(2,1)}, bf16[2,1,4,3584]{3,2,1,0:T(4,128)(2,1)}) custom-call(s32[2,1,2,4]{3,2,1,0:T(2,128)S(1)} %bitcast.7, f32[2,1,2,4]{3,2,1,0:T(2,128)S(1)} %bitcast.11, s32[2,1,2,4]{3,2,1,0:T(2,128)S(1)} %bitcast.15, f32[2,1,2,4]{3,2,1,0:T(2,128)S(1)} %bitcast.19, bf16[8,8,1792]{2,1,0:T(8,128)(2,1)S(1)} %all_to_all.23.back_ref, ...), custom_call_target="tpu_custom_call" | custom-call | tf_op jit(solution)/shard_map/pallas_call | solution.py:139
  (18 shorter events, 0.0 us)
Async XLA Ops:
  0.6 49.1 %copy-start.11 = (s32[2,1,4,2]{2,3,1,0:T(2,128)S(1)}, s32[2,1,4,2]{2,3,1,0:T(2,128)}, u32[]{:S(2)}) copy-start(s32[2,1,4,2]{2,3,1,0:T(2,128)} %param.19) | copy-start | bytes 196
  0.6 49.1 %copy-start.9 = (f32[2,1,4,2]{2,3,1,0:T(2,128)S(1)}, f32[2,1,4,2]{2,3,1,0:T(2,128)}, u32[]{:S(2)}) copy-start(f32[2,1,4,2]{2,3,1,0:T(2,128)} %param.18) | copy-start | bytes 196
  0.7 49.1 %copy-start.7 = (s32[2,1,4,2]{2,3,1,0:T(2,128)S(1)}, s32[2,1,4,2]{2,3,1,0:T(2,128)}, u32[]{:S(2)}) copy-start(s32[2,1,4,2]{2,3,1,0:T(2,128)} %param.17) | copy-start | bytes 196
  0.7 0.8 copy-start
  1.4 0.7 copy-start.2
  2.2 0.7 copy-start.6
  2.9 0.7 copy-start.8
  3.5 0.7 copy-start.10
  4.2 0.7 copy-start.12
  4.9 44.9 %copy-start.1 = (bf16[1,4,3584]{2,1,0:T(4,128)(2,1)S(1)}, bf16[1,4,3584]{2,1,0:T(4,128)(2,1)}, u32[]{:S(2)}) copy-start(bf16[1,4,3584]{2,1,0:T(4,128)(2,1)} %fwd_ref.3) | copy-start | bytes 86020
  4.9 44.9 %copy-start.3 = (bf16[1,4,3584]{2,1,0:T(4,128)(2,1)S(1)}, bf16[1,4,3584]{2,1,0:T(4,128)(2,1)}, u32[]{:S(2)}) copy-start(bf16[1,4,3584]{2,1,0:T(4,128)(2,1)} %bwd_ref.3) | copy-start | bytes 86020
  4.9 44.9 %copy-start.13 = (f32[2,1,4,2]{2,3,1,0:T(2,128)S(1)}, f32[2,1,4,2]{2,3,1,0:T(2,128)}, u32[]{:S(2)}) copy-start(f32[2,1,4,2]{2,3,1,0:T(2,128)} %param.20) | copy-start | bytes 196
  4.9 54.6 %copy-start.4 = (bf16[4,3584]{1,0:T(4,128)(2,1)S(1)}, bf16[4,3584]{1,0:T(4,128)(2,1)}, u32[]{:S(2)}) copy-start(bf16[4,3584]{1,0:T(4,128)(2,1)} %rest_0_.5) | copy-start | bytes 86020
  4.9 54.6 %copy-start.5 = (bf16[4,3584]{1,0:T(4,128)(2,1)S(1)}, bf16[4,3584]{1,0:T(4,128)(2,1)}, u32[]{:S(2)}) copy-start(bf16[4,3584]{1,0:T(4,128)(2,1)} %rest_1_.5) | copy-start | bytes 86020
  50.4 4.9 %collective-permute-start = (bf16[4,3584]{1,0:T(4,128)(2,1)S(1)}, bf16[4,3584]{1,0:T(4,128)(2,1)S(1)}, u32[]{:S(2)}, u32[]{:S(2)}) collective-permute-start(bf16[4,3584]{1,0:T(4,128)(2,1)S(1)} %get-tuple-element.8.rest_2_), channel_id=1, source_target_pairs={{0,8},{8,16},{16,24},{1,9},{9,17},{17,25},{2,10},{10,18},{18,26},{... | collective-permute-start | bytes 86024 | tf_op jit(solution)/shard_map/ppermute | solution.py:316
  53.8 5.8 %collective-permute-start.1 = (bf16[4,3584]{1,0:T(4,128)(2,1)S(1)}, bf16[4,3584]{1,0:T(4,128)(2,1)S(1)}, u32[]{:S(2)}, u32[]{:S(2)}) collective-permute-start(bf16[4,3584]{1,0:T(4,128)(2,1)S(1)} %get-tuple-element.9.rest_3_), channel_id=1, source_target_pairs={{8,0},{16,8},{24,16},{9,1},{17,9},{25,17},{10,2},{18,10},{26,18},{... | collective-permute-start | bytes 86024 | tf_op jit(solution)/shard_map/ppermute | solution.py:317

commit v4 on v3

--- a/solution.py
+++ b/solution.py
@@ -10,6 +10,7 @@
 FF = 1024
 TICKS = 2
 EXPERT_VMEM = 16 * 1024 * 1024
+IN_FLIGHT = 2
 SMALL_VMEM = 8 * 1024 * 1024
 VMEM = pl.BlockSpec(memory_space=pltpu.VMEM)
 HBM = pl.BlockSpec(memory_space=pltpu.HBM)
@@ -48,62 +49,100 @@
     return (row // (2 * per_expert)) % 2
 
 
-def pack_kernel(
-    tick, per_expert, slices,
-    fwd_route_ref, fwd_gate_ref, bwd_route_ref, bwd_gate_ref, fwd_ref, bwd_ref, *rest,
-):
-    devices, block, half_width = rest[-1].shape
-    out_ref = rest[-1]
+def whole_rows(rows_ref, index):
+    block = rows_ref[index]
+    count = block.shape[0] // 2
+    return block[:count], block[count:]
+
+
+def arriving(section_ref, enter_refs):
+    section, last = lax.axis_index("section"), lax.axis_size("section") - 1
+    pairs = []
+    for source, edge, enter_ref in (
+        (section - 1, section == 0, enter_refs[0]),
+        (section + 1, section == last, enter_refs[1]),
+    ):
+        halves = whole_rows(section_ref, jnp.clip(source, 0, last))
+        half_width = halves[0].shape[1]
+        pairs.append(
+            [
+                jnp.where(edge, enter_ref[:, half * half_width : (half + 1) * half_width], halves[half])
+                for half in range(2)
+            ]
+        )
+    return pairs
+
+
+def split_rows(rows):
+    half_width = rows.shape[-1] // 2
+    return [rows[:, :half_width], rows[:, half_width:]]
+
+
+def pack_into(out_ref, tick, per_expert, slices, tables, pairs):
+    devices, block, half_width = out_ref.shape
     rows = devices * block
-    fwd = fwd_ref[...].reshape(fwd_ref.shape[-2:])
-    bwd = bwd_ref[...].reshape(bwd_ref.shape[-2:])
-    if len(rest) == 3:
-        section = lax.axis_index("section")
-        fwd = jnp.where(section == 0, rest[0][...], fwd)
-        bwd = jnp.where(section == lax.axis_size("section") - 1, rest[1][...], bwd)
     total = jnp.zeros((rows, half_width), jnp.float32)
-    for direction, (route_ref, gate_ref, tokens) in enumerate(
-        ((fwd_route_ref, fwd_gate_ref, fwd), (bwd_route_ref, bwd_gate_ref, bwd))
-    ):
-        place, _ = placing(route_ref, gate_ref, tick, direction, rows, per_expert, slices)
+    for direction, halves in enumerate(pairs):
+        place, _ = placing(
+            tables[2 * direction], tables[2 * direction + 1], tick, direction, rows, per_expert, slices
+        )
         side = half_of(rows, place.shape[1], per_expert)
         for half in range(2):
-            total = total + exact_dot(
-                jnp.where(side == half, place, 0.0),
-                tokens[:, half * half_width : (half + 1) * half_width],
-            )
+            total = total + exact_dot(jnp.where(side == half, place, 0.0), halves[half])
     out_ref[...] = total.astype(jnp.bfloat16).reshape(out_ref.shape)
 
 
-def pack(tick, devices, per_expert, slices, routing, fwd, bwd, *entering):
-    width = fwd.shape[-1]
+def first_pack_kernel(tick, per_expert, slices, *refs):
+    operands, out_ref, local, sem = refs[:6], refs[6], refs[7:13], refs[13]
+    copies = [
+        pltpu.make_async_copy(source, target, sem.at[index])
+        for index, (source, target) in enumerate(zip(operands, local))
+    ]
+    for copy in copies:
+        copy.start()
+    for copy in copies:
+        copy.wait()
+    pairs = [split_rows(tokens_ref[0]) for tokens_ref in local[4:]]
+    pack_into(out_ref, tick, per_expert, slices, local[:4], pairs)
+
+
+def first_pack(tick, devices, per_expert, slices, routing, fwd, bwd):
+    operands = [*routing, fwd, bwd]
     return pl.pallas_call(
-        functools.partial(pack_kernel, tick, per_expert, slices),
-        out_shape=pltpu.VMEM((devices, 4 * per_expert, width // 2), jnp.bfloat16),
-        in_specs=[VMEM] * (6 + len(entering)),
+        functools.partial(first_pack_kernel, tick, per_expert, slices),
+        out_shape=pltpu.VMEM((devices, 4 * per_expert, fwd.shape[-1] // 2), jnp.bfloat16),
+        in_specs=[HBM] * len(operands),
+        out_specs=VMEM,
+        scratch_shapes=[pltpu.VMEM(operand.shape, operand.dtype) for operand in operands]
+        + [pltpu.SemaphoreType.DMA((len(operands),))],
+        compiler_params=pltpu.CompilerParams(vmem_limit_bytes=SMALL_VMEM),
+    )(*(pltpu.with_memory_space_constraint(operand, pltpu.HBM) for operand in operands))
+
+
+def later_pack_kernel(tick, per_expert, slices, *refs):
+    tables, section_ref, enter_refs, out_ref = refs[:4], refs[4], refs[5:7], refs[7]
+    pack_into(out_ref, tick, per_expert, slices, tables, arriving(section_ref, enter_refs))
+
+
+def later_pack(tick, devices, per_expert, slices, routing, arrived, *entering):
+    return pl.pallas_call(
+        functools.partial(later_pack_kernel, tick, per_expert, slices),
+        out_shape=pltpu.VMEM((devices, 4 * per_expert, arrived.shape[-1]), jnp.bfloat16),
+        in_specs=[VMEM] * 7,
         out_specs=VMEM,
         compiler_params=pltpu.CompilerParams(vmem_limit_bytes=SMALL_VMEM),
-    )(*routing, fwd, bwd, *entering)
-
-
-def combine_kernel(
-    tick, per_expert, slices,
-    fwd_route_ref, fwd_gate_ref, bwd_route_ref, bwd_gate_ref, back_ref, fwd_ref, bwd_ref, *rest,
-):
+    )(*routing, arrived, *entering)
+
+
+def mixed_halves(tick, per_expert, slices, tables, back_ref, pairs):
     devices, block, half_width = back_ref.shape
     rows = devices * block
-    fwd = fwd_ref[...].reshape(fwd_ref.shape[-2:])
-    bwd = bwd_ref[...].reshape(bwd_ref.shape[-2:])
-    last = len(rest) == 6
-    if last:
-        section = lax.axis_index("section")
-        fwd = jnp.where(section == 0, rest[0][...], fwd)
-        bwd = jnp.where(section == lax.axis_size("section") - 1, rest[1][...], bwd)
     back = back_ref[...].reshape(rows, half_width)
-    for direction, (route_ref, gate_ref, tokens) in enumerate(
-        ((fwd_route_ref, fwd_gate_ref, fwd), (bwd_route_ref, bwd_gate_ref, bwd))
-    ):
-        _, weight = placing(route_ref, gate_ref, tick, direction, rows, per_expert, slices)
+    results = []
+    for direction, halves in enumerate(pairs):
+        _, weight = placing(
+            tables[2 * direction], tables[2 * direction + 1], tick, direction, rows, per_expert, slices
+        )
         side = half_of(rows, weight.shape[1], per_expert)
         sides = jnp.concatenate(
             [jnp.where(side == half, weight, 0.0) for half in range(2)], axis=1
@@ -112,37 +151,76 @@
         left = sides - high.astype(jnp.float32)
         middle = left.astype(jnp.bfloat16)
         low = (left - middle.astype(jnp.float32)).astype(jnp.bfloat16)
-        mixed = jnp.zeros((sides.shape[1], half_width), jnp.float32)
+        mixed = jnp.concatenate(halves, axis=0).astype(jnp.float32)
         for term in (low, middle, high):
             mixed = mixed + lax.dot_general(
                 term, back, (((0,), (0,)), ((), ())), preferred_element_type=jnp.float32
             )
-        count = tokens.shape[0]
+        results.append(mixed.astype(jnp.bfloat16))
+    return results
+
+
+def relay_kernel(tick, per_expert, slices, *refs):
+    tables, back_ref, token_refs, section_ref, next_refs = refs[:4], refs[4], refs[5:7], refs[7], refs[8:]
+    half_width = back_ref.shape[2]
+    section, last = lax.axis_index("section"), lax.axis_size("section") - 1
+    pairs = [split_rows(tokens_ref[0]) for tokens_ref in token_refs]
+    results = mixed_halves(tick, per_expert, slices, tables, back_ref, pairs)
+    section_ref[...] = jnp.zeros_like(section_ref)
+    for result, next_ref in zip(results, next_refs):
+        count = result.shape[0] // 2
         for half in range(2):
-            columns = slice(half * half_width, (half + 1) * half_width)
-            value = tokens[:, columns].astype(jnp.float32) + mixed[half * count : (half + 1) * count]
-            if last:
-                rest[4 + direction][tick, 0, :, columns] = value.astype(jnp.bfloat16)
-            else:
-                rest[direction][:, columns] = value.astype(jnp.bfloat16)
-        if last:
-            for earlier in range(tick):
-                rest[4 + direction][earlier, 0] = rest[2 + direction][...]
-
-
-def combine(tick, per_expert, slices, routing, back, fwd, bwd, *others):
+            next_ref[:, half * half_width : (half + 1) * half_width] = result[
+                half * count : (half + 1) * count
+            ]
+
+    @pl.when(section < last)
+    def _():
+        section_ref[jnp.minimum(section + 1, last)] = results[0]
+
+    @pl.when(section > 0)
+    def _():
+        section_ref[jnp.maximum(section - 1, 0)] = results[1]
+
+
+def relay(tick, per_expert, slices, routing, back, fwd, bwd):
     tokens, width = fwd.shape[-2:]
-    if others:
-        out_shape = [jax.ShapeDtypeStruct((TICKS, 1, tokens, width), jnp.bfloat16)] * 2
-    else:
-        out_shape = [pltpu.VMEM((tokens, width), jnp.bfloat16)] * 2
+    sections = lax.axis_size("section")
     return pl.pallas_call(
-        functools.partial(combine_kernel, tick, per_expert, slices),
-        out_shape=out_shape,
-        in_specs=[VMEM] * (7 + len(others)),
+        functools.partial(relay_kernel, tick, per_expert, slices),
+        out_shape=[pltpu.VMEM((sections, 2 * tokens, width // 2), jnp.bfloat16)]
+        + [pltpu.VMEM((tokens, width), jnp.bfloat16)] * 2,
+        in_specs=[VMEM] * 7,
+        out_specs=[VMEM] * 3,
+        compiler_params=pltpu.CompilerParams(vmem_limit_bytes=SMALL_VMEM),
+    )(*routing, back, fwd, bwd)
+
+
+def finish_kernel(tick, per_expert, slices, *refs):
+    tables, back_ref, section_ref, enter_refs, earlier_refs, out_refs = (
+        refs[:4], refs[4], refs[5], refs[6:8], refs[8:10], refs[10:],
+    )
+    half_width = back_ref.shape[2]
+    pairs = arriving(section_ref, enter_refs)
+    results = mixed_halves(tick, per_expert, slices, tables, back_ref, pairs)
+    for result, earlier_ref, out_ref in zip(results, earlier_refs, out_refs):
+        count = result.shape[0] // 2
+        out_ref[0, 0] = earlier_ref[...]
+        for half in range(2):
+            out_ref[tick, 0, :, half * half_width : (half + 1) * half_width] = result[
+                half * count : (half + 1) * count
+            ]
+
+
+def finish(tick, per_expert, slices, routing, back, arrived, *others):
+    tokens, width = others[0].shape
+    return pl.pallas_call(
+        functools.partial(finish_kernel, tick, per_expert, slices),
+        out_shape=[jax.ShapeDtypeStruct((TICKS, 1, tokens, width), jnp.bfloat16)] * 2,
+        in_specs=[VMEM] * 10,
         out_specs=[VMEM] * 2,
         compiler_params=pltpu.CompilerParams(vmem_limit_bytes=SMALL_VMEM),
-    )(*routing, back, fwd, bwd, *others)
+    )(*routing, back, arrived, *others)
 
 
 def expert_kernel(tick, loads, in_chunk, out_chunk, rows_ref, saved_ref, *rest):
@@ -168,11 +246,18 @@
 
     saved_copy = pltpu.make_async_copy(saved_ref.at[tick, 0, 0], saved, saved_sem)
     saved_copy.start()
+    copies = []
     if loads:
-        for index in range(hidden_units // out_chunk):
-            out_copy(index).start()
-        for index in range(width // in_chunk):
-            in_copy(index).start()
+        copies = [out_copy(index) for index in range(hidden_units // out_chunk)]
+        copies += [in_copy(index) for index in range(width // in_chunk)]
+    for copy in copies[:IN_FLIGHT]:
+        copy.start()
+
+    def arrive(index):
+        if loads:
+            copies[index].wait()
+            if index + IN_FLIGHT < len(copies):
+                copies[index + IN_FLIGHT].start()
 
     received = rows_ref[...].reshape(rows, half_width)
     slot = lax.broadcasted_iota(jnp.int32, (2 * slots, rows), 0)
@@ -186,8 +271,7 @@
 
     saved_copy.wait()
     for index in range(hidden_units // out_chunk):
-        if loads:
-            out_copy(index).wait()
+        arrive(index)
         start, stop = index * out_chunk, (index + 1) * out_chunk
         grad = lax.dot_general(
             slot_rows[slots:],
@@ -206,8 +290,7 @@
 
     gate_up = jnp.zeros((slots, both), jnp.float32)
     for index in range(width // in_chunk):
-        if loads:
-            in_copy(index).wait()
+        arrive(hidden_units // out_chunk + index)
         at = slice(index * in_chunk, (index + 1) * in_chunk)
         gate_up = gate_up + jnp.dot(
             slot_rows[:slots, at], w_in[at, :], preferred_element_type=jnp.float32
@@ -276,8 +359,8 @@
     )(rows, *pinned)
 
 
-def exchange(array):
-    return lax.all_to_all(array, "expert", split_axis=0, concat_axis=0, tiled=True)
+def exchange(array, axis):
+    return lax.all_to_all(array, axis, split_axis=0, concat_axis=0, tiled=True)
 
 
 def shards(
@@ -296,26 +379,21 @@
     devices = lax.axis_size("expert")
     slices = FF // w_out.shape[2]
     per_expert = saved_pre.shape[3] // devices
-    section_total = lax.axis_size("section")
-    up = [(i, i + 1) for i in range(section_total - 1)]
-    down = [(j, i) for i, j in up]
     routing = [
         jnp.swapaxes(table, 2, 3) for table in (fwd_route, fwd_gate, bwd_route, bwd_gate)
     ]
-    fwd_now, bwd_now, entering, earlier = fwd_act, bwd_grad, (), ()
-    for tick in range(TICKS):
-        sent = pack(tick, devices, per_expert, slices, routing, fwd_now, bwd_now, *entering)
-        parts, *kept = expert_step(tick, exchange(sent), saved_pre, w_in, w_out)
-        w_in, w_out = kept or (w_in, w_out)
-        fwd_next, bwd_next = combine(
-            tick, per_expert, slices, routing, exchange(parts), fwd_now, bwd_now, *entering, *earlier
-        )
-        if tick + 1 < TICKS:
-            earlier = (fwd_next, bwd_next)
-            entering = (fwd_enter, bwd_enter)
-            fwd_now = lax.ppermute(fwd_next, "section", up)
-            bwd_now = lax.ppermute(bwd_next, "section", down)
-    return fwd_next, bwd_next
+    sent = first_pack(0, devices, per_expert, slices, routing, fwd_act, bwd_grad)
+    parts, w_in, w_out = expert_step(0, exchange(sent, "expert"), saved_pre, w_in, w_out)
+    moved, fwd_next, bwd_next = relay(
+        0, per_expert, slices, routing, exchange(parts, "expert"), fwd_act, bwd_grad
+    )
+    arrived = exchange(moved, "section")
+    sent = later_pack(1, devices, per_expert, slices, routing, arrived, fwd_enter, bwd_enter)
+    (parts,) = expert_step(1, exchange(sent, "expert"), saved_pre, w_in, w_out)
+    return finish(
+        1, per_expert, slices, routing, exchange(parts, "expert"), arrived,
+        fwd_enter, bwd_enter, fwd_next, bwd_next,
+    )
 
 
 def solution(mesh):

time: 94.6 us -> 86.3 us (0.912)
  blocking collectives: 49.5 us -> 58 us
  starting transfers between devices: 4.69 us -> 0 us
  waiting for transfers between devices: 4.46 us -> 0 us
  local copies, waits for them, and re-layouts: 4.26 us -> 0.03 us
  Pallas kernels: 30.3 us -> 27.2 us
    all_to_all x4 -> x5, blocking collectives: 49.5 us -> 58 us  [exchange(): return lax.all_to_all(array, axis, split_axis=0, concat_axis=0, tiled=True)]
    ppermute x2 -> x0, starting transfers between devices: 4.69 us -> none  [the longest x1 3.4 us: shards(): fwd_now = lax.ppermute(fwd_next, 'section', up)]
    ppermute x2 -> x0, waiting for transfers between devices: 4.46 us -> none  [the longest x1 4.22 us: shards(): bwd_now = lax.ppermute(bwd_next, 'section', down)]
    unnamed x28 -> x16, local copies, waits for them, and re-layouts: 4.26 us -> 0.03 us
    pallas_call x2, Pallas kernels: 27.7 us -> 23.5 us  [expert_step(): pl.pallas_call(functools.partial(expert_kernel, tick, loads, in_chunk, ou...]
    pallas_call x4, Pallas kernels: 2.66 us -> 3.64 us  [the longest x1 1.39 us: first_pack(): pl.pallas_call(functools.partial(first_pack_kernel, tick, per_expert, sli...]
  transfers between devices with their start and end apart: 2 -> 0, of which waited for: 2 -> 0; matrix products, arithmetic and copies ran while one was open for 0% -> 0% of each run, Pallas kernels for 0% -> 0%
where the time goes in v4:
time: 86.3 us; the launch traced here: 85.9 us
  blocking collectives  58 us (67%)
  Pallas kernels  27.2 us (32%)
    all_to_all x5, blocking collectives, exchange(): return lax.all_to_all(array, axis, split_axis=0, concat_axis=0, tiled=True)  58 us
    pallas_call x2, Pallas kernels, expert_step(): pl.pallas_call(functools.partial(expert_kernel, tick, loads, in_chunk, ou...  23.5 us

profile of v4, /device:TPU:0, one launch (start us, length us, event | category | flops | bytes accessed | tf_op | source)
XLA Modules:
  0.0 85.9 jit_solution(11300326673001111852)
XLA Ops:
  0.6 0.0 copy-start.3
  0.6 0.0 copy-start.2
  0.7 0.0 copy-start.7
  0.7 0.0 copy-start.6
  0.7 0.0 copy-start.5
  0.7 0.0 copy-start.4
  0.7 0.0 copy-start.1
  0.7 0.0 copy-start
  0.7 1.4 %shard_map.122 = bf16[8,8,1792]{2,1,0:T(8,128)(2,1)S(1)} custom-call(s32[2,1,2,4]{3,2,1,0:T(2,128)} %bitcast.4, f32[2,1,2,4]{3,2,1,0:T(2,128)} %bitcast.8, s32[2,1,2,4]{3,2,1,0:T(2,128)} %bitcast.12, f32[2,1,2,4]{3,2,1,0:T(2,128)} %bitcast.16, bf16[1,4,3584]{2,1,0:T(4,128)(2,1)} %refs_5_.4, bf16[1,4,3584]{2,1,0:T(4,128)(2,1)} %refs_6_.3), custom_call_target="tpu_custom_call" | custom-call | tf_op jit(solution)/shard_map/pallas_call | solution.py:111
  2.1 15.2 %all_to_all.25.rows_ref = bf16[8,8,1792]{2,1,0:T(8,128)(2,1)S(1)} all-to-all(bf16[8,8,1792]{2,1,0:T(8,128)(2,1)S(1)} %shard_map.122), channel_id=1, replica_groups=mesh['section'=4,'expert'=8] {'expert'}, dimensions={0} | all-to-all | bytes 458752 | tf_op jit(solution)/shard_map/all_to_all | solution.py:363
  17.3 13.6 %shard_map.123 = (bf16[8,8,1792]{2,1,0:T(8,128)(2,1)S(1)}, bf16[3584,2048]{1,0:T(8,128)(2,1)S(1)}, bf16[1024,3584]{1,0:T(8,128)(2,1)S(1)}) custom-call(bf16[8,8,1792]{2,1,0:T(8,128)(2,1)S(1)} %all_to_all.25.rows_ref, f32[2,1,1,16,2048]{4,3,2,1,0:T(8,128)} %saved_ref.3, bf16[1,1,3584,2048]{3,2,1,0:T(8,128)(2,1)} %rest_0_.1, bf16[1,1,1024,3584]{3,2,1,0:T(8,128)(2,1)} %rest_1_.1), custom_call_target="tpu_custom_call" | custom-call | flops 704643072 | bytes 22020096 | tf_op jit(solution)/shard_map/pallas_call | solution.py:339
  30.9 11.4 %all_to_all.26.refs_4_ = bf16[8,8,1792]{2,1,0:T(8,128)(2,1)S(1)} all-to-all(bf16[8,8,1792]{2,1,0:T(8,128)(2,1)S(1)} %get-tuple-element.8), channel_id=1, replica_groups=mesh['section'=4,'expert'=8] {'expert'}, dimensions={0} | all-to-all | bytes 458752 | tf_op jit(solution)/shard_map/all_to_all | solution.py:363
  42.3 0.0 copy-done.3
  42.3 0.0 copy-done.2
  42.3 0.0 copy-done.7
  42.3 0.0 copy-done.6
  42.3 0.0 copy-done.5
  42.4 0.6 shard_map.124
  42.9 8.5 %all_to_all.27.refs_4_.refs_5_ = bf16[4,8,1792]{2,1,0:T(8,128)(2,1)S(1)} all-to-all(bf16[4,8,1792]{2,1,0:T(8,128)(2,1)S(1)} %get-tuple-element.9), channel_id=1, replica_groups=mesh['section'=4,'expert'=8] {'section'}, dimensions={0} | all-to-all | bytes 229376 | tf_op jit(solution)/shard_map/all_to_all | solution.py:363
  51.4 0.5 shard_map.125
  51.9 11.4 %all_to_all.28.rows_ref = bf16[8,8,1792]{2,1,0:T(8,128)(2,1)S(1)} all-to-all(bf16[8,8,1792]{2,1,0:T(8,128)(2,1)S(1)} %shard_map.125), channel_id=1, replica_groups=mesh['section'=4,'expert'=8] {'expert'}, dimensions={0} | all-to-all | bytes 458752 | tf_op jit(solution)/shard_map/all_to_all | solution.py:363
  63.4 9.9 %shard_map.126 = bf16[8,8,1792]{2,1,0:T(8,128)(2,1)S(1)} custom-call(bf16[8,8,1792]{2,1,0:T(8,128)(2,1)S(1)} %all_to_all.28.rows_ref, f32[2,1,1,16,2048]{4,3,2,1,0:T(8,128)} %saved_ref.3, bf16[3584,2048]{1,0:T(8,128)(2,1)S(1)} %get-tuple-element.10.rest_0_, bf16[1024,3584]{1,0:T(8,128)(2,1)S(1)} %get-tuple-element.11.rest_1_), custom_call_target="tpu_custom_call" | custom-call | flops 704643072 | bytes 22020096 | tf_op jit(solution)/shard_map/pallas_call | solution.py:339
  73.3 11.4 %all_to_all.29.refs_4_ = bf16[8,8,1792]{2,1,0:T(8,128)(2,1)S(1)} all-to-all(bf16[8,8,1792]{2,1,0:T(8,128)(2,1)S(1)} %shard_map.126), channel_id=1, replica_groups=mesh['section'=4,'expert'=8] {'expert'}, dimensions={0} | all-to-all | bytes 458752 | tf_op jit(solution)/shard_map/all_to_all | solution.py:363
  84.7 1.2 %shard_map.127 = (bf16[2,1,4,3584]{3,2,1,0:T(4,128)(2,1)}, bf16[2,1,4,3584]{3,2,1,0:T(4,128)(2,1)}) custom-call(s32[2,1,2,4]{3,2,1,0:T(2,128)S(1)} %bitcast.7, f32[2,1,2,4]{3,2,1,0:T(2,128)S(1)} %bitcast.11, s32[2,1,2,4]{3,2,1,0:T(2,128)S(1)} %bitcast.15, f32[2,1,2,4]{3,2,1,0:T(2,128)S(1)} %bitcast.19, bf16[8,8,1792]{2,1,0:T(8,128)(2,1)S(1)} %all_to_all.29.refs_4_, ...), custom_call_target="tpu_custom_call" | custom-call | tf_op jit(solution)/shard_map/pallas_call | solution.py:217
  (3 shorter events, 0.0 us)
Async XLA Ops:
  0.6 41.7 %copy-start.3 = (bf16[1,4,3584]{2,1,0:T(4,128)(2,1)S(1)}, bf16[1,4,3584]{2,1,0:T(4,128)(2,1)}, u32[]{:S(2)}) copy-start(bf16[1,4,3584]{2,1,0:T(4,128)(2,1)} %refs_6_.3) | copy-start | bytes 86020
  0.6 41.7 %copy-start.2 = (bf16[1,4,3584]{2,1,0:T(4,128)(2,1)S(1)}, bf16[1,4,3584]{2,1,0:T(4,128)(2,1)}, u32[]{:S(2)}) copy-start(bf16[1,4,3584]{2,1,0:T(4,128)(2,1)} %refs_5_.4) | copy-start | bytes 86020
  0.7 41.7 %copy-start.7 = (f32[2,1,4,2]{2,3,1,0:T(2,128)S(1)}, f32[2,1,4,2]{2,3,1,0:T(2,128)}, u32[]{:S(2)}) copy-start(f32[2,1,4,2]{2,3,1,0:T(2,128)} %param.20) | copy-start | bytes 196
  0.7 41.7 %copy-start.6 = (s32[2,1,4,2]{2,3,1,0:T(2,128)S(1)}, s32[2,1,4,2]{2,3,1,0:T(2,128)}, u32[]{:S(2)}) copy-start(s32[2,1,4,2]{2,3,1,0:T(2,128)} %param.19) | copy-start | bytes 196
  0.7 41.7 %copy-start.5 = (f32[2,1,4,2]{2,3,1,0:T(2,128)S(1)}, f32[2,1,4,2]{2,3,1,0:T(2,128)}, u32[]{:S(2)}) copy-start(f32[2,1,4,2]{2,3,1,0:T(2,128)} %param.18) | copy-start | bytes 196
  0.7 41.7 %copy-start.4 = (s32[2,1,4,2]{2,3,1,0:T(2,128)S(1)}, s32[2,1,4,2]{2,3,1,0:T(2,128)}, u32[]{:S(2)}) copy-start(s32[2,1,4,2]{2,3,1,0:T(2,128)} %param.17) | copy-start | bytes 196
  0.7 50.7 %copy-start.1 = (bf16[4,3584]{1,0:T(4,128)(2,1)S(1)}, bf16[4,3584]{1,0:T(4,128)(2,1)}, u32[]{:S(2)}) copy-start(bf16[4,3584]{1,0:T(4,128)(2,1)} %refs_7_.1) | copy-start | bytes 86020
  0.7 50.7 %copy-start = (bf16[4,3584]{1,0:T(4,128)(2,1)S(1)}, bf16[4,3584]{1,0:T(4,128)(2,1)}, u32[]{:S(2)}) copy-start(bf16[4,3584]{1,0:T(4,128)(2,1)} %refs_6_.5) | copy-start | bytes 86020

commit v5 on v4

--- a/solution.py
+++ b/solution.py
@@ -10,7 +10,7 @@
 FF = 1024
 TICKS = 2
 EXPERT_VMEM = 16 * 1024 * 1024
-IN_FLIGHT = 2
+BESIDE = 2000
 SMALL_VMEM = 8 * 1024 * 1024
 VMEM = pl.BlockSpec(memory_space=pltpu.VMEM)
 HBM = pl.BlockSpec(memory_space=pltpu.HBM)
@@ -106,7 +106,7 @@
     pack_into(out_ref, tick, per_expert, slices, local[:4], pairs)
 
 
-def first_pack(tick, devices, per_expert, slices, routing, fwd, bwd):
+def first_pack(tick, devices, per_expert, slices, routing, fwd, bwd, beside):
     operands = [*routing, fwd, bwd]
     return pl.pallas_call(
         functools.partial(first_pack_kernel, tick, per_expert, slices),
@@ -116,6 +116,7 @@
         scratch_shapes=[pltpu.VMEM(operand.shape, operand.dtype) for operand in operands]
         + [pltpu.SemaphoreType.DMA((len(operands),))],
         compiler_params=pltpu.CompilerParams(vmem_limit_bytes=SMALL_VMEM),
+        cost_estimate=pl.CostEstimate(flops=beside, bytes_accessed=0, transcendentals=0),
     )(*(pltpu.with_memory_space_constraint(operand, pltpu.HBM) for operand in operands))
 
 
@@ -223,12 +224,8 @@
     )(*routing, back, arrived, *others)
 
 
-def expert_kernel(tick, loads, in_chunk, out_chunk, rows_ref, saved_ref, *rest):
-    if loads:
-        w_in_hbm, w_out_hbm, out_ref, w_in, w_out = rest[:5]
-    else:
-        w_in, w_out, out_ref = rest[:3]
-    saved, slot_rows, joined, parts, in_sem, out_sem, saved_sem = rest[-7:]
+def expert_kernel(tick, rows_ref, saved_ref, w_in, w_out, out_ref, *rest):
+    saved, slot_rows, joined, parts, saved_sem = rest[-5:]
     devices, block, half_width = rows_ref.shape
     per_expert = block // 4
     slots = devices * per_expert
@@ -236,28 +233,8 @@
     hidden_units = both // 2
     rows = devices * block
 
-    def in_copy(index):
-        at = pl.ds(index * in_chunk, in_chunk)
-        return pltpu.make_async_copy(w_in_hbm.at[0, 0, at, :], w_in.at[at, :], in_sem.at[index])
-
-    def out_copy(index):
-        at = pl.ds(index * out_chunk, out_chunk)
-        return pltpu.make_async_copy(w_out_hbm.at[0, 0, at, :], w_out.at[at, :], out_sem.at[index])
-
     saved_copy = pltpu.make_async_copy(saved_ref.at[tick, 0, 0], saved, saved_sem)
     saved_copy.start()
-    copies = []
-    if loads:
-        copies = [out_copy(index) for index in range(hidden_units // out_chunk)]
-        copies += [in_copy(index) for index in range(width // in_chunk)]
-    for copy in copies[:IN_FLIGHT]:
-        copy.start()
-
-    def arrive(index):
-        if loads:
-            copies[index].wait()
-            if index + IN_FLIGHT < len(copies):
-                copies[index + IN_FLIGHT].start()
 
     received = rows_ref[...].reshape(rows, half_width)
     slot = lax.broadcasted_iota(jnp.int32, (2 * slots, rows), 0)
@@ -269,46 +246,27 @@
             pick, received
         ).astype(jnp.bfloat16)
 
+    grad = lax.dot_general(
+        slot_rows[slots:],
+        w_out[...],
+        (((1,), (1,)), ((), ())),
+        preferred_element_type=jnp.float32,
+    )
+    gate_up = jnp.dot(slot_rows[:slots], w_in[...], preferred_element_type=jnp.float32)
     saved_copy.wait()
-    for index in range(hidden_units // out_chunk):
-        arrive(index)
-        start, stop = index * out_chunk, (index + 1) * out_chunk
-        grad = lax.dot_general(
-            slot_rows[slots:],
-            w_out[start:stop, :],
-            (((1,), (1,)), ((), ())),
-            preferred_element_type=jnp.float32,
-        )
-        gate_pre = saved[:, start:stop]
-        up_pre = saved[:, hidden_units + start : hidden_units + stop]
-        sigma = jax.nn.sigmoid(gate_pre)
-        slope = sigma * (1.0 + gate_pre * (1.0 - sigma))
-        joined[:, start:stop] = (grad * up_pre * slope).astype(jnp.bfloat16)
-        joined[:, hidden_units + start : hidden_units + stop] = (
-            grad * (gate_pre * sigma)
-        ).astype(jnp.bfloat16)
-
-    gate_up = jnp.zeros((slots, both), jnp.float32)
-    for index in range(width // in_chunk):
-        arrive(hidden_units // out_chunk + index)
-        at = slice(index * in_chunk, (index + 1) * in_chunk)
-        gate_up = gate_up + jnp.dot(
-            slot_rows[:slots, at], w_in[at, :], preferred_element_type=jnp.float32
-        )
-        parts[slots:, at] = lax.dot_general(
-            joined[...],
-            w_in[at, :],
-            (((1,), (1,)), ((), ())),
-            preferred_element_type=jnp.float32,
-        ).astype(jnp.bfloat16)
-
+    gate_pre = saved[:, :hidden_units]
+    sigma = jax.nn.sigmoid(gate_pre)
+    slope = sigma * (1.0 + gate_pre * (1.0 - sigma))
+    joined[:, :hidden_units] = (grad * saved[:, hidden_units:] * slope).astype(jnp.bfloat16)
+    joined[:, hidden_units:] = (grad * (gate_pre * sigma)).astype(jnp.bfloat16)
     gate = gate_up[:, :hidden_units]
     hidden = (gate * jax.nn.sigmoid(gate) * gate_up[:, hidden_units:]).astype(jnp.bfloat16)
-    for half in range(2):
-        columns = slice(half * half_width, (half + 1) * half_width)
-        parts[:slots, columns] = jnp.dot(
-            hidden, w_out[:, columns], preferred_element_type=jnp.float32
-        ).astype(jnp.bfloat16)
+    parts[slots:] = lax.dot_general(
+        joined[...], w_in[...], (((1,), (1,)), ((), ())), preferred_element_type=jnp.float32
+    ).astype(jnp.bfloat16)
+    parts[:slots] = jnp.dot(hidden, w_out[...], preferred_element_type=jnp.float32).astype(
+        jnp.bfloat16
+    )
 
     row = lax.broadcasted_iota(jnp.int32, (rows, 2 * slots), 0)
     slot = lax.broadcasted_iota(jnp.int32, (rows, 2 * slots), 1)
@@ -321,42 +279,27 @@
 
 
 def expert_step(tick, rows, saved_pre, w_in, w_out):
-    loads = w_in.ndim == 4
-    width, both = w_in.shape[-2:]
-    hidden_units = both // 2
+    width, both = w_in.shape
     slots = saved_pre.shape[3]
-    in_chunk, out_chunk = width // 7, min(hidden_units, 256)
-    out_shape = [pltpu.VMEM(rows.shape, jnp.bfloat16)]
-    if loads:
-        out_shape += [
-            pltpu.VMEM((width, both), jnp.bfloat16),
-            pltpu.VMEM((hidden_units, width), jnp.bfloat16),
-        ]
-    home = HBM if loads else VMEM
-    pinned = [pltpu.with_memory_space_constraint(saved_pre, pltpu.HBM), w_in, w_out]
-    if loads:
-        pinned[1:] = [pltpu.with_memory_space_constraint(w, pltpu.HBM) for w in (w_in, w_out)]
-    return pl.pallas_call(
-        functools.partial(expert_kernel, tick, loads, in_chunk, out_chunk),
-        out_shape=out_shape,
-        in_specs=[VMEM, HBM, home, home],
-        out_specs=[VMEM] * len(out_shape),
+    return pl.pallas_call(
+        functools.partial(expert_kernel, tick),
+        out_shape=pltpu.VMEM(rows.shape, jnp.bfloat16),
+        in_specs=[VMEM, HBM, VMEM, VMEM],
+        out_specs=VMEM,
         scratch_shapes=[
             pltpu.VMEM((slots, both), jnp.float32),
             pltpu.VMEM((2 * slots, width), jnp.bfloat16),
             pltpu.VMEM((slots, both), jnp.bfloat16),
             pltpu.VMEM((2 * slots, width), jnp.bfloat16),
-            pltpu.SemaphoreType.DMA((width // in_chunk,)),
-            pltpu.SemaphoreType.DMA((hidden_units // out_chunk,)),
             pltpu.SemaphoreType.DMA,
         ],
         compiler_params=pltpu.CompilerParams(vmem_limit_bytes=EXPERT_VMEM),
         cost_estimate=pl.CostEstimate(
-            flops=12 * slots * width * hidden_units,
-            bytes_accessed=6 * width * hidden_units,
+            flops=12 * slots * width * (both // 2),
+            bytes_accessed=0,
             transcendentals=0,
         ),
-    )(rows, *pinned)
+    )(rows, pltpu.with_memory_space_constraint(saved_pre, pltpu.HBM), w_in, w_out)
 
 
 def exchange(array, axis):
@@ -382,14 +325,18 @@
     routing = [
         jnp.swapaxes(table, 2, 3) for table in (fwd_route, fwd_gate, bwd_route, bwd_gate)
     ]
-    sent = first_pack(0, devices, per_expert, slices, routing, fwd_act, bwd_grad)
-    parts, w_in, w_out = expert_step(0, exchange(sent, "expert"), saved_pre, w_in, w_out)
+    beside = BESIDE * (w_in.size + w_out.size)
+    w_in, w_out = (
+        pltpu.with_memory_space_constraint(w.reshape(w.shape[2:]), pltpu.VMEM) for w in (w_in, w_out)
+    )
+    sent = first_pack(0, devices, per_expert, slices, routing, fwd_act, bwd_grad, beside)
+    parts = expert_step(0, exchange(sent, "expert"), saved_pre, w_in, w_out)
     moved, fwd_next, bwd_next = relay(
         0, per_expert, slices, routing, exchange(parts, "expert"), fwd_act, bwd_grad
     )
     arrived = exchange(moved, "section")
     sent = later_pack(1, devices, per_expert, slices, routing, arrived, fwd_enter, bwd_enter)
-    (parts,) = expert_step(1, exchange(sent, "expert"), saved_pre, w_in, w_out)
+    parts = expert_step(1, exchange(sent, "expert"), saved_pre, w_in, w_out)
     return finish(
         1, per_expert, slices, routing, exchange(parts, "expert"), arrived,
         fwd_enter, bwd_enter, fwd_next, bwd_next,

time: 86.3 us -> 81.3 us (0.942)
  Pallas kernels: 27.2 us -> 21.9 us
    pallas_call x2, Pallas kernels: 23.5 us -> 18.2 us  [expert_step(): pl.pallas_call(functools.partial(expert_kernel, tick), out_shape=pltpu.VM...]
where the time goes in v5:
time: 81.3 us; the launch traced here: 81 us
  blocking collectives  58.2 us (72%)
  Pallas kernels  21.9 us (27%)
    all_to_all x5, blocking collectives, exchange(): return lax.all_to_all(array, axis, split_axis=0, concat_axis=0, tiled=True)  58.2 us
    pallas_call x2, Pallas kernels, expert_step(): pl.pallas_call(functools.partial(expert_kernel, tick), out_shape=pltpu.VM...  18.2 us

profile of v5, /device:TPU:0, one launch (start us, length us, event | category | flops | bytes accessed | tf_op | source)
XLA Modules:
  0.0 81.0 jit_solution(10056969082571009050)
XLA Ops:
  0.6 0.0 copy-start
  0.6 0.0 copy-start.1
  0.6 1.5 %shard_map.122 = bf16[8,8,1792]{2,1,0:T(8,128)(2,1)S(1)} custom-call(s32[2,1,2,4]{3,2,1,0:T(2,128)} %bitcast.10, f32[2,1,2,4]{3,2,1,0:T(2,128)} %bitcast.14, s32[2,1,2,4]{3,2,1,0:T(2,128)} %bitcast.18, f32[2,1,2,4]{3,2,1,0:T(2,128)} %bitcast.22, bf16[1,4,3584]{2,1,0:T(4,128)(2,1)} %refs_5_.4, bf16[1,4,3584]{2,1,0:T(4,128)(2,1)} %refs_6_.3), custom_call_target="tpu_custom_call" | custom-call | flops 22020096000 | tf_op jit(solution)/shard_map/pallas_call | solution.py:111
  2.2 0.0 copy-start.4
  2.2 0.0 copy-start.5
  2.2 0.0 copy-start.6
  2.2 0.0 copy-start.7
  2.2 0.0 copy-start.8
  2.2 0.0 copy-start.9
  2.2 0.0 copy-start.2
  2.2 0.0 copy-start.3
  2.2 15.4 %all_to_all.25.rows_ref = bf16[8,8,1792]{2,1,0:T(8,128)(2,1)S(1)} all-to-all(bf16[8,8,1792]{2,1,0:T(8,128)(2,1)S(1)} %shard_map.122), channel_id=1, replica_groups=mesh['section'=4,'expert'=8] {'expert'}, dimensions={0} | all-to-all | bytes 458752 | tf_op jit(solution)/shard_map/all_to_all | solution.py:306
  17.7 0.0 copy-done
  17.7 9.1 %shard_map.123 = bf16[8,8,1792]{2,1,0:T(8,128)(2,1)S(1)} custom-call(bf16[8,8,1792]{2,1,0:T(8,128)(2,1)S(1)} %all_to_all.25.rows_ref, f32[2,1,1,16,2048]{4,3,2,1,0:T(8,128)} %saved_ref.3, bf16[3584,2048]{1,0:T(8,128)(2,1)S(1)} %bitcast.6, bf16[1024,3584]{1,0:T(8,128)(2,1)S(1)} %bitcast.8), custom_call_target="tpu_custom_call" | custom-call | flops 704643072 | tf_op jit(solution)/shard_map/pallas_call | solution.py:284
  26.8 11.4 %all_to_all.26.refs_4_ = bf16[8,8,1792]{2,1,0:T(8,128)(2,1)S(1)} all-to-all(bf16[8,8,1792]{2,1,0:T(8,128)(2,1)S(1)} %shard_map.123), channel_id=1, replica_groups=mesh['section'=4,'expert'=8] {'expert'}, dimensions={0} | all-to-all | bytes 458752 | tf_op jit(solution)/shard_map/all_to_all | solution.py:306
  38.2 0.0 copy-done.4
  38.3 0.6 shard_map.124
  38.8 8.5 %all_to_all.27.refs_4_.refs_5_ = bf16[4,8,1792]{2,1,0:T(8,128)(2,1)S(1)} all-to-all(bf16[4,8,1792]{2,1,0:T(8,128)(2,1)S(1)} %get-tuple-element.5), channel_id=1, replica_groups=mesh['section'=4,'expert'=8] {'section'}, dimensions={0} | all-to-all | bytes 229376 | tf_op jit(solution)/shard_map/all_to_all | solution.py:306
  47.3 0.0 copy-done.3
  47.3 0.5 shard_map.125
  47.8 11.4 %all_to_all.28.rows_ref = bf16[8,8,1792]{2,1,0:T(8,128)(2,1)S(1)} all-to-all(bf16[8,8,1792]{2,1,0:T(8,128)(2,1)S(1)} %shard_map.125), channel_id=1, replica_groups=mesh['section'=4,'expert'=8] {'expert'}, dimensions={0} | all-to-all | bytes 458752 | tf_op jit(solution)/shard_map/all_to_all | solution.py:306
  59.3 9.1 %shard_map.126 = bf16[8,8,1792]{2,1,0:T(8,128)(2,1)S(1)} custom-call(bf16[8,8,1792]{2,1,0:T(8,128)(2,1)S(1)} %all_to_all.28.rows_ref, f32[2,1,1,16,2048]{4,3,2,1,0:T(8,128)} %saved_ref.3, bf16[3584,2048]{1,0:T(8,128)(2,1)S(1)} %bitcast.7, bf16[1024,3584]{1,0:T(8,128)(2,1)S(1)} %bitcast.9), custom_call_target="tpu_custom_call" | custom-call | flops 704643072 | tf_op jit(solution)/shard_map/pallas_call | solution.py:284
  68.4 11.4 %all_to_all.29.refs_4_ = bf16[8,8,1792]{2,1,0:T(8,128)(2,1)S(1)} all-to-all(bf16[8,8,1792]{2,1,0:T(8,128)(2,1)S(1)} %shard_map.126), channel_id=1, replica_groups=mesh['section'=4,'expert'=8] {'expert'}, dimensions={0} | all-to-all | bytes 458752 | tf_op jit(solution)/shard_map/all_to_all | solution.py:306
  79.8 1.2 %shard_map.127 = (bf16[2,1,4,3584]{3,2,1,0:T(4,128)(2,1)}, bf16[2,1,4,3584]{3,2,1,0:T(4,128)(2,1)}) custom-call(s32[2,1,2,4]{3,2,1,0:T(2,128)S(1)} %bitcast.13, f32[2,1,2,4]{3,2,1,0:T(2,128)S(1)} %bitcast.17, s32[2,1,2,4]{3,2,1,0:T(2,128)S(1)} %bitcast.21, f32[2,1,2,4]{3,2,1,0:T(2,128)S(1)} %bitcast.25, bf16[8,8,1792]{2,1,0:T(8,128)(2,1)S(1)} %all_to_all.29.refs_4_, ...), custom_call_target="tpu_custom_call" | custom-call | tf_op jit(solution)/shard_map/pallas_call | solution.py:218
  (7 shorter events, 0.0 us)
Async XLA Ops:
  0.6 17.0 %copy-start = (bf16[1,1,3584,2048]{3,2,1,0:T(8,128)(2,1)S(1)}, bf16[1,1,3584,2048]{3,2,1,0:T(8,128)(2,1)}, u32[]{:S(2)}) copy-start(bf16[1,1,3584,2048]{3,2,1,0:T(8,128)(2,1)} %param.15) | copy-start | bytes 44040196
  0.6 17.0 %copy-start.1 = (bf16[1,1,1024,3584]{3,2,1,0:T(8,128)(2,1)S(1)}, bf16[1,1,1024,3584]{3,2,1,0:T(8,128)(2,1)}, u32[]{:S(2)}) copy-start(bf16[1,1,1024,3584]{3,2,1,0:T(8,128)(2,1)} %param.16) | copy-start | bytes 22020100
  2.2 36.1 %copy-start.4 = (bf16[1,4,3584]{2,1,0:T(4,128)(2,1)S(1)}, bf16[1,4,3584]{2,1,0:T(4,128)(2,1)}, u32[]{:S(2)}) copy-start(bf16[1,4,3584]{2,1,0:T(4,128)(2,1)} %refs_5_.4) | copy-start | bytes 86020
  2.2 36.1 %copy-start.5 = (bf16[1,4,3584]{2,1,0:T(4,128)(2,1)S(1)}, bf16[1,4,3584]{2,1,0:T(4,128)(2,1)}, u32[]{:S(2)}) copy-start(bf16[1,4,3584]{2,1,0:T(4,128)(2,1)} %refs_6_.3) | copy-start | bytes 86020
  2.2 36.0 %copy-start.6 = (s32[2,1,4,2]{2,3,1,0:T(2,128)S(1)}, s32[2,1,4,2]{2,3,1,0:T(2,128)}, u32[]{:S(2)}) copy-start(s32[2,1,4,2]{2,3,1,0:T(2,128)} %param.17) | copy-start | bytes 196
  2.2 36.0 %copy-start.7 = (f32[2,1,4,2]{2,3,1,0:T(2,128)S(1)}, f32[2,1,4,2]{2,3,1,0:T(2,128)}, u32[]{:S(2)}) copy-start(f32[2,1,4,2]{2,3,1,0:T(2,128)} %param.18) | copy-start | bytes 196
  2.2 36.0 %copy-start.8 = (s32[2,1,4,2]{2,3,1,0:T(2,128)S(1)}, s32[2,1,4,2]{2,3,1,0:T(2,128)}, u32[]{:S(2)}) copy-start(s32[2,1,4,2]{2,3,1,0:T(2,128)} %param.19) | copy-start | bytes 196
  2.2 36.0 %copy-start.9 = (f32[2,1,4,2]{2,3,1,0:T(2,128)S(1)}, f32[2,1,4,2]{2,3,1,0:T(2,128)}, u32[]{:S(2)}) copy-start(f32[2,1,4,2]{2,3,1,0:T(2,128)} %param.20) | copy-start | bytes 196
  2.2 45.1 %copy-start.2 = (bf16[4,3584]{1,0:T(4,128)(2,1)S(1)}, bf16[4,3584]{1,0:T(4,128)(2,1)}, u32[]{:S(2)}) copy-start(bf16[4,3584]{1,0:T(4,128)(2,1)} %refs_6_.5) | copy-start | bytes 86020
  2.2 45.1 %copy-start.3 = (bf16[4,3584]{1,0:T(4,128)(2,1)S(1)}, bf16[4,3584]{1,0:T(4,128)(2,1)}, u32[]{:S(2)}) copy-start(bf16[4,3584]{1,0:T(4,128)(2,1)} %refs_7_.1) | copy-start | bytes 86020

commit v6 on v5

--- a/solution.py
+++ b/solution.py
@@ -11,6 +11,7 @@
 TICKS = 2
 EXPERT_VMEM = 16 * 1024 * 1024
 BESIDE = 2000
+COLUMNS = 256
 SMALL_VMEM = 8 * 1024 * 1024
 VMEM = pl.BlockSpec(memory_space=pltpu.VMEM)
 HBM = pl.BlockSpec(memory_space=pltpu.HBM)
@@ -198,19 +199,28 @@
 
 
 def finish_kernel(tick, per_expert, slices, *refs):
-    tables, back_ref, section_ref, enter_refs, earlier_refs, out_refs = (
-        refs[:4], refs[4], refs[5], refs[6:8], refs[8:10], refs[10:],
+    tables, back_ref, section_ref, enter_refs, earlier_refs, out_refs, new_refs, sem = (
+        refs[:4], refs[4], refs[5], refs[6:8], refs[8:10], refs[10:12], refs[12:14], refs[14],
     )
     half_width = back_ref.shape[2]
+    copies = [
+        pltpu.make_async_copy(source, out_ref.at[place, 0], sem.at[place, direction])
+        for place, sources in ((0, earlier_refs), (tick, new_refs))
+        for direction, (source, out_ref) in enumerate(zip(sources, out_refs))
+    ]
+    for copy in copies[:2]:
+        copy.start()
     pairs = arriving(section_ref, enter_refs)
     results = mixed_halves(tick, per_expert, slices, tables, back_ref, pairs)
-    for result, earlier_ref, out_ref in zip(results, earlier_refs, out_refs):
+    for result, new_ref, copy in zip(results, new_refs, copies[2:]):
         count = result.shape[0] // 2
-        out_ref[0, 0] = earlier_ref[...]
         for half in range(2):
-            out_ref[tick, 0, :, half * half_width : (half + 1) * half_width] = result[
+            new_ref[:, half * half_width : (half + 1) * half_width] = result[
                 half * count : (half + 1) * count
             ]
+        copy.start()
+    for copy in copies:
+        copy.wait()
 
 
 def finish(tick, per_expert, slices, routing, back, arrived, *others):
@@ -219,13 +229,15 @@
         functools.partial(finish_kernel, tick, per_expert, slices),
         out_shape=[jax.ShapeDtypeStruct((TICKS, 1, tokens, width), jnp.bfloat16)] * 2,
         in_specs=[VMEM] * 10,
-        out_specs=[VMEM] * 2,
+        out_specs=[HBM] * 2,
+        scratch_shapes=[pltpu.VMEM((tokens, width), jnp.bfloat16)] * 2
+        + [pltpu.SemaphoreType.DMA((TICKS, 2))],
         compiler_params=pltpu.CompilerParams(vmem_limit_bytes=SMALL_VMEM),
     )(*routing, back, arrived, *others)
 
 
 def expert_kernel(tick, rows_ref, saved_ref, w_in, w_out, out_ref, *rest):
-    saved, slot_rows, joined, parts, saved_sem = rest[-5:]
+    saved, slot_rows, joined, hidden, saved_sem = rest
     devices, block, half_width = rows_ref.shape
     per_expert = block // 4
     slots = devices * per_expert
@@ -246,36 +258,43 @@
             pick, received
         ).astype(jnp.bfloat16)
 
-    grad = lax.dot_general(
-        slot_rows[slots:],
-        w_out[...],
-        (((1,), (1,)), ((), ())),
-        preferred_element_type=jnp.float32,
-    )
-    gate_up = jnp.dot(slot_rows[:slots], w_in[...], preferred_element_type=jnp.float32)
     saved_copy.wait()
-    gate_pre = saved[:, :hidden_units]
-    sigma = jax.nn.sigmoid(gate_pre)
-    slope = sigma * (1.0 + gate_pre * (1.0 - sigma))
-    joined[:, :hidden_units] = (grad * saved[:, hidden_units:] * slope).astype(jnp.bfloat16)
-    joined[:, hidden_units:] = (grad * (gate_pre * sigma)).astype(jnp.bfloat16)
-    gate = gate_up[:, :hidden_units]
-    hidden = (gate * jax.nn.sigmoid(gate) * gate_up[:, hidden_units:]).astype(jnp.bfloat16)
-    parts[slots:] = lax.dot_general(
-        joined[...], w_in[...], (((1,), (1,)), ((), ())), preferred_element_type=jnp.float32
-    ).astype(jnp.bfloat16)
-    parts[:slots] = jnp.dot(hidden, w_out[...], preferred_element_type=jnp.float32).astype(
-        jnp.bfloat16
-    )
-
-    row = lax.broadcasted_iota(jnp.int32, (rows, 2 * slots), 0)
-    slot = lax.broadcasted_iota(jnp.int32, (rows, 2 * slots), 1)
+    chunk = min(hidden_units, COLUMNS)
+    for start in range(0, hidden_units, chunk):
+        at, up_at = (pl.ds(start + side, chunk) for side in (0, hidden_units))
+        grad = lax.dot_general(
+            slot_rows[slots:],
+            w_out[at, :],
+            (((1,), (1,)), ((), ())),
+            preferred_element_type=jnp.float32,
+        )
+        gate = jnp.dot(slot_rows[:slots], w_in[:, at], preferred_element_type=jnp.float32)
+        up = jnp.dot(slot_rows[:slots], w_in[:, up_at], preferred_element_type=jnp.float32)
+        gate_pre = saved[:, at]
+        sigma = jax.nn.sigmoid(gate_pre)
+        slope = sigma * (1.0 + gate_pre * (1.0 - sigma))
+        joined[:, at] = (grad * saved[:, up_at] * slope).astype(jnp.bfloat16)
+        joined[:, up_at] = (grad * (gate_pre * sigma)).astype(jnp.bfloat16)
+        hidden[:, at] = (gate * jax.nn.sigmoid(gate) * up).astype(jnp.bfloat16)
+
+    row = lax.broadcasted_iota(jnp.int32, (rows, 4 * slots), 0)
+    line = lax.broadcasted_iota(jnp.int32, (rows, 4 * slots), 1)
+    slot = line % (2 * slots)
     home = (slot % slots) // per_expert * block + slot // slots * per_expert + slot % per_expert
-    total = jnp.zeros((rows, half_width), jnp.float32)
-    for half in range(2):
-        spread = jnp.where(row == home + half * 2 * per_expert, 1.0, 0.0)
-        total = total + exact_dot(spread, parts[:, half * half_width : (half + 1) * half_width])
-    out_ref[...] = total.astype(jnp.bfloat16).reshape(out_ref.shape)
+    spread = jnp.where(row == home + line // (2 * slots) * 2 * per_expert, 1.0, 0.0)
+    for start in range(0, half_width, COLUMNS):
+        parts = []
+        for half in range(2):
+            at = pl.ds(half * half_width + start, min(COLUMNS, half_width - start))
+            back = lax.dot_general(
+                joined[...], w_in[at, :], (((1,), (1,)), ((), ())), preferred_element_type=jnp.float32
+            )
+            ahead = jnp.dot(hidden[...], w_out[:, at], preferred_element_type=jnp.float32)
+            parts += [ahead.astype(jnp.bfloat16), back.astype(jnp.bfloat16)]
+        laid = exact_dot(spread, jnp.concatenate(parts, axis=0))
+        out_ref[:, :, start : start + laid.shape[1]] = laid.astype(jnp.bfloat16).reshape(
+            devices, block, laid.shape[1]
+        )
 
 
 def expert_step(tick, rows, saved_pre, w_in, w_out):
@@ -290,7 +309,7 @@
             pltpu.VMEM((slots, both), jnp.float32),
             pltpu.VMEM((2 * slots, width), jnp.bfloat16),
             pltpu.VMEM((slots, both), jnp.bfloat16),
-            pltpu.VMEM((2 * slots, width), jnp.bfloat16),
+            pltpu.VMEM((slots, both // 2), jnp.bfloat16),
             pltpu.SemaphoreType.DMA,
         ],
         compiler_params=pltpu.CompilerParams(vmem_limit_bytes=EXPERT_VMEM),

time: 81.3 us -> 84.2 us (1.036)
  Pallas kernels: 21.9 us -> 24.7 us
    pallas_call x2, Pallas kernels: 18.2 us -> 20.9 us  [expert_step(): pl.pallas_call(functools.partial(expert_kernel, tick), out_shape=pltpu.VM...]
where the time goes in v6:
time: 84.2 us; the launch traced here: 83.9 us
  blocking collectives  58.2 us (69%)
  Pallas kernels  24.7 us (29%)
  between operations  0.94 us (1%)
    all_to_all x5, blocking collectives, exchange(): return lax.all_to_all(array, axis, split_axis=0, concat_axis=0, tiled=True)  58.2 us
    pallas_call x2, Pallas kernels, expert_step(): pl.pallas_call(functools.partial(expert_kernel, tick), out_shape=pltpu.VM...  20.9 us

profile of v6, /device:TPU:0, one launch (start us, length us, event | category | flops | bytes accessed | tf_op | source)
XLA Modules:
  0.0 83.9 jit_solution(6015043296454197292)
XLA Ops:
  0.6 0.0 copy-start
  0.6 0.0 copy-start.1
  0.6 1.5 %shard_map.122 = bf16[8,8,1792]{2,1,0:T(8,128)(2,1)S(1)} custom-call(s32[2,1,2,4]{3,2,1,0:T(2,128)} %bitcast.10, f32[2,1,2,4]{3,2,1,0:T(2,128)} %bitcast.14, s32[2,1,2,4]{3,2,1,0:T(2,128)} %bitcast.18, f32[2,1,2,4]{3,2,1,0:T(2,128)} %bitcast.22, bf16[1,4,3584]{2,1,0:T(4,128)(2,1)} %refs_5_.4, bf16[1,4,3584]{2,1,0:T(4,128)(2,1)} %refs_6_.3), custom_call_target="tpu_custom_call" | custom-call | flops 22020096000 | tf_op jit(solution)/shard_map/pallas_call | solution.py:112
  2.2 0.0 copy-start.4
  2.2 0.0 copy-start.5
  2.2 0.0 copy-start.6
  2.2 0.0 copy-start.7
  2.2 0.0 copy-start.8
  2.2 0.0 copy-start.9
  2.2 0.0 copy-start.2
  2.2 0.0 copy-start.3
  2.2 15.4 %all_to_all.25.rows_ref = bf16[8,8,1792]{2,1,0:T(8,128)(2,1)S(1)} all-to-all(bf16[8,8,1792]{2,1,0:T(8,128)(2,1)S(1)} %shard_map.122), channel_id=1, replica_groups=mesh['section'=4,'expert'=8] {'expert'}, dimensions={0} | all-to-all | bytes 458752 | tf_op jit(solution)/shard_map/all_to_all | solution.py:325
  17.7 0.0 copy-done.1
  17.7 10.4 %shard_map.123 = bf16[8,8,1792]{2,1,0:T(8,128)(2,1)S(1)} custom-call(bf16[8,8,1792]{2,1,0:T(8,128)(2,1)S(1)} %all_to_all.25.rows_ref, f32[2,1,1,16,2048]{4,3,2,1,0:T(8,128)} %saved_ref.3, bf16[3584,2048]{1,0:T(8,128)(2,1)S(1)} %bitcast.6, bf16[1024,3584]{1,0:T(8,128)(2,1)S(1)} %bitcast.8), custom_call_target="tpu_custom_call" | custom-call | flops 704643072 | tf_op jit(solution)/shard_map/pallas_call | solution.py:303
  28.1 11.4 %all_to_all.26.refs_4_ = bf16[8,8,1792]{2,1,0:T(8,128)(2,1)S(1)} all-to-all(bf16[8,8,1792]{2,1,0:T(8,128)(2,1)S(1)} %shard_map.123), channel_id=1, replica_groups=mesh['section'=4,'expert'=8] {'expert'}, dimensions={0} | all-to-all | bytes 458752 | tf_op jit(solution)/shard_map/all_to_all | solution.py:325
  39.6 0.0 copy-done.7
  39.6 0.0 copy-done.8
  39.6 0.6 shard_map.124
  40.2 8.5 %all_to_all.27.refs_4_.refs_5_ = bf16[4,8,1792]{2,1,0:T(8,128)(2,1)S(1)} all-to-all(bf16[4,8,1792]{2,1,0:T(8,128)(2,1)S(1)} %get-tuple-element.5), channel_id=1, replica_groups=mesh['section'=4,'expert'=8] {'section'}, dimensions={0} | all-to-all | bytes 229376 | tf_op jit(solution)/shard_map/all_to_all | solution.py:325
  48.7 0.5 shard_map.125
  49.2 11.4 %all_to_all.28.rows_ref = bf16[8,8,1792]{2,1,0:T(8,128)(2,1)S(1)} all-to-all(bf16[8,8,1792]{2,1,0:T(8,128)(2,1)S(1)} %shard_map.125), channel_id=1, replica_groups=mesh['section'=4,'expert'=8] {'expert'}, dimensions={0} | all-to-all | bytes 458752 | tf_op jit(solution)/shard_map/all_to_all | solution.py:325
  60.6 10.4 %shard_map.126 = bf16[8,8,1792]{2,1,0:T(8,128)(2,1)S(1)} custom-call(bf16[8,8,1792]{2,1,0:T(8,128)(2,1)S(1)} %all_to_all.28.rows_ref, f32[2,1,1,16,2048]{4,3,2,1,0:T(8,128)} %saved_ref.3, bf16[3584,2048]{1,0:T(8,128)(2,1)S(1)} %bitcast.7, bf16[1024,3584]{1,0:T(8,128)(2,1)S(1)} %bitcast.9), custom_call_target="tpu_custom_call" | custom-call | flops 704643072 | tf_op jit(solution)/shard_map/pallas_call | solution.py:303
  71.1 11.4 %all_to_all.29.refs_4_ = bf16[8,8,1792]{2,1,0:T(8,128)(2,1)S(1)} all-to-all(bf16[8,8,1792]{2,1,0:T(8,128)(2,1)S(1)} %shard_map.126), channel_id=1, replica_groups=mesh['section'=4,'expert'=8] {'expert'}, dimensions={0} | all-to-all | bytes 458752 | tf_op jit(solution)/shard_map/all_to_all | solution.py:325
  82.5 1.2 %shard_map.127 = (bf16[2,1,4,3584]{3,2,1,0:T(4,128)(2,1)}, bf16[2,1,4,3584]{3,2,1,0:T(4,128)(2,1)}) custom-call(s32[2,1,2,4]{3,2,1,0:T(2,128)S(1)} %bitcast.13, f32[2,1,2,4]{3,2,1,0:T(2,128)S(1)} %bitcast.17, s32[2,1,2,4]{3,2,1,0:T(2,128)S(1)} %bitcast.21, f32[2,1,2,4]{3,2,1,0:T(2,128)S(1)} %bitcast.25, bf16[8,8,1792]{2,1,0:T(8,128)(2,1)S(1)} %all_to_all.29.refs_4_, ...), custom_call_target="tpu_custom_call" | custom-call | tf_op jit(solution)/shard_map/pallas_call | solution.py:228
  (7 shorter events, 0.0 us)
Async XLA Ops:
  0.6 17.0 %copy-start = (bf16[1,1,3584,2048]{3,2,1,0:T(8,128)(2,1)S(1)}, bf16[1,1,3584,2048]{3,2,1,0:T(8,128)(2,1)}, u32[]{:S(2)}) copy-start(bf16[1,1,3584,2048]{3,2,1,0:T(8,128)(2,1)} %param.15) | copy-start | bytes 44040196
  0.6 17.0 %copy-start.1 = (bf16[1,1,1024,3584]{3,2,1,0:T(8,128)(2,1)S(1)}, bf16[1,1,1024,3584]{3,2,1,0:T(8,128)(2,1)}, u32[]{:S(2)}) copy-start(bf16[1,1,1024,3584]{3,2,1,0:T(8,128)(2,1)} %param.16) | copy-start | bytes 22020100
  2.2 37.4 %copy-start.4 = (bf16[1,4,3584]{2,1,0:T(4,128)(2,1)S(1)}, bf16[1,4,3584]{2,1,0:T(4,128)(2,1)}, u32[]{:S(2)}) copy-start(bf16[1,4,3584]{2,1,0:T(4,128)(2,1)} %refs_5_.4) | copy-start | bytes 86020
  2.2 37.4 %copy-start.5 = (bf16[1,4,3584]{2,1,0:T(4,128)(2,1)S(1)}, bf16[1,4,3584]{2,1,0:T(4,128)(2,1)}, u32[]{:S(2)}) copy-start(bf16[1,4,3584]{2,1,0:T(4,128)(2,1)} %refs_6_.3) | copy-start | bytes 86020
  2.2 37.4 %copy-start.6 = (s32[2,1,4,2]{2,3,1,0:T(2,128)S(1)}, s32[2,1,4,2]{2,3,1,0:T(2,128)}, u32[]{:S(2)}) copy-start(s32[2,1,4,2]{2,3,1,0:T(2,128)} %param.17) | copy-start | bytes 196
  2.2 37.4 %copy-start.7 = (f32[2,1,4,2]{2,3,1,0:T(2,128)S(1)}, f32[2,1,4,2]{2,3,1,0:T(2,128)}, u32[]{:S(2)}) copy-start(f32[2,1,4,2]{2,3,1,0:T(2,128)} %param.18) | copy-start | bytes 196
  2.2 37.4 %copy-start.8 = (s32[2,1,4,2]{2,3,1,0:T(2,128)S(1)}, s32[2,1,4,2]{2,3,1,0:T(2,128)}, u32[]{:S(2)}) copy-start(s32[2,1,4,2]{2,3,1,0:T(2,128)} %param.19) | copy-start | bytes 196
  2.2 37.4 %copy-start.9 = (f32[2,1,4,2]{2,3,1,0:T(2,128)S(1)}, f32[2,1,4,2]{2,3,1,0:T(2,128)}, u32[]{:S(2)}) copy-start(f32[2,1,4,2]{2,3,1,0:T(2,128)} %param.20) | copy-start | bytes 196
  2.2 46.5 %copy-start.2 = (bf16[4,3584]{1,0:T(4,128)(2,1)S(1)}, bf16[4,3584]{1,0:T(4,128)(2,1)}, u32[]{:S(2)}) copy-start(bf16[4,3584]{1,0:T(4,128)(2,1)} %refs_6_.5) | copy-start | bytes 86020
  2.2 46.5 %copy-start.3 = (bf16[4,3584]{1,0:T(4,128)(2,1)S(1)}, bf16[4,3584]{1,0:T(4,128)(2,1)}, u32[]{:S(2)}) copy-start(bf16[4,3584]{1,0:T(4,128)(2,1)} %refs_7_.1) | copy-start | bytes 86020

commit v7 on v5

--- a/solution.py
+++ b/solution.py
@@ -81,14 +81,17 @@
 def pack_into(out_ref, tick, per_expert, slices, tables, pairs):
     devices, block, half_width = out_ref.shape
     rows = devices * block
-    total = jnp.zeros((rows, half_width), jnp.float32)
+    places, values = [], []
     for direction, halves in enumerate(pairs):
         place, _ = placing(
             tables[2 * direction], tables[2 * direction + 1], tick, direction, rows, per_expert, slices
         )
         side = half_of(rows, place.shape[1], per_expert)
-        for half in range(2):
-            total = total + exact_dot(jnp.where(side == half, place, 0.0), halves[half])
+        places += [jnp.where(side == half, place, 0.0) for half in range(2)]
+        values += [value.astype(jnp.float32) for value in halves]
+    total = exact_dot(
+        jnp.concatenate(places, axis=1), jnp.concatenate(values, axis=0).astype(jnp.bfloat16)
+    )
     out_ref[...] = total.astype(jnp.bfloat16).reshape(out_ref.shape)
 
 
@@ -139,8 +142,8 @@
     devices, block, half_width = back_ref.shape
     rows = devices * block
     back = back_ref[...].reshape(rows, half_width)
-    results = []
-    for direction, halves in enumerate(pairs):
+    terms = []
+    for direction in range(2):
         _, weight = placing(
             tables[2 * direction], tables[2 * direction + 1], tick, direction, rows, per_expert, slices
         )
@@ -148,16 +151,23 @@
         sides = jnp.concatenate(
             [jnp.where(side == half, weight, 0.0) for half in range(2)], axis=1
         )
-        high = sides.astype(jnp.bfloat16)
-        left = sides - high.astype(jnp.float32)
-        middle = left.astype(jnp.bfloat16)
-        low = (left - middle.astype(jnp.float32)).astype(jnp.bfloat16)
-        mixed = jnp.concatenate(halves, axis=0).astype(jnp.float32)
-        for term in (low, middle, high):
-            mixed = mixed + lax.dot_general(
-                term, back, (((0,), (0,)), ((), ())), preferred_element_type=jnp.float32
-            )
-        results.append(mixed.astype(jnp.bfloat16))
+        high = sides.astype(jnp.bfloat16).astype(jnp.float32)
+        middle = (sides - high).astype(jnp.bfloat16).astype(jnp.float32)
+        terms += [sides - high - middle, middle, high]
+    mixed = lax.dot_general(
+        jnp.concatenate(terms, axis=1).astype(jnp.bfloat16),
+        back,
+        (((0,), (0,)), ((), ())),
+        preferred_element_type=jnp.float32,
+    )
+    results = []
+    for direction, halves in enumerate(pairs):
+        total = jnp.concatenate([half.astype(jnp.float32) for half in halves], axis=0)
+        count = total.shape[0]
+        for term in range(3):
+            start = (3 * direction + term) * count
+            total = total + mixed[start : start + count]
+        results.append(total.astype(jnp.bfloat16))
     return results
 
 
@@ -224,6 +234,15 @@
     )(*routing, back, arrived, *others)
 
 
+def home_of(line, slots, per_expert):
+    half, direction, slot = line // (2 * slots), line // slots % 2, line % slots
+    return (
+        slot // per_expert * (4 * per_expert)
+        + (2 * half + direction) * per_expert
+        + slot % per_expert
+    )
+
+
 def expert_kernel(tick, rows_ref, saved_ref, w_in, w_out, out_ref, *rest):
     saved, slot_rows, joined, parts, saved_sem = rest[-5:]
     devices, block, half_width = rows_ref.shape
@@ -237,14 +256,14 @@
     saved_copy.start()
 
     received = rows_ref[...].reshape(rows, half_width)
-    slot = lax.broadcasted_iota(jnp.int32, (2 * slots, rows), 0)
-    row = lax.broadcasted_iota(jnp.int32, (2 * slots, rows), 1)
-    home = (slot % slots) // per_expert * block + slot // slots * per_expert + slot % per_expert
+    line = lax.broadcasted_iota(jnp.int32, (4 * slots, rows), 0)
+    row = lax.broadcasted_iota(jnp.int32, (4 * slots, rows), 1)
+    pick = jnp.where(row == home_of(line, slots, per_expert), 1.0, 0.0)
+    picked = exact_dot(pick, received).astype(jnp.bfloat16)
     for half in range(2):
-        pick = jnp.where(row == home + half * 2 * per_expert, 1.0, 0.0)
-        slot_rows[:, half * half_width : (half + 1) * half_width] = exact_dot(
-            pick, received
-        ).astype(jnp.bfloat16)
+        slot_rows[:, half * half_width : (half + 1) * half_width] = picked[
+            half * 2 * slots : (half + 1) * 2 * slots
+        ]
 
     grad = lax.dot_general(
         slot_rows[slots:],
@@ -261,21 +280,20 @@
     joined[:, hidden_units:] = (grad * (gate_pre * sigma)).astype(jnp.bfloat16)
     gate = gate_up[:, :hidden_units]
     hidden = (gate * jax.nn.sigmoid(gate) * gate_up[:, hidden_units:]).astype(jnp.bfloat16)
-    parts[slots:] = lax.dot_general(
+    back = lax.dot_general(
         joined[...], w_in[...], (((1,), (1,)), ((), ())), preferred_element_type=jnp.float32
     ).astype(jnp.bfloat16)
-    parts[:slots] = jnp.dot(hidden, w_out[...], preferred_element_type=jnp.float32).astype(
-        jnp.bfloat16
-    )
-
-    row = lax.broadcasted_iota(jnp.int32, (rows, 2 * slots), 0)
-    slot = lax.broadcasted_iota(jnp.int32, (rows, 2 * slots), 1)
-    home = (slot % slots) // per_expert * block + slot // slots * per_expert + slot % per_expert
-    total = jnp.zeros((rows, half_width), jnp.float32)
+    ahead = jnp.dot(hidden, w_out[...], preferred_element_type=jnp.float32).astype(jnp.bfloat16)
     for half in range(2):
-        spread = jnp.where(row == home + half * 2 * per_expert, 1.0, 0.0)
-        total = total + exact_dot(spread, parts[:, half * half_width : (half + 1) * half_width])
-    out_ref[...] = total.astype(jnp.bfloat16).reshape(out_ref.shape)
+        columns = slice(half * half_width, (half + 1) * half_width)
+        start = half * 2 * slots
+        parts[start : start + slots] = ahead[:, columns]
+        parts[start + slots : start + 2 * slots] = back[:, columns]
+
+    row = lax.broadcasted_iota(jnp.int32, (rows, 4 * slots), 0)
+    line = lax.broadcasted_iota(jnp.int32, (rows, 4 * slots), 1)
+    spread = jnp.where(row == home_of(line, slots, per_expert), 1.0, 0.0)
+    out_ref[...] = exact_dot(spread, parts[...]).astype(jnp.bfloat16).reshape(out_ref.shape)
 
 
 def expert_step(tick, rows, saved_pre, w_in, w_out):
@@ -290,7 +308,7 @@
             pltpu.VMEM((slots, both), jnp.float32),
             pltpu.VMEM((2 * slots, width), jnp.bfloat16),
             pltpu.VMEM((slots, both), jnp.bfloat16),
-            pltpu.VMEM((2 * slots, width), jnp.bfloat16),
+            pltpu.VMEM((4 * slots, width // 2), jnp.bfloat16),
             pltpu.SemaphoreType.DMA,
         ],
         compiler_params=pltpu.CompilerParams(vmem_limit_bytes=EXPERT_VMEM),

time: 81.3 us -> 80.9 us (level)
  no operation moved by 1% of the time
where the time goes in v7:
time: 80.9 us; the launch traced here: 80.5 us
  blocking collectives  58.2 us (72%)
  Pallas kernels  21.4 us (26%)
    all_to_all x5, blocking collectives, exchange(): return lax.all_to_all(array, axis, split_axis=0, concat_axis=0, tiled=True)  58.2 us
    pallas_call x2, Pallas kernels, expert_step(): pl.pallas_call(functools.partial(expert_kernel, tick), out_shape=pltpu.VM...  18 us

profile of v7, /device:TPU:0, one launch (start us, length us, event | category | flops | bytes accessed | tf_op | source)
XLA Modules:
  0.0 80.5 jit_solution(6930794766887963840)
XLA Ops:
  0.6 0.0 copy-start
  0.6 0.0 copy-start.1
  0.6 1.4 %shard_map.122 = bf16[8,8,1792]{2,1,0:T(8,128)(2,1)S(1)} custom-call(s32[2,1,2,4]{3,2,1,0:T(2,128)} %bitcast.10, f32[2,1,2,4]{3,2,1,0:T(2,128)} %bitcast.14, s32[2,1,2,4]{3,2,1,0:T(2,128)} %bitcast.18, f32[2,1,2,4]{3,2,1,0:T(2,128)} %bitcast.22, bf16[1,4,3584]{2,1,0:T(4,128)(2,1)} %refs_5_.4, bf16[1,4,3584]{2,1,0:T(4,128)(2,1)} %refs_6_.3), custom_call_target="tpu_custom_call" | custom-call | flops 22020096000 | tf_op jit(solution)/shard_map/pallas_call | solution.py:114
  2.1 0.0 copy-start.4
  2.1 0.0 copy-start.5
  2.1 0.0 copy-start.6
  2.1 0.0 copy-start.7
  2.1 0.0 copy-start.8
  2.1 0.0 copy-start.9
  2.1 0.0 copy-start.2
  2.2 0.0 copy-start.3
  2.2 15.4 %all_to_all.25.rows_ref = bf16[8,8,1792]{2,1,0:T(8,128)(2,1)S(1)} all-to-all(bf16[8,8,1792]{2,1,0:T(8,128)(2,1)S(1)} %shard_map.122), channel_id=1, replica_groups=mesh['section'=4,'expert'=8] {'expert'}, dimensions={0} | all-to-all | bytes 458752 | tf_op jit(solution)/shard_map/all_to_all | solution.py:324
  17.6 0.0 copy-done
  17.6 0.0 copy-done.1
  17.6 9.0 %shard_map.123 = bf16[8,8,1792]{2,1,0:T(8,128)(2,1)S(1)} custom-call(bf16[8,8,1792]{2,1,0:T(8,128)(2,1)S(1)} %all_to_all.25.rows_ref, f32[2,1,1,16,2048]{4,3,2,1,0:T(8,128)} %saved_ref.3, bf16[3584,2048]{1,0:T(8,128)(2,1)S(1)} %bitcast.6, bf16[1024,3584]{1,0:T(8,128)(2,1)S(1)} %bitcast.8), custom_call_target="tpu_custom_call" | custom-call | flops 704643072 | tf_op jit(solution)/shard_map/pallas_call | solution.py:302
  26.6 11.4 %all_to_all.26.refs_4_ = bf16[8,8,1792]{2,1,0:T(8,128)(2,1)S(1)} all-to-all(bf16[8,8,1792]{2,1,0:T(8,128)(2,1)S(1)} %shard_map.123), channel_id=1, replica_groups=mesh['section'=4,'expert'=8] {'expert'}, dimensions={0} | all-to-all | bytes 458752 | tf_op jit(solution)/shard_map/all_to_all | solution.py:324
  38.1 0.5 shard_map.124
  38.6 8.5 %all_to_all.27.refs_4_.refs_5_ = bf16[4,8,1792]{2,1,0:T(8,128)(2,1)S(1)} all-to-all(bf16[4,8,1792]{2,1,0:T(8,128)(2,1)S(1)} %get-tuple-element.5), channel_id=1, replica_groups=mesh['section'=4,'expert'=8] {'section'}, dimensions={0} | all-to-all | bytes 229376 | tf_op jit(solution)/shard_map/all_to_all | solution.py:324
  47.1 0.0 copy-done.3
  47.1 0.4 shard_map.125
  47.5 11.4 %all_to_all.28.rows_ref = bf16[8,8,1792]{2,1,0:T(8,128)(2,1)S(1)} all-to-all(bf16[8,8,1792]{2,1,0:T(8,128)(2,1)S(1)} %shard_map.125), channel_id=1, replica_groups=mesh['section'=4,'expert'=8] {'expert'}, dimensions={0} | all-to-all | bytes 458752 | tf_op jit(solution)/shard_map/all_to_all | solution.py:324
  58.9 9.0 %shard_map.126 = bf16[8,8,1792]{2,1,0:T(8,128)(2,1)S(1)} custom-call(bf16[8,8,1792]{2,1,0:T(8,128)(2,1)S(1)} %all_to_all.28.rows_ref, f32[2,1,1,16,2048]{4,3,2,1,0:T(8,128)} %saved_ref.3, bf16[3584,2048]{1,0:T(8,128)(2,1)S(1)} %bitcast.7, bf16[1024,3584]{1,0:T(8,128)(2,1)S(1)} %bitcast.9), custom_call_target="tpu_custom_call" | custom-call | flops 704643072 | tf_op jit(solution)/shard_map/pallas_call | solution.py:302
  67.9 11.4 %all_to_all.29.refs_4_ = bf16[8,8,1792]{2,1,0:T(8,128)(2,1)S(1)} all-to-all(bf16[8,8,1792]{2,1,0:T(8,128)(2,1)S(1)} %shard_map.126), channel_id=1, replica_groups=mesh['section'=4,'expert'=8] {'expert'}, dimensions={0} | all-to-all | bytes 458752 | tf_op jit(solution)/shard_map/all_to_all | solution.py:324
  79.4 1.2 %shard_map.127 = (bf16[2,1,4,3584]{3,2,1,0:T(4,128)(2,1)}, bf16[2,1,4,3584]{3,2,1,0:T(4,128)(2,1)}) custom-call(s32[2,1,2,4]{3,2,1,0:T(2,128)S(1)} %bitcast.13, f32[2,1,2,4]{3,2,1,0:T(2,128)S(1)} %bitcast.17, s32[2,1,2,4]{3,2,1,0:T(2,128)S(1)} %bitcast.21, f32[2,1,2,4]{3,2,1,0:T(2,128)S(1)} %bitcast.25, bf16[8,8,1792]{2,1,0:T(8,128)(2,1)S(1)} %all_to_all.29.refs_4_, ...), custom_call_target="tpu_custom_call" | custom-call | tf_op jit(solution)/shard_map/pallas_call | solution.py:228
  (7 shorter events, 0.0 us)
Async XLA Ops:
  0.6 17.0 %copy-start = (bf16[1,1,3584,2048]{3,2,1,0:T(8,128)(2,1)S(1)}, bf16[1,1,3584,2048]{3,2,1,0:T(8,128)(2,1)}, u32[]{:S(2)}) copy-start(bf16[1,1,3584,2048]{3,2,1,0:T(8,128)(2,1)} %param.15) | copy-start | bytes 44040196
  0.6 17.0 %copy-start.1 = (bf16[1,1,1024,3584]{3,2,1,0:T(8,128)(2,1)S(1)}, bf16[1,1,1024,3584]{3,2,1,0:T(8,128)(2,1)}, u32[]{:S(2)}) copy-start(bf16[1,1,1024,3584]{3,2,1,0:T(8,128)(2,1)} %param.16) | copy-start | bytes 22020100
  2.1 36.0 %copy-start.4 = (bf16[1,4,3584]{2,1,0:T(4,128)(2,1)S(1)}, bf16[1,4,3584]{2,1,0:T(4,128)(2,1)}, u32[]{:S(2)}) copy-start(bf16[1,4,3584]{2,1,0:T(4,128)(2,1)} %refs_5_.4) | copy-start | bytes 86020
  2.1 36.0 %copy-start.5 = (bf16[1,4,3584]{2,1,0:T(4,128)(2,1)S(1)}, bf16[1,4,3584]{2,1,0:T(4,128)(2,1)}, u32[]{:S(2)}) copy-start(bf16[1,4,3584]{2,1,0:T(4,128)(2,1)} %refs_6_.3) | copy-start | bytes 86020
  2.1 36.0 %copy-start.6 = (s32[2,1,4,2]{2,3,1,0:T(2,128)S(1)}, s32[2,1,4,2]{2,3,1,0:T(2,128)}, u32[]{:S(2)}) copy-start(s32[2,1,4,2]{2,3,1,0:T(2,128)} %param.17) | copy-start | bytes 196
  2.1 36.0 %copy-start.7 = (f32[2,1,4,2]{2,3,1,0:T(2,128)S(1)}, f32[2,1,4,2]{2,3,1,0:T(2,128)}, u32[]{:S(2)}) copy-start(f32[2,1,4,2]{2,3,1,0:T(2,128)} %param.18) | copy-start | bytes 196
  2.1 36.0 %copy-start.8 = (s32[2,1,4,2]{2,3,1,0:T(2,128)S(1)}, s32[2,1,4,2]{2,3,1,0:T(2,128)}, u32[]{:S(2)}) copy-start(s32[2,1,4,2]{2,3,1,0:T(2,128)} %param.19) | copy-start | bytes 196
  2.1 36.0 %copy-start.9 = (f32[2,1,4,2]{2,3,1,0:T(2,128)S(1)}, f32[2,1,4,2]{2,3,1,0:T(2,128)}, u32[]{:S(2)}) copy-start(f32[2,1,4,2]{2,3,1,0:T(2,128)} %param.20) | copy-start | bytes 196
  2.1 45.0 %copy-start.2 = (bf16[4,3584]{1,0:T(4,128)(2,1)S(1)}, bf16[4,3584]{1,0:T(4,128)(2,1)}, u32[]{:S(2)}) copy-start(bf16[4,3584]{1,0:T(4,128)(2,1)} %refs_6_.5) | copy-start | bytes 86020
  2.2 45.0 %copy-start.3 = (bf16[4,3584]{1,0:T(4,128)(2,1)S(1)}, bf16[4,3584]{1,0:T(4,128)(2,1)}, u32[]{:S(2)}) copy-start(bf16[4,3584]{1,0:T(4,128)(2,1)} %refs_7_.1) | copy-start | bytes 86020

commit v8 on v7

--- a/solution.py
+++ b/solution.py
@@ -243,13 +243,11 @@
     )
 
 
-def expert_kernel(tick, rows_ref, saved_ref, w_in, w_out, out_ref, *rest):
-    saved, slot_rows, joined, parts, saved_sem = rest[-5:]
+def backward_kernel(tick, rows_ref, saved_ref, w_in, w_out, fwd_rows, back_ref, saved, bwd_rows, joined, saved_sem):
     devices, block, half_width = rows_ref.shape
     per_expert = block // 4
     slots = devices * per_expert
-    width, both = w_in.shape
-    hidden_units = both // 2
+    hidden_units = w_out.shape[0]
     rows = devices * block
 
     saved_copy = pltpu.make_async_copy(saved_ref.at[tick, 0, 0], saved, saved_sem)
@@ -261,63 +259,75 @@
     pick = jnp.where(row == home_of(line, slots, per_expert), 1.0, 0.0)
     picked = exact_dot(pick, received).astype(jnp.bfloat16)
     for half in range(2):
-        slot_rows[:, half * half_width : (half + 1) * half_width] = picked[
-            half * 2 * slots : (half + 1) * 2 * slots
-        ]
+        columns = slice(half * half_width, (half + 1) * half_width)
+        start = half * 2 * slots
+        fwd_rows[:, columns] = picked[start : start + slots]
+        bwd_rows[:, columns] = picked[start + slots : start + 2 * slots]
 
     grad = lax.dot_general(
-        slot_rows[slots:],
-        w_out[...],
-        (((1,), (1,)), ((), ())),
-        preferred_element_type=jnp.float32,
-    )
-    gate_up = jnp.dot(slot_rows[:slots], w_in[...], preferred_element_type=jnp.float32)
+        bwd_rows[...], w_out[...], (((1,), (1,)), ((), ())), preferred_element_type=jnp.float32
+    )
     saved_copy.wait()
     gate_pre = saved[:, :hidden_units]
     sigma = jax.nn.sigmoid(gate_pre)
     slope = sigma * (1.0 + gate_pre * (1.0 - sigma))
     joined[:, :hidden_units] = (grad * saved[:, hidden_units:] * slope).astype(jnp.bfloat16)
     joined[:, hidden_units:] = (grad * (gate_pre * sigma)).astype(jnp.bfloat16)
-    gate = gate_up[:, :hidden_units]
-    hidden = (gate * jax.nn.sigmoid(gate) * gate_up[:, hidden_units:]).astype(jnp.bfloat16)
-    back = lax.dot_general(
+    back_ref[...] = lax.dot_general(
         joined[...], w_in[...], (((1,), (1,)), ((), ())), preferred_element_type=jnp.float32
     ).astype(jnp.bfloat16)
-    ahead = jnp.dot(hidden, w_out[...], preferred_element_type=jnp.float32).astype(jnp.bfloat16)
+
+
+def lay_kernel(ahead_ref, back_ref, out_ref, parts):
+    devices, block, half_width = out_ref.shape
+    per_expert = block // 4
+    slots = devices * per_expert
+    rows = devices * block
     for half in range(2):
         columns = slice(half * half_width, (half + 1) * half_width)
         start = half * 2 * slots
-        parts[start : start + slots] = ahead[:, columns]
-        parts[start + slots : start + 2 * slots] = back[:, columns]
-
+        parts[start : start + slots] = ahead_ref[:, columns]
+        parts[start + slots : start + 2 * slots] = back_ref[:, columns]
     row = lax.broadcasted_iota(jnp.int32, (rows, 4 * slots), 0)
     line = lax.broadcasted_iota(jnp.int32, (rows, 4 * slots), 1)
     spread = jnp.where(row == home_of(line, slots, per_expert), 1.0, 0.0)
     out_ref[...] = exact_dot(spread, parts[...]).astype(jnp.bfloat16).reshape(out_ref.shape)
 
 
-def expert_step(tick, rows, saved_pre, w_in, w_out):
+def expert_step(tick, rows, saved_pre, plain, pinned):
+    w_in, w_out = plain
     width, both = w_in.shape
+    hidden_units = both // 2
     slots = saved_pre.shape[3]
-    return pl.pallas_call(
-        functools.partial(expert_kernel, tick),
-        out_shape=pltpu.VMEM(rows.shape, jnp.bfloat16),
+    fwd_rows, back = pl.pallas_call(
+        functools.partial(backward_kernel, tick),
+        out_shape=[pltpu.VMEM((slots, width), jnp.bfloat16)] * 2,
         in_specs=[VMEM, HBM, VMEM, VMEM],
-        out_specs=VMEM,
+        out_specs=[VMEM] * 2,
         scratch_shapes=[
             pltpu.VMEM((slots, both), jnp.float32),
-            pltpu.VMEM((2 * slots, width), jnp.bfloat16),
+            pltpu.VMEM((slots, width), jnp.bfloat16),
             pltpu.VMEM((slots, both), jnp.bfloat16),
-            pltpu.VMEM((4 * slots, width // 2), jnp.bfloat16),
             pltpu.SemaphoreType.DMA,
         ],
         compiler_params=pltpu.CompilerParams(vmem_limit_bytes=EXPERT_VMEM),
         cost_estimate=pl.CostEstimate(
-            flops=12 * slots * width * (both // 2),
-            bytes_accessed=0,
-            transcendentals=0,
+            flops=6 * slots * width * hidden_units, bytes_accessed=0, transcendentals=0
         ),
-    )(rows, pltpu.with_memory_space_constraint(saved_pre, pltpu.HBM), w_in, w_out)
+    )(rows, pltpu.with_memory_space_constraint(saved_pre, pltpu.HBM), *pinned)
+    gate_up = jnp.dot(fwd_rows, w_in, preferred_element_type=jnp.float32)
+    hidden = (jax.nn.silu(gate_up[:, :hidden_units]) * gate_up[:, hidden_units:]).astype(
+        jnp.bfloat16
+    )
+    ahead = jnp.dot(hidden, w_out, preferred_element_type=jnp.float32).astype(jnp.bfloat16)
+    return pl.pallas_call(
+        lay_kernel,
+        out_shape=pltpu.VMEM(rows.shape, jnp.bfloat16),
+        in_specs=[VMEM] * 2,
+        out_specs=VMEM,
+        scratch_shapes=[pltpu.VMEM((4 * slots, width // 2), jnp.bfloat16)],
+        compiler_params=pltpu.CompilerParams(vmem_limit_bytes=SMALL_VMEM),
+    )(ahead, back)
 
 
 def exchange(array, axis):
@@ -344,17 +354,16 @@
         jnp.swapaxes(table, 2, 3) for table in (fwd_route, fwd_gate, bwd_route, bwd_gate)
     ]
     beside = BESIDE * (w_in.size + w_out.size)
-    w_in, w_out = (
-        pltpu.with_memory_space_constraint(w.reshape(w.shape[2:]), pltpu.VMEM) for w in (w_in, w_out)
-    )
+    plain = [w.reshape(w.shape[2:]) for w in (w_in, w_out)]
+    pinned = [pltpu.with_memory_space_constraint(w, pltpu.VMEM) for w in plain]
     sent = first_pack(0, devices, per_expert, slices, routing, fwd_act, bwd_grad, beside)
-    parts = expert_step(0, exchange(sent, "expert"), saved_pre, w_in, w_out)
+    parts = expert_step(0, exchange(sent, "expert"), saved_pre, plain, pinned)
     moved, fwd_next, bwd_next = relay(
         0, per_expert, slices, routing, exchange(parts, "expert"), fwd_act, bwd_grad
     )
     arrived = exchange(moved, "section")
     sent = later_pack(1, devices, per_expert, slices, routing, arrived, fwd_enter, bwd_enter)
-    parts = expert_step(1, exchange(sent, "expert"), saved_pre, w_in, w_out)
+    parts = expert_step(1, exchange(sent, "expert"), saved_pre, plain, pinned)
     return finish(
         1, per_expert, slices, routing, exchange(parts, "expert"), arrived,
         fwd_enter, bwd_enter, fwd_next, bwd_next,

time: 80.9 us -> 81.4 us (level)
  matrix products: 0 us -> 6.13 us
  Pallas kernels: 21.4 us -> 15.9 us
    dot_general x0 -> x4, matrix products: none -> 6.13 us  [the longest x2 4.01 us: expert_step(): gate_up = jnp.dot(fwd_rows, w_in, preferred_element_type=jnp.float32)]
    pallas_call x2 -> x4, Pallas kernels: 18 us -> 12.5 us  [the longest x2 12 us: expert_step(): pl.pallas_call(functools.partial(backward_kernel, tick), out_shape=[pltpu...]
where the time goes in v8:
time: 81.4 us; the launch traced here: 81.1 us
  blocking collectives  58.2 us (71%)
  Pallas kernels  15.9 us (20%)
  matrix products  6.13 us (8%)
    all_to_all x5, blocking collectives, exchange(): return lax.all_to_all(array, axis, split_axis=0, concat_axis=0, tiled=True)  58.2 us
    pallas_call x2, Pallas kernels, expert_step(): pl.pallas_call(functools.partial(backward_kernel, tick), out_shape=[pltpu...  12 us
    dot_general x2, matrix products, expert_step(): gate_up = jnp.dot(fwd_rows, w_in, preferred_element_type=jnp.float32)  4.01 us
    dot_general x2, matrix products, expert_step(): jnp.dot(hidden, w_out, preferred_element_type=jnp.float32)  2.12 us

profile of v8, /device:TPU:0, one launch (start us, length us, event | category | flops | bytes accessed | tf_op | source)
XLA Modules:
  0.0 81.1 jit_solution(8078140593830270098)
XLA Ops:
  0.6 1.4 %shard_map.122 = bf16[8,8,1792]{2,1,0:T(8,128)(2,1)S(1)} custom-call(s32[2,1,2,4]{3,2,1,0:T(2,128)} %bitcast.20, f32[2,1,2,4]{3,2,1,0:T(2,128)} %bitcast.24, s32[2,1,2,4]{3,2,1,0:T(2,128)} %bitcast.28, f32[2,1,2,4]{3,2,1,0:T(2,128)} %bitcast.32, bf16[1,4,3584]{2,1,0:T(4,128)(2,1)} %refs_5_.4, bf16[1,4,3584]{2,1,0:T(4,128)(2,1)} %refs_6_.3), custom_call_target="tpu_custom_call" | custom-call | flops 22020096000 | tf_op jit(solution)/shard_map/pallas_call | solution.py:114
  2.1 15.4 %all_to_all.25.rows_ref = bf16[8,8,1792]{2,1,0:T(8,128)(2,1)S(1)} all-to-all(bf16[8,8,1792]{2,1,0:T(8,128)(2,1)S(1)} %shard_map.122), channel_id=1, replica_groups=mesh['section'=4,'expert'=8] {'expert'}, dimensions={0} | all-to-all | bytes 458752 | tf_op jit(solution)/shard_map/all_to_all | solution.py:334
  17.5 6.0 %shard_map.123 = (bf16[16,3584]{1,0:T(8,128)(2,1)S(1)}, bf16[16,3584]{1,0:T(8,128)(2,1)S(1)}) custom-call(bf16[8,8,1792]{2,1,0:T(8,128)(2,1)S(1)} %all_to_all.25.rows_ref, f32[2,1,1,16,2048]{4,3,2,1,0:T(8,128)} %saved_ref.3, bf16[3584,2048]{1,0:T(8,128)(2,1)S(1)} %bitcast.16, bf16[1024,3584]{1,0:T(8,128)(2,1)S(1)} %bitcast.18), custom_call_target="tpu_custom_call" | custom-call | flops 352321536 | tf_op jit(solution)/shard_map/pallas_call | solution.py:302
  23.5 0.0 copy-start.4
  23.5 0.0 copy-start.5
  23.5 0.0 copy-start.6
  23.6 0.0 copy-start.7
  23.6 0.0 copy-start.8
  23.6 0.0 copy-start.9
  23.6 0.0 copy-start.2
  23.6 2.0 %fusion.10 = f32[16,2048]{1,0:T(8,128)S(1)} fusion(bf16[16,3584]{1,0:T(8,128)(2,1)S(1)} %get-tuple-element.9, bf16[1,1,3584,2048]{3,2,1,0:T(8,128)(2,1)S(1)} %copy-done), kind=kOutput, calls=%fused_computation.12 | convolution fusion | flops 234881024 | bytes 14925824 | tf_op jit(solution)/shard_map/dot_general | solution.py:318
  25.6 1.1 %convolution_convert_fusion.1.ahead_ref = bf16[16,3584]{1,0:T(8,128)(2,1)S(1)} fusion(f32[16,2048]{1,0:T(8,128)S(1)} %fusion.10, bf16[1,1,1024,3584]{3,2,1,0:T(8,128)(2,1)S(1)} %copy-done.1), kind=kOutput, calls=%fused_computation.1 | convolution fusion | flops 117596160 | bytes 7585792 | tf_op jit(solution)/shard_map/dot_general | solution.py:322
  26.7 0.2 shard_map.124
  26.9 11.4 %all_to_all.26.refs_4_ = bf16[8,8,1792]{2,1,0:T(8,128)(2,1)S(1)} all-to-all(bf16[8,8,1792]{2,1,0:T(8,128)(2,1)S(1)} %shard_map.124), channel_id=1, replica_groups=mesh['section'=4,'expert'=8] {'expert'}, dimensions={0} | all-to-all | bytes 458752 | tf_op jit(solution)/shard_map/all_to_all | solution.py:334
  38.4 0.5 shard_map.125
  38.9 8.5 %all_to_all.27.refs_4_.refs_5_ = bf16[4,8,1792]{2,1,0:T(8,128)(2,1)S(1)} all-to-all(bf16[4,8,1792]{2,1,0:T(8,128)(2,1)S(1)} %get-tuple-element.11), channel_id=1, replica_groups=mesh['section'=4,'expert'=8] {'section'}, dimensions={0} | all-to-all | bytes 229376 | tf_op jit(solution)/shard_map/all_to_all | solution.py:334
  47.4 0.4 shard_map.126
  47.8 11.4 %all_to_all.28.rows_ref = bf16[8,8,1792]{2,1,0:T(8,128)(2,1)S(1)} all-to-all(bf16[8,8,1792]{2,1,0:T(8,128)(2,1)S(1)} %shard_map.126), channel_id=1, replica_groups=mesh['section'=4,'expert'=8] {'expert'}, dimensions={0} | all-to-all | bytes 458752 | tf_op jit(solution)/shard_map/all_to_all | solution.py:334
  59.2 6.0 %shard_map.127 = (bf16[16,3584]{1,0:T(8,128)(2,1)S(1)}, bf16[16,3584]{1,0:T(8,128)(2,1)S(1)}) custom-call(bf16[8,8,1792]{2,1,0:T(8,128)(2,1)S(1)} %all_to_all.28.rows_ref, f32[2,1,1,16,2048]{4,3,2,1,0:T(8,128)} %saved_ref.3, bf16[3584,2048]{1,0:T(8,128)(2,1)S(1)} %bitcast.17, bf16[1024,3584]{1,0:T(8,128)(2,1)S(1)} %bitcast.19), custom_call_target="tpu_custom_call" | custom-call | flops 352321536 | tf_op jit(solution)/shard_map/pallas_call | solution.py:302
  65.2 2.0 %fusion.8 = f32[16,2048]{1,0:T(8,128)S(1)} fusion(bf16[16,3584]{1,0:T(8,128)(2,1)S(1)} %get-tuple-element.12, bf16[1,1,3584,2048]{3,2,1,0:T(8,128)(2,1)S(1)} %copy-done), kind=kOutput, calls=%fused_computation.10 | convolution fusion | flops 234881024 | bytes 14925824 | tf_op jit(solution)/shard_map/dot_general | solution.py:318
  67.2 1.1 %convolution_convert_fusion.ahead_ref = bf16[16,3584]{1,0:T(8,128)(2,1)S(1)} fusion(f32[16,2048]{1,0:T(8,128)S(1)} %fusion.8, bf16[1,1,1024,3584]{3,2,1,0:T(8,128)(2,1)S(1)} %copy-done.1), kind=kOutput, calls=%fused_computation | convolution fusion | flops 117596160 | bytes 7585792 | tf_op jit(solution)/shard_map/dot_general | solution.py:322
  68.3 0.2 shard_map.128
  68.5 11.4 %all_to_all.29.refs_4_ = bf16[8,8,1792]{2,1,0:T(8,128)(2,1)S(1)} all-to-all(bf16[8,8,1792]{2,1,0:T(8,128)(2,1)S(1)} %shard_map.128), channel_id=1, replica_groups=mesh['section'=4,'expert'=8] {'expert'}, dimensions={0} | all-to-all | bytes 458752 | tf_op jit(solution)/shard_map/all_to_all | solution.py:334
  80.0 1.2 %shard_map.129 = (bf16[2,1,4,3584]{3,2,1,0:T(4,128)(2,1)}, bf16[2,1,4,3584]{3,2,1,0:T(4,128)(2,1)}) custom-call(s32[2,1,2,4]{3,2,1,0:T(2,128)S(1)} %bitcast.23, f32[2,1,2,4]{3,2,1,0:T(2,128)S(1)} %bitcast.27, s32[2,1,2,4]{3,2,1,0:T(2,128)S(1)} %bitcast.31, f32[2,1,2,4]{3,2,1,0:T(2,128)S(1)} %bitcast.35, bf16[8,8,1792]{2,1,0:T(8,128)(2,1)S(1)} %all_to_all.29.refs_4_, ...), custom_call_target="tpu_custom_call" | custom-call | tf_op jit(solution)/shard_map/pallas_call | solution.py:228
  (13 shorter events, 0.0 us)
Async XLA Ops:
  0.6 16.9 %copy-start = (bf16[1,1,3584,2048]{3,2,1,0:T(8,128)(2,1)S(1)}, bf16[1,1,3584,2048]{3,2,1,0:T(8,128)(2,1)}, u32[]{:S(2)}) copy-start(bf16[1,1,3584,2048]{3,2,1,0:T(8,128)(2,1)} %param.15) | copy-start | bytes 44040196
  0.6 16.9 %copy-start.1 = (bf16[1,1,1024,3584]{3,2,1,0:T(8,128)(2,1)S(1)}, bf16[1,1,1024,3584]{3,2,1,0:T(8,128)(2,1)}, u32[]{:S(2)}) copy-start(bf16[1,1,1024,3584]{3,2,1,0:T(8,128)(2,1)} %param.16) | copy-start | bytes 22020100
  23.5 14.8 %copy-start.4 = (bf16[1,4,3584]{2,1,0:T(4,128)(2,1)S(1)}, bf16[1,4,3584]{2,1,0:T(4,128)(2,1)}, u32[]{:S(2)}) copy-start(bf16[1,4,3584]{2,1,0:T(4,128)(2,1)} %refs_5_.4) | copy-start | bytes 86020
  23.5 14.8 %copy-start.5 = (bf16[1,4,3584]{2,1,0:T(4,128)(2,1)S(1)}, bf16[1,4,3584]{2,1,0:T(4,128)(2,1)}, u32[]{:S(2)}) copy-start(bf16[1,4,3584]{2,1,0:T(4,128)(2,1)} %refs_6_.3) | copy-start | bytes 86020
  23.5 14.8 %copy-start.6 = (s32[2,1,4,2]{2,3,1,0:T(2,128)S(1)}, s32[2,1,4,2]{2,3,1,0:T(2,128)}, u32[]{:S(2)}) copy-start(s32[2,1,4,2]{2,3,1,0:T(2,128)} %param.17) | copy-start | bytes 196
  23.6 14.8 %copy-start.7 = (f32[2,1,4,2]{2,3,1,0:T(2,128)S(1)}, f32[2,1,4,2]{2,3,1,0:T(2,128)}, u32[]{:S(2)}) copy-start(f32[2,1,4,2]{2,3,1,0:T(2,128)} %param.18) | copy-start | bytes 196
  23.6 14.8 %copy-start.8 = (s32[2,1,4,2]{2,3,1,0:T(2,128)S(1)}, s32[2,1,4,2]{2,3,1,0:T(2,128)}, u32[]{:S(2)}) copy-start(s32[2,1,4,2]{2,3,1,0:T(2,128)} %param.19) | copy-start | bytes 196
  23.6 14.8 %copy-start.9 = (f32[2,1,4,2]{2,3,1,0:T(2,128)S(1)}, f32[2,1,4,2]{2,3,1,0:T(2,128)}, u32[]{:S(2)}) copy-start(f32[2,1,4,2]{2,3,1,0:T(2,128)} %param.20) | copy-start | bytes 196
  23.6 23.8 %copy-start.2 = (bf16[4,3584]{1,0:T(4,128)(2,1)S(1)}, bf16[4,3584]{1,0:T(4,128)(2,1)}, u32[]{:S(2)}) copy-start(bf16[4,3584]{1,0:T(4,128)(2,1)} %refs_6_.5) | copy-start | bytes 86020
  23.6 23.8 %copy-start.3 = (bf16[4,3584]{1,0:T(4,128)(2,1)S(1)}, bf16[4,3584]{1,0:T(4,128)(2,1)}, u32[]{:S(2)}) copy-start(bf16[4,3584]{1,0:T(4,128)(2,1)} %refs_7_.1) | copy-start | bytes 86020

commit v9 on v7

--- a/solution.py
+++ b/solution.py
@@ -244,7 +244,7 @@
 
 
 def expert_kernel(tick, rows_ref, saved_ref, w_in, w_out, out_ref, *rest):
-    saved, slot_rows, joined, parts, saved_sem = rest[-5:]
+    saved, fwd_rows, bwd_columns, joined, parts, saved_sem = rest
     devices, block, half_width = rows_ref.shape
     per_expert = block // 4
     slots = devices * per_expert
@@ -259,30 +259,24 @@
     line = lax.broadcasted_iota(jnp.int32, (4 * slots, rows), 0)
     row = lax.broadcasted_iota(jnp.int32, (4 * slots, rows), 1)
     pick = jnp.where(row == home_of(line, slots, per_expert), 1.0, 0.0)
-    picked = exact_dot(pick, received).astype(jnp.bfloat16)
+    picked = exact_dot(pick, received)
     for half in range(2):
-        slot_rows[:, half * half_width : (half + 1) * half_width] = picked[
-            half * 2 * slots : (half + 1) * 2 * slots
-        ]
-
-    grad = lax.dot_general(
-        slot_rows[slots:],
-        w_out[...],
-        (((1,), (1,)), ((), ())),
-        preferred_element_type=jnp.float32,
-    )
-    gate_up = jnp.dot(slot_rows[:slots], w_in[...], preferred_element_type=jnp.float32)
+        columns = slice(half * half_width, (half + 1) * half_width)
+        start = half * 2 * slots
+        fwd_rows[:, columns] = picked[start : start + slots].astype(jnp.bfloat16)
+        bwd_columns[columns, :] = picked[start + slots : start + 2 * slots].T.astype(jnp.bfloat16)
+
+    grad = jnp.dot(w_out[...], bwd_columns[...], preferred_element_type=jnp.float32).T
+    gate_up = jnp.dot(fwd_rows[...], w_in[...], preferred_element_type=jnp.float32)
     saved_copy.wait()
     gate_pre = saved[:, :hidden_units]
     sigma = jax.nn.sigmoid(gate_pre)
     slope = sigma * (1.0 + gate_pre * (1.0 - sigma))
-    joined[:, :hidden_units] = (grad * saved[:, hidden_units:] * slope).astype(jnp.bfloat16)
-    joined[:, hidden_units:] = (grad * (gate_pre * sigma)).astype(jnp.bfloat16)
+    joined[:hidden_units] = (grad * saved[:, hidden_units:] * slope).T.astype(jnp.bfloat16)
+    joined[hidden_units:] = (grad * (gate_pre * sigma)).T.astype(jnp.bfloat16)
     gate = gate_up[:, :hidden_units]
     hidden = (gate * jax.nn.sigmoid(gate) * gate_up[:, hidden_units:]).astype(jnp.bfloat16)
-    back = lax.dot_general(
-        joined[...], w_in[...], (((1,), (1,)), ((), ())), preferred_element_type=jnp.float32
-    ).astype(jnp.bfloat16)
+    back = jnp.dot(w_in[...], joined[...], preferred_element_type=jnp.float32).T.astype(jnp.bfloat16)
     ahead = jnp.dot(hidden, w_out[...], preferred_element_type=jnp.float32).astype(jnp.bfloat16)
     for half in range(2):
         columns = slice(half * half_width, (half + 1) * half_width)
@@ -306,8 +300,9 @@
         out_specs=VMEM,
         scratch_shapes=[
             pltpu.VMEM((slots, both), jnp.float32),
-            pltpu.VMEM((2 * slots, width), jnp.bfloat16),
-            pltpu.VMEM((slots, both), jnp.bfloat16),
+            pltpu.VMEM((slots, width), jnp.bfloat16),
+            pltpu.VMEM((width, slots), jnp.bfloat16),
+            pltpu.VMEM((both, slots), jnp.bfloat16),
             pltpu.VMEM((4 * slots, width // 2), jnp.bfloat16),
             pltpu.SemaphoreType.DMA,
         ],

time: 80.9 us -> 82.1 us (1.015)
  Pallas kernels: 21.4 us -> 22.7 us
    pallas_call x2, Pallas kernels: 18 us -> 19.3 us  [expert_step(): pl.pallas_call(functools.partial(expert_kernel, tick), out_shape=pltpu.VM...]
where the time goes in v9:
time: 82.1 us; the launch traced here: 81.8 us
  blocking collectives  58.2 us (71%)
  Pallas kernels  22.7 us (28%)
    all_to_all x5, blocking collectives, exchange(): return lax.all_to_all(array, axis, split_axis=0, concat_axis=0, tiled=True)  58.2 us
    pallas_call x2, Pallas kernels, expert_step(): pl.pallas_call(functools.partial(expert_kernel, tick), out_shape=pltpu.VM...  19.3 us

profile of v9, /device:TPU:0, one launch (start us, length us, event | category | flops | bytes accessed | tf_op | source)
XLA Modules:
  0.0 81.8 jit_solution(6726131681148667774)
XLA Ops:
  0.6 0.0 copy-start
  0.6 0.0 copy-start.1
  0.6 1.4 %shard_map.122 = bf16[8,8,1792]{2,1,0:T(8,128)(2,1)S(1)} custom-call(s32[2,1,2,4]{3,2,1,0:T(2,128)} %bitcast.10, f32[2,1,2,4]{3,2,1,0:T(2,128)} %bitcast.14, s32[2,1,2,4]{3,2,1,0:T(2,128)} %bitcast.18, f32[2,1,2,4]{3,2,1,0:T(2,128)} %bitcast.22, bf16[1,4,3584]{2,1,0:T(4,128)(2,1)} %refs_5_.4, bf16[1,4,3584]{2,1,0:T(4,128)(2,1)} %refs_6_.3), custom_call_target="tpu_custom_call" | custom-call | flops 22020096000 | tf_op jit(solution)/shard_map/pallas_call | solution.py:114
  2.1 0.0 copy-start.4
  2.1 0.0 copy-start.5
  2.1 0.0 copy-start.6
  2.1 0.0 copy-start.7
  2.1 0.0 copy-start.8
  2.1 0.0 copy-start.9
  2.1 0.0 copy-start.2
  2.2 0.0 copy-start.3
  2.2 15.4 %all_to_all.25.rows_ref = bf16[8,8,1792]{2,1,0:T(8,128)(2,1)S(1)} all-to-all(bf16[8,8,1792]{2,1,0:T(8,128)(2,1)S(1)} %shard_map.122), channel_id=1, replica_groups=mesh['section'=4,'expert'=8] {'expert'}, dimensions={0} | all-to-all | bytes 458752 | tf_op jit(solution)/shard_map/all_to_all | solution.py:319
  17.6 0.0 copy-done
  17.6 9.6 %shard_map.123 = bf16[8,8,1792]{2,1,0:T(8,128)(2,1)S(1)} custom-call(bf16[8,8,1792]{2,1,0:T(8,128)(2,1)S(1)} %all_to_all.25.rows_ref, f32[2,1,1,16,2048]{4,3,2,1,0:T(8,128)} %saved_ref.3, bf16[3584,2048]{1,0:T(8,128)(2,1)S(1)} %bitcast.6, bf16[1024,3584]{1,0:T(8,128)(2,1)S(1)} %bitcast.8), custom_call_target="tpu_custom_call" | custom-call | flops 704643072 | tf_op jit(solution)/shard_map/pallas_call | solution.py:296
  27.2 11.4 %all_to_all.26.refs_4_ = bf16[8,8,1792]{2,1,0:T(8,128)(2,1)S(1)} all-to-all(bf16[8,8,1792]{2,1,0:T(8,128)(2,1)S(1)} %shard_map.123), channel_id=1, replica_groups=mesh['section'=4,'expert'=8] {'expert'}, dimensions={0} | all-to-all | bytes 458752 | tf_op jit(solution)/shard_map/all_to_all | solution.py:319
  38.7 0.0 copy-done.6
  38.7 0.5 shard_map.124
  39.2 8.5 %all_to_all.27.refs_4_.refs_5_ = bf16[4,8,1792]{2,1,0:T(8,128)(2,1)S(1)} all-to-all(bf16[4,8,1792]{2,1,0:T(8,128)(2,1)S(1)} %get-tuple-element.5), channel_id=1, replica_groups=mesh['section'=4,'expert'=8] {'section'}, dimensions={0} | all-to-all | bytes 229376 | tf_op jit(solution)/shard_map/all_to_all | solution.py:319
  47.7 0.0 copy-done.3
  47.7 0.4 shard_map.125
  48.1 11.4 %all_to_all.28.rows_ref = bf16[8,8,1792]{2,1,0:T(8,128)(2,1)S(1)} all-to-all(bf16[8,8,1792]{2,1,0:T(8,128)(2,1)S(1)} %shard_map.125), channel_id=1, replica_groups=mesh['section'=4,'expert'=8] {'expert'}, dimensions={0} | all-to-all | bytes 458752 | tf_op jit(solution)/shard_map/all_to_all | solution.py:319
  59.6 9.6 %shard_map.126 = bf16[8,8,1792]{2,1,0:T(8,128)(2,1)S(1)} custom-call(bf16[8,8,1792]{2,1,0:T(8,128)(2,1)S(1)} %all_to_all.28.rows_ref, f32[2,1,1,16,2048]{4,3,2,1,0:T(8,128)} %saved_ref.3, bf16[3584,2048]{1,0:T(8,128)(2,1)S(1)} %bitcast.7, bf16[1024,3584]{1,0:T(8,128)(2,1)S(1)} %bitcast.9), custom_call_target="tpu_custom_call" | custom-call | flops 704643072 | tf_op jit(solution)/shard_map/pallas_call | solution.py:296
  69.2 11.4 %all_to_all.29.refs_4_ = bf16[8,8,1792]{2,1,0:T(8,128)(2,1)S(1)} all-to-all(bf16[8,8,1792]{2,1,0:T(8,128)(2,1)S(1)} %shard_map.126), channel_id=1, replica_groups=mesh['section'=4,'expert'=8] {'expert'}, dimensions={0} | all-to-all | bytes 458752 | tf_op jit(solution)/shard_map/all_to_all | solution.py:319
  80.6 1.2 %shard_map.127 = (bf16[2,1,4,3584]{3,2,1,0:T(4,128)(2,1)}, bf16[2,1,4,3584]{3,2,1,0:T(4,128)(2,1)}) custom-call(s32[2,1,2,4]{3,2,1,0:T(2,128)S(1)} %bitcast.13, f32[2,1,2,4]{3,2,1,0:T(2,128)S(1)} %bitcast.17, s32[2,1,2,4]{3,2,1,0:T(2,128)S(1)} %bitcast.21, f32[2,1,2,4]{3,2,1,0:T(2,128)S(1)} %bitcast.25, bf16[8,8,1792]{2,1,0:T(8,128)(2,1)S(1)} %all_to_all.29.refs_4_, ...), custom_call_target="tpu_custom_call" | custom-call | tf_op jit(solution)/shard_map/pallas_call | solution.py:228
  (7 shorter events, 0.0 us)
Async XLA Ops:
  0.6 17.0 %copy-start = (bf16[1,1,3584,2048]{3,2,1,0:T(8,128)(2,1)S(1)}, bf16[1,1,3584,2048]{3,2,1,0:T(8,128)(2,1)}, u32[]{:S(2)}) copy-start(bf16[1,1,3584,2048]{3,2,1,0:T(8,128)(2,1)} %param.15) | copy-start | bytes 44040196
  0.6 17.0 %copy-start.1 = (bf16[1,1,1024,3584]{3,2,1,0:T(8,128)(2,1)S(1)}, bf16[1,1,1024,3584]{3,2,1,0:T(8,128)(2,1)}, u32[]{:S(2)}) copy-start(bf16[1,1,1024,3584]{3,2,1,0:T(8,128)(2,1)} %param.16) | copy-start | bytes 22020100
  2.1 36.6 %copy-start.4 = (bf16[1,4,3584]{2,1,0:T(4,128)(2,1)S(1)}, bf16[1,4,3584]{2,1,0:T(4,128)(2,1)}, u32[]{:S(2)}) copy-start(bf16[1,4,3584]{2,1,0:T(4,128)(2,1)} %refs_5_.4) | copy-start | bytes 86020
  2.1 36.6 %copy-start.5 = (bf16[1,4,3584]{2,1,0:T(4,128)(2,1)S(1)}, bf16[1,4,3584]{2,1,0:T(4,128)(2,1)}, u32[]{:S(2)}) copy-start(bf16[1,4,3584]{2,1,0:T(4,128)(2,1)} %refs_6_.3) | copy-start | bytes 86020
  2.1 36.6 %copy-start.6 = (s32[2,1,4,2]{2,3,1,0:T(2,128)S(1)}, s32[2,1,4,2]{2,3,1,0:T(2,128)}, u32[]{:S(2)}) copy-start(s32[2,1,4,2]{2,3,1,0:T(2,128)} %param.17) | copy-start | bytes 196
  2.1 36.6 %copy-start.7 = (f32[2,1,4,2]{2,3,1,0:T(2,128)S(1)}, f32[2,1,4,2]{2,3,1,0:T(2,128)}, u32[]{:S(2)}) copy-start(f32[2,1,4,2]{2,3,1,0:T(2,128)} %param.18) | copy-start | bytes 196
  2.1 36.6 %copy-start.8 = (s32[2,1,4,2]{2,3,1,0:T(2,128)S(1)}, s32[2,1,4,2]{2,3,1,0:T(2,128)}, u32[]{:S(2)}) copy-start(s32[2,1,4,2]{2,3,1,0:T(2,128)} %param.19) | copy-start | bytes 196
  2.1 36.6 %copy-start.9 = (f32[2,1,4,2]{2,3,1,0:T(2,128)S(1)}, f32[2,1,4,2]{2,3,1,0:T(2,128)}, u32[]{:S(2)}) copy-start(f32[2,1,4,2]{2,3,1,0:T(2,128)} %param.20) | copy-start | bytes 196
  2.1 45.6 %copy-start.2 = (bf16[4,3584]{1,0:T(4,128)(2,1)S(1)}, bf16[4,3584]{1,0:T(4,128)(2,1)}, u32[]{:S(2)}) copy-start(bf16[4,3584]{1,0:T(4,128)(2,1)} %refs_6_.5) | copy-start | bytes 86020
  2.2 45.6 %copy-start.3 = (bf16[4,3584]{1,0:T(4,128)(2,1)S(1)}, bf16[4,3584]{1,0:T(4,128)(2,1)}, u32[]{:S(2)}) copy-start(bf16[4,3584]{1,0:T(4,128)(2,1)} %refs_7_.1) | copy-start | bytes 86020

commit v10 on v7

--- a/solution.py
+++ b/solution.py
@@ -81,14 +81,14 @@
 def pack_into(out_ref, tick, per_expert, slices, tables, pairs):
     devices, block, half_width = out_ref.shape
     rows = devices * block
-    places, values = [], []
-    for direction, halves in enumerate(pairs):
+    places = []
+    for direction in range(2):
         place, _ = placing(
             tables[2 * direction], tables[2 * direction + 1], tick, direction, rows, per_expert, slices
         )
         side = half_of(rows, place.shape[1], per_expert)
         places += [jnp.where(side == half, place, 0.0) for half in range(2)]
-        values += [value.astype(jnp.float32) for value in halves]
+    values = [half.astype(jnp.float32) for halves in pairs() for half in halves]
     total = exact_dot(
         jnp.concatenate(places, axis=1), jnp.concatenate(values, axis=0).astype(jnp.bfloat16)
     )
@@ -103,9 +103,14 @@
     ]
     for copy in copies:
         copy.start()
-    for copy in copies:
+    for copy in copies[:4]:
         copy.wait()
-    pairs = [split_rows(tokens_ref[0]) for tokens_ref in local[4:]]
+
+    def pairs():
+        for copy in copies[4:]:
+            copy.wait()
+        return [split_rows(tokens_ref[0]) for tokens_ref in local[4:]]
+
     pack_into(out_ref, tick, per_expert, slices, local[:4], pairs)
 
 
@@ -125,7 +130,7 @@
 
 def later_pack_kernel(tick, per_expert, slices, *refs):
     tables, section_ref, enter_refs, out_ref = refs[:4], refs[4], refs[5:7], refs[7]
-    pack_into(out_ref, tick, per_expert, slices, tables, arriving(section_ref, enter_refs))
+    pack_into(out_ref, tick, per_expert, slices, tables, lambda: arriving(section_ref, enter_refs))
 
 
 def later_pack(tick, devices, per_expert, slices, routing, arrived, *entering):
@@ -244,16 +249,13 @@
 
 
 def expert_kernel(tick, rows_ref, saved_ref, w_in, w_out, out_ref, *rest):
-    saved, slot_rows, joined, parts, saved_sem = rest[-5:]
+    slot_rows, joined, parts = rest
     devices, block, half_width = rows_ref.shape
     per_expert = block // 4
     slots = devices * per_expert
     width, both = w_in.shape
     hidden_units = both // 2
     rows = devices * block
-
-    saved_copy = pltpu.make_async_copy(saved_ref.at[tick, 0, 0], saved, saved_sem)
-    saved_copy.start()
 
     received = rows_ref[...].reshape(rows, half_width)
     line = lax.broadcasted_iota(jnp.int32, (4 * slots, rows), 0)
@@ -272,11 +274,10 @@
         preferred_element_type=jnp.float32,
     )
     gate_up = jnp.dot(slot_rows[:slots], w_in[...], preferred_element_type=jnp.float32)
-    saved_copy.wait()
-    gate_pre = saved[:, :hidden_units]
+    gate_pre = saved_ref[tick, 0, 0, :, :hidden_units]
     sigma = jax.nn.sigmoid(gate_pre)
     slope = sigma * (1.0 + gate_pre * (1.0 - sigma))
-    joined[:, :hidden_units] = (grad * saved[:, hidden_units:] * slope).astype(jnp.bfloat16)
+    joined[:, :hidden_units] = (grad * saved_ref[tick, 0, 0, :, hidden_units:] * slope).astype(jnp.bfloat16)
     joined[:, hidden_units:] = (grad * (gate_pre * sigma)).astype(jnp.bfloat16)
     gate = gate_up[:, :hidden_units]
     hidden = (gate * jax.nn.sigmoid(gate) * gate_up[:, hidden_units:]).astype(jnp.bfloat16)
@@ -302,14 +303,12 @@
     return pl.pallas_call(
         functools.partial(expert_kernel, tick),
         out_shape=pltpu.VMEM(rows.shape, jnp.bfloat16),
-        in_specs=[VMEM, HBM, VMEM, VMEM],
+        in_specs=[VMEM] * 4,
         out_specs=VMEM,
         scratch_shapes=[
-            pltpu.VMEM((slots, both), jnp.float32),
             pltpu.VMEM((2 * slots, width), jnp.bfloat16),
             pltpu.VMEM((slots, both), jnp.bfloat16),
             pltpu.VMEM((4 * slots, width // 2), jnp.bfloat16),
-            pltpu.SemaphoreType.DMA,
         ],
         compiler_params=pltpu.CompilerParams(vmem_limit_bytes=EXPERT_VMEM),
         cost_estimate=pl.CostEstimate(
@@ -317,7 +316,7 @@
             bytes_accessed=0,
             transcendentals=0,
         ),
-    )(rows, pltpu.with_memory_space_constraint(saved_pre, pltpu.HBM), w_in, w_out)
+    )(rows, saved_pre, w_in, w_out)
 
 
 def exchange(array, axis):
@@ -347,6 +346,7 @@
     w_in, w_out = (
         pltpu.with_memory_space_constraint(w.reshape(w.shape[2:]), pltpu.VMEM) for w in (w_in, w_out)
     )
+    saved_pre = pltpu.with_memory_space_constraint(saved_pre, pltpu.VMEM)
     sent = first_pack(0, devices, per_expert, slices, routing, fwd_act, bwd_grad, beside)
     parts = expert_step(0, exchange(sent, "expert"), saved_pre, w_in, w_out)
     moved, fwd_next, bwd_next = relay(

time: 80.9 us -> 80.4 us (level)
  no operation moved by 1% of the time
where the time goes in v10:
time: 80.4 us; the launch traced here: 80.2 us
  blocking collectives  58.2 us (72%)
  Pallas kernels  21.1 us (26%)
    all_to_all x5, blocking collectives, exchange(): return lax.all_to_all(array, axis, split_axis=0, concat_axis=0, tiled=True)  58.2 us
    pallas_call x2, Pallas kernels, expert_step(): pl.pallas_call(functools.partial(expert_kernel, tick), out_shape=pltpu.VM...  17.7 us

profile of v10, /device:TPU:0, one launch (start us, length us, event | category | flops | bytes accessed | tf_op | source)
XLA Modules:
  0.0 80.2 jit_solution(1950964901146558922)
XLA Ops:
  0.6 0.0 copy-start
  0.6 0.0 copy-start.1
  0.7 1.3 %shard_map.122 = bf16[8,8,1792]{2,1,0:T(8,128)(2,1)S(1)} custom-call(s32[2,1,2,4]{3,2,1,0:T(2,128)} %bitcast.10, f32[2,1,2,4]{3,2,1,0:T(2,128)} %bitcast.14, s32[2,1,2,4]{3,2,1,0:T(2,128)} %bitcast.18, f32[2,1,2,4]{3,2,1,0:T(2,128)} %bitcast.22, bf16[1,4,3584]{2,1,0:T(4,128)(2,1)} %refs_5_.4, bf16[1,4,3584]{2,1,0:T(4,128)(2,1)} %refs_6_.3), custom_call_target="tpu_custom_call" | custom-call | flops 22020096000 | tf_op jit(solution)/shard_map/pallas_call | solution.py:119
  2.0 0.0 copy-start.5
  2.0 0.0 copy-start.6
  2.0 0.0 copy-start.7
  2.0 0.0 copy-start.8
  2.0 0.0 copy-start.9
  2.0 0.0 copy-start.10
  2.1 0.0 copy-start.3
  2.1 0.0 copy-start.4
  2.1 15.4 %all_to_all.25.rows_ref = bf16[8,8,1792]{2,1,0:T(8,128)(2,1)S(1)} all-to-all(bf16[8,8,1792]{2,1,0:T(8,128)(2,1)S(1)} %shard_map.122), channel_id=1, replica_groups=mesh['section'=4,'expert'=8] {'expert'}, dimensions={0} | all-to-all | bytes 458752 | tf_op jit(solution)/shard_map/all_to_all | solution.py:323
  17.5 0.0 copy-done
  17.5 8.9 %shard_map.123 = bf16[8,8,1792]{2,1,0:T(8,128)(2,1)S(1)} custom-call(bf16[8,8,1792]{2,1,0:T(8,128)(2,1)S(1)} %all_to_all.25.rows_ref, f32[2,1,1,16,2048]{4,3,2,1,0:T(8,128)S(1)} %copy-done.2, bf16[3584,2048]{1,0:T(8,128)(2,1)S(1)} %bitcast.6, bf16[1024,3584]{1,0:T(8,128)(2,1)S(1)} %bitcast.8), custom_call_target="tpu_custom_call" | custom-call | flops 704643072 | tf_op jit(solution)/shard_map/pallas_call | solution.py:303
  26.4 11.4 %all_to_all.26.refs_4_ = bf16[8,8,1792]{2,1,0:T(8,128)(2,1)S(1)} all-to-all(bf16[8,8,1792]{2,1,0:T(8,128)(2,1)S(1)} %shard_map.123), channel_id=1, replica_groups=mesh['section'=4,'expert'=8] {'expert'}, dimensions={0} | all-to-all | bytes 458752 | tf_op jit(solution)/shard_map/all_to_all | solution.py:323
  37.8 0.0 copy-done.5
  37.9 0.5 shard_map.124
  38.4 8.5 %all_to_all.27.refs_4_.refs_5_ = bf16[4,8,1792]{2,1,0:T(8,128)(2,1)S(1)} all-to-all(bf16[4,8,1792]{2,1,0:T(8,128)(2,1)S(1)} %get-tuple-element.5), channel_id=1, replica_groups=mesh['section'=4,'expert'=8] {'section'}, dimensions={0} | all-to-all | bytes 229376 | tf_op jit(solution)/shard_map/all_to_all | solution.py:323
  46.9 0.0 copy-done.3
  46.9 0.4 shard_map.125
  47.3 11.4 %all_to_all.28.rows_ref = bf16[8,8,1792]{2,1,0:T(8,128)(2,1)S(1)} all-to-all(bf16[8,8,1792]{2,1,0:T(8,128)(2,1)S(1)} %shard_map.125), channel_id=1, replica_groups=mesh['section'=4,'expert'=8] {'expert'}, dimensions={0} | all-to-all | bytes 458752 | tf_op jit(solution)/shard_map/all_to_all | solution.py:323
  58.7 8.9 %shard_map.126 = bf16[8,8,1792]{2,1,0:T(8,128)(2,1)S(1)} custom-call(bf16[8,8,1792]{2,1,0:T(8,128)(2,1)S(1)} %all_to_all.28.rows_ref, f32[2,1,1,16,2048]{4,3,2,1,0:T(8,128)S(1)} %copy-done.2, bf16[3584,2048]{1,0:T(8,128)(2,1)S(1)} %bitcast.7, bf16[1024,3584]{1,0:T(8,128)(2,1)S(1)} %bitcast.9), custom_call_target="tpu_custom_call" | custom-call | flops 704643072 | tf_op jit(solution)/shard_map/pallas_call | solution.py:303
  67.6 11.4 %all_to_all.29.refs_4_ = bf16[8,8,1792]{2,1,0:T(8,128)(2,1)S(1)} all-to-all(bf16[8,8,1792]{2,1,0:T(8,128)(2,1)S(1)} %shard_map.126), channel_id=1, replica_groups=mesh['section'=4,'expert'=8] {'expert'}, dimensions={0} | all-to-all | bytes 458752 | tf_op jit(solution)/shard_map/all_to_all | solution.py:323
  79.0 1.2 %shard_map.127 = (bf16[2,1,4,3584]{3,2,1,0:T(4,128)(2,1)}, bf16[2,1,4,3584]{3,2,1,0:T(4,128)(2,1)}) custom-call(s32[2,1,2,4]{3,2,1,0:T(2,128)S(1)} %bitcast.13, f32[2,1,2,4]{3,2,1,0:T(2,128)S(1)} %bitcast.17, s32[2,1,2,4]{3,2,1,0:T(2,128)S(1)} %bitcast.21, f32[2,1,2,4]{3,2,1,0:T(2,128)S(1)} %bitcast.25, bf16[8,8,1792]{2,1,0:T(8,128)(2,1)S(1)} %all_to_all.29.refs_4_, ...), custom_call_target="tpu_custom_call" | custom-call | tf_op jit(solution)/shard_map/pallas_call | solution.py:233
  (9 shorter events, 0.0 us)
Async XLA Ops:
  0.6 16.9 %copy-start = (bf16[1,1,3584,2048]{3,2,1,0:T(8,128)(2,1)S(1)}, bf16[1,1,3584,2048]{3,2,1,0:T(8,128)(2,1)}, u32[]{:S(2)}) copy-start(bf16[1,1,3584,2048]{3,2,1,0:T(8,128)(2,1)} %param.15) | copy-start | bytes 44040196
  0.6 16.9 %copy-start.1 = (bf16[1,1,1024,3584]{3,2,1,0:T(8,128)(2,1)S(1)}, bf16[1,1,1024,3584]{3,2,1,0:T(8,128)(2,1)}, u32[]{:S(2)}) copy-start(bf16[1,1,1024,3584]{3,2,1,0:T(8,128)(2,1)} %param.16) | copy-start | bytes 22020100
  0.7 16.9 %copy-start.2 = (f32[2,1,1,16,2048]{4,3,2,1,0:T(8,128)S(1)}, f32[2,1,1,16,2048]{4,3,2,1,0:T(8,128)}, u32[]{:S(2)}) copy-start(f32[2,1,1,16,2048]{4,3,2,1,0:T(8,128)} %saved_ref.3) | copy-start | bytes 786436
  2.0 35.8 %copy-start.5 = (bf16[1,4,3584]{2,1,0:T(4,128)(2,1)S(1)}, bf16[1,4,3584]{2,1,0:T(4,128)(2,1)}, u32[]{:S(2)}) copy-start(bf16[1,4,3584]{2,1,0:T(4,128)(2,1)} %refs_5_.4) | copy-start | bytes 86020
  2.0 35.8 %copy-start.6 = (bf16[1,4,3584]{2,1,0:T(4,128)(2,1)S(1)}, bf16[1,4,3584]{2,1,0:T(4,128)(2,1)}, u32[]{:S(2)}) copy-start(bf16[1,4,3584]{2,1,0:T(4,128)(2,1)} %refs_6_.3) | copy-start | bytes 86020
  2.0 35.8 %copy-start.7 = (s32[2,1,4,2]{2,3,1,0:T(2,128)S(1)}, s32[2,1,4,2]{2,3,1,0:T(2,128)}, u32[]{:S(2)}) copy-start(s32[2,1,4,2]{2,3,1,0:T(2,128)} %param.17) | copy-start | bytes 196
  2.0 35.8 %copy-start.8 = (f32[2,1,4,2]{2,3,1,0:T(2,128)S(1)}, f32[2,1,4,2]{2,3,1,0:T(2,128)}, u32[]{:S(2)}) copy-start(f32[2,1,4,2]{2,3,1,0:T(2,128)} %param.18) | copy-start | bytes 196
  2.0 35.8 %copy-start.9 = (s32[2,1,4,2]{2,3,1,0:T(2,128)S(1)}, s32[2,1,4,2]{2,3,1,0:T(2,128)}, u32[]{:S(2)}) copy-start(s32[2,1,4,2]{2,3,1,0:T(2,128)} %param.19) | copy-start | bytes 196
  2.0 35.8 %copy-start.10 = (f32[2,1,4,2]{2,3,1,0:T(2,128)S(1)}, f32[2,1,4,2]{2,3,1,0:T(2,128)}, u32[]{:S(2)}) copy-start(f32[2,1,4,2]{2,3,1,0:T(2,128)} %param.20) | copy-start | bytes 196
  2.1 44.8 %copy-start.3 = (bf16[4,3584]{1,0:T(4,128)(2,1)S(1)}, bf16[4,3584]{1,0:T(4,128)(2,1)}, u32[]{:S(2)}) copy-start(bf16[4,3584]{1,0:T(4,128)(2,1)} %refs_6_.5) | copy-start | bytes 86020
  2.1 44.8 %copy-start.4 = (bf16[4,3584]{1,0:T(4,128)(2,1)S(1)}, bf16[4,3584]{1,0:T(4,128)(2,1)}, u32[]{:S(2)}) copy-start(bf16[4,3584]{1,0:T(4,128)(2,1)} %refs_7_.1) | copy-start | bytes 86020

commit v11 on v10

--- a/solution.py
+++ b/solution.py
@@ -248,8 +248,7 @@
     )
 
 
-def expert_kernel(tick, rows_ref, saved_ref, w_in, w_out, out_ref, *rest):
-    slot_rows, joined, parts = rest
+def expert_kernel(tick, rows_ref, saved_ref, w_in, w_out, out_ref):
     devices, block, half_width = rows_ref.shape
     per_expert = block // 4
     slots = devices * per_expert
@@ -262,10 +261,7 @@
     row = lax.broadcasted_iota(jnp.int32, (4 * slots, rows), 1)
     pick = jnp.where(row == home_of(line, slots, per_expert), 1.0, 0.0)
     picked = exact_dot(pick, received).astype(jnp.bfloat16)
-    for half in range(2):
-        slot_rows[:, half * half_width : (half + 1) * half_width] = picked[
-            half * 2 * slots : (half + 1) * 2 * slots
-        ]
+    slot_rows = jnp.concatenate([picked[: 2 * slots], picked[2 * slots :]], axis=1)
 
     grad = lax.dot_general(
         slot_rows[slots:],
@@ -277,24 +273,24 @@
     gate_pre = saved_ref[tick, 0, 0, :, :hidden_units]
     sigma = jax.nn.sigmoid(gate_pre)
     slope = sigma * (1.0 + gate_pre * (1.0 - sigma))
-    joined[:, :hidden_units] = (grad * saved_ref[tick, 0, 0, :, hidden_units:] * slope).astype(jnp.bfloat16)
-    joined[:, hidden_units:] = (grad * (gate_pre * sigma)).astype(jnp.bfloat16)
+    joined_gate = (grad * saved_ref[tick, 0, 0, :, hidden_units:] * slope).astype(jnp.bfloat16)
+    joined_up = (grad * (gate_pre * sigma)).astype(jnp.bfloat16)
+    joined = jnp.concatenate([joined_gate, joined_up], axis=1)
     gate = gate_up[:, :hidden_units]
     hidden = (gate * jax.nn.sigmoid(gate) * gate_up[:, hidden_units:]).astype(jnp.bfloat16)
     back = lax.dot_general(
-        joined[...], w_in[...], (((1,), (1,)), ((), ())), preferred_element_type=jnp.float32
+        joined, w_in[...], (((1,), (1,)), ((), ())), preferred_element_type=jnp.float32
     ).astype(jnp.bfloat16)
     ahead = jnp.dot(hidden, w_out[...], preferred_element_type=jnp.float32).astype(jnp.bfloat16)
-    for half in range(2):
-        columns = slice(half * half_width, (half + 1) * half_width)
-        start = half * 2 * slots
-        parts[start : start + slots] = ahead[:, columns]
-        parts[start + slots : start + 2 * slots] = back[:, columns]
+    parts = jnp.concatenate(
+        [ahead[:, :half_width], back[:, :half_width], ahead[:, half_width:], back[:, half_width:]],
+        axis=0,
+    )
 
     row = lax.broadcasted_iota(jnp.int32, (rows, 4 * slots), 0)
     line = lax.broadcasted_iota(jnp.int32, (rows, 4 * slots), 1)
     spread = jnp.where(row == home_of(line, slots, per_expert), 1.0, 0.0)
-    out_ref[...] = exact_dot(spread, parts[...]).astype(jnp.bfloat16).reshape(out_ref.shape)
+    out_ref[...] = exact_dot(spread, parts).astype(jnp.bfloat16).reshape(out_ref.shape)
 
 
 def expert_step(tick, rows, saved_pre, w_in, w_out):
@@ -305,11 +301,6 @@
         out_shape=pltpu.VMEM(rows.shape, jnp.bfloat16),
         in_specs=[VMEM] * 4,
         out_specs=VMEM,
-        scratch_shapes=[
-            pltpu.VMEM((2 * slots, width), jnp.bfloat16),
-            pltpu.VMEM((slots, both), jnp.bfloat16),
-            pltpu.VMEM((4 * slots, width // 2), jnp.bfloat16),
-        ],
         compiler_params=pltpu.CompilerParams(vmem_limit_bytes=EXPERT_VMEM),
         cost_estimate=pl.CostEstimate(
             flops=12 * slots * width * (both // 2),

time: 80.4 us -> 80.4 us (level)
  no operation moved by 1% of the time
where the time goes in v11:
time: 80.4 us; the launch traced here: 80.2 us
  blocking collectives  58.2 us (72%)
  Pallas kernels  21.1 us (26%)
    all_to_all x5, blocking collectives, exchange(): return lax.all_to_all(array, axis, split_axis=0, concat_axis=0, tiled=True)  58.2 us
    pallas_call x2, Pallas kernels, expert_step(): pl.pallas_call(functools.partial(expert_kernel, tick), out_shape=pltpu.VM...  17.7 us

profile of v11, /device:TPU:0, one launch (start us, length us, event | category | flops | bytes accessed | tf_op | source)
XLA Modules:
  0.0 80.2 jit_solution(4084673096587874875)
XLA Ops:
  0.6 0.0 copy-start
  0.6 0.0 copy-start.1
  0.7 1.3 %shard_map.122 = bf16[8,8,1792]{2,1,0:T(8,128)(2,1)S(1)} custom-call(s32[2,1,2,4]{3,2,1,0:T(2,128)} %bitcast.10, f32[2,1,2,4]{3,2,1,0:T(2,128)} %bitcast.14, s32[2,1,2,4]{3,2,1,0:T(2,128)} %bitcast.18, f32[2,1,2,4]{3,2,1,0:T(2,128)} %bitcast.22, bf16[1,4,3584]{2,1,0:T(4,128)(2,1)} %refs_5_.4, bf16[1,4,3584]{2,1,0:T(4,128)(2,1)} %refs_6_.3), custom_call_target="tpu_custom_call" | custom-call | flops 22020096000 | tf_op jit(solution)/shard_map/pallas_call | solution.py:119
  2.0 0.0 copy-start.5
  2.0 0.0 copy-start.6
  2.0 0.0 copy-start.7
  2.0 0.0 copy-start.8
  2.0 0.0 copy-start.9
  2.0 0.0 copy-start.10
  2.1 0.0 copy-start.3
  2.1 0.0 copy-start.4
  2.1 15.4 %all_to_all.25.rows_ref = bf16[8,8,1792]{2,1,0:T(8,128)(2,1)S(1)} all-to-all(bf16[8,8,1792]{2,1,0:T(8,128)(2,1)S(1)} %shard_map.122), channel_id=1, replica_groups=mesh['section'=4,'expert'=8] {'expert'}, dimensions={0} | all-to-all | bytes 458752 | tf_op jit(solution)/shard_map/all_to_all | solution.py:314
  17.5 0.0 copy-done
  17.5 8.9 %shard_map.123 = bf16[8,8,1792]{2,1,0:T(8,128)(2,1)S(1)} custom-call(bf16[8,8,1792]{2,1,0:T(8,128)(2,1)S(1)} %all_to_all.25.rows_ref, f32[2,1,1,16,2048]{4,3,2,1,0:T(8,128)S(1)} %copy-done.2, bf16[3584,2048]{1,0:T(8,128)(2,1)S(1)} %bitcast.6, bf16[1024,3584]{1,0:T(8,128)(2,1)S(1)} %bitcast.8), custom_call_target="tpu_custom_call" | custom-call | flops 704643072 | tf_op jit(solution)/shard_map/pallas_call | solution.py:299
  26.4 11.4 %all_to_all.26.refs_4_ = bf16[8,8,1792]{2,1,0:T(8,128)(2,1)S(1)} all-to-all(bf16[8,8,1792]{2,1,0:T(8,128)(2,1)S(1)} %shard_map.123), channel_id=1, replica_groups=mesh['section'=4,'expert'=8] {'expert'}, dimensions={0} | all-to-all | bytes 458752 | tf_op jit(solution)/shard_map/all_to_all | solution.py:314
  37.8 0.0 copy-done.6
  37.9 0.5 shard_map.124
  38.4 8.5 %all_to_all.27.refs_4_.refs_5_ = bf16[4,8,1792]{2,1,0:T(8,128)(2,1)S(1)} all-to-all(bf16[4,8,1792]{2,1,0:T(8,128)(2,1)S(1)} %get-tuple-element.5), channel_id=1, replica_groups=mesh['section'=4,'expert'=8] {'section'}, dimensions={0} | all-to-all | bytes 229376 | tf_op jit(solution)/shard_map/all_to_all | solution.py:314
  46.9 0.0 copy-done.3
  46.9 0.4 shard_map.125
  47.3 11.4 %all_to_all.28.rows_ref = bf16[8,8,1792]{2,1,0:T(8,128)(2,1)S(1)} all-to-all(bf16[8,8,1792]{2,1,0:T(8,128)(2,1)S(1)} %shard_map.125), channel_id=1, replica_groups=mesh['section'=4,'expert'=8] {'expert'}, dimensions={0} | all-to-all | bytes 458752 | tf_op jit(solution)/shard_map/all_to_all | solution.py:314
  58.7 8.9 %shard_map.126 = bf16[8,8,1792]{2,1,0:T(8,128)(2,1)S(1)} custom-call(bf16[8,8,1792]{2,1,0:T(8,128)(2,1)S(1)} %all_to_all.28.rows_ref, f32[2,1,1,16,2048]{4,3,2,1,0:T(8,128)S(1)} %copy-done.2, bf16[3584,2048]{1,0:T(8,128)(2,1)S(1)} %bitcast.7, bf16[1024,3584]{1,0:T(8,128)(2,1)S(1)} %bitcast.9), custom_call_target="tpu_custom_call" | custom-call | flops 704643072 | tf_op jit(solution)/shard_map/pallas_call | solution.py:299
  67.6 11.4 %all_to_all.29.refs_4_ = bf16[8,8,1792]{2,1,0:T(8,128)(2,1)S(1)} all-to-all(bf16[8,8,1792]{2,1,0:T(8,128)(2,1)S(1)} %shard_map.126), channel_id=1, replica_groups=mesh['section'=4,'expert'=8] {'expert'}, dimensions={0} | all-to-all | bytes 458752 | tf_op jit(solution)/shard_map/all_to_all | solution.py:314
  79.0 1.2 %shard_map.127 = (bf16[2,1,4,3584]{3,2,1,0:T(4,128)(2,1)}, bf16[2,1,4,3584]{3,2,1,0:T(4,128)(2,1)}) custom-call(s32[2,1,2,4]{3,2,1,0:T(2,128)S(1)} %bitcast.13, f32[2,1,2,4]{3,2,1,0:T(2,128)S(1)} %bitcast.17, s32[2,1,2,4]{3,2,1,0:T(2,128)S(1)} %bitcast.21, f32[2,1,2,4]{3,2,1,0:T(2,128)S(1)} %bitcast.25, bf16[8,8,1792]{2,1,0:T(8,128)(2,1)S(1)} %all_to_all.29.refs_4_, ...), custom_call_target="tpu_custom_call" | custom-call | tf_op jit(solution)/shard_map/pallas_call | solution.py:233
  (9 shorter events, 0.0 us)
Async XLA Ops:
  0.6 16.9 %copy-start = (bf16[1,1,3584,2048]{3,2,1,0:T(8,128)(2,1)S(1)}, bf16[1,1,3584,2048]{3,2,1,0:T(8,128)(2,1)}, u32[]{:S(2)}) copy-start(bf16[1,1,3584,2048]{3,2,1,0:T(8,128)(2,1)} %param.15) | copy-start | bytes 44040196
  0.6 16.9 %copy-start.1 = (bf16[1,1,1024,3584]{3,2,1,0:T(8,128)(2,1)S(1)}, bf16[1,1,1024,3584]{3,2,1,0:T(8,128)(2,1)}, u32[]{:S(2)}) copy-start(bf16[1,1,1024,3584]{3,2,1,0:T(8,128)(2,1)} %param.16) | copy-start | bytes 22020100
  0.7 16.9 %copy-start.2 = (f32[2,1,1,16,2048]{4,3,2,1,0:T(8,128)S(1)}, f32[2,1,1,16,2048]{4,3,2,1,0:T(8,128)}, u32[]{:S(2)}) copy-start(f32[2,1,1,16,2048]{4,3,2,1,0:T(8,128)} %saved_ref.3) | copy-start | bytes 786436
  2.0 35.8 %copy-start.5 = (bf16[1,4,3584]{2,1,0:T(4,128)(2,1)S(1)}, bf16[1,4,3584]{2,1,0:T(4,128)(2,1)}, u32[]{:S(2)}) copy-start(bf16[1,4,3584]{2,1,0:T(4,128)(2,1)} %refs_5_.4) | copy-start | bytes 86020
  2.0 35.8 %copy-start.6 = (bf16[1,4,3584]{2,1,0:T(4,128)(2,1)S(1)}, bf16[1,4,3584]{2,1,0:T(4,128)(2,1)}, u32[]{:S(2)}) copy-start(bf16[1,4,3584]{2,1,0:T(4,128)(2,1)} %refs_6_.3) | copy-start | bytes 86020
  2.0 35.8 %copy-start.7 = (s32[2,1,4,2]{2,3,1,0:T(2,128)S(1)}, s32[2,1,4,2]{2,3,1,0:T(2,128)}, u32[]{:S(2)}) copy-start(s32[2,1,4,2]{2,3,1,0:T(2,128)} %param.17) | copy-start | bytes 196
  2.0 35.8 %copy-start.8 = (f32[2,1,4,2]{2,3,1,0:T(2,128)S(1)}, f32[2,1,4,2]{2,3,1,0:T(2,128)}, u32[]{:S(2)}) copy-start(f32[2,1,4,2]{2,3,1,0:T(2,128)} %param.18) | copy-start | bytes 196
  2.0 35.8 %copy-start.9 = (s32[2,1,4,2]{2,3,1,0:T(2,128)S(1)}, s32[2,1,4,2]{2,3,1,0:T(2,128)}, u32[]{:S(2)}) copy-start(s32[2,1,4,2]{2,3,1,0:T(2,128)} %param.19) | copy-start | bytes 196
  2.0 35.8 %copy-start.10 = (f32[2,1,4,2]{2,3,1,0:T(2,128)S(1)}, f32[2,1,4,2]{2,3,1,0:T(2,128)}, u32[]{:S(2)}) copy-start(f32[2,1,4,2]{2,3,1,0:T(2,128)} %param.20) | copy-start | bytes 196
  2.1 44.8 %copy-start.3 = (bf16[4,3584]{1,0:T(4,128)(2,1)S(1)}, bf16[4,3584]{1,0:T(4,128)(2,1)}, u32[]{:S(2)}) copy-start(bf16[4,3584]{1,0:T(4,128)(2,1)} %refs_6_.5) | copy-start | bytes 86020
  2.1 44.8 %copy-start.4 = (bf16[4,3584]{1,0:T(4,128)(2,1)S(1)}, bf16[4,3584]{1,0:T(4,128)(2,1)}, u32[]{:S(2)}) copy-start(bf16[4,3584]{1,0:T(4,128)(2,1)} %refs_7_.1) | copy-start | bytes 86020

commit v12 on v11

--- a/solution.py
+++ b/solution.py
@@ -263,13 +263,13 @@
     picked = exact_dot(pick, received).astype(jnp.bfloat16)
     slot_rows = jnp.concatenate([picked[: 2 * slots], picked[2 * slots :]], axis=1)
 
+    gate_up = jnp.dot(slot_rows[:slots], w_in[...], preferred_element_type=jnp.float32)
     grad = lax.dot_general(
         slot_rows[slots:],
         w_out[...],
         (((1,), (1,)), ((), ())),
         preferred_element_type=jnp.float32,
     )
-    gate_up = jnp.dot(slot_rows[:slots], w_in[...], preferred_element_type=jnp.float32)
     gate_pre = saved_ref[tick, 0, 0, :, :hidden_units]
     sigma = jax.nn.sigmoid(gate_pre)
     slope = sigma * (1.0 + gate_pre * (1.0 - sigma))

time: 80.4 us -> 80.5 us (level)
  no operation moved by 1% of the time
where the time goes in v12:
time: 80.5 us; the launch traced here: 80.2 us
  blocking collectives  58.2 us (72%)
  Pallas kernels  21.2 us (26%)
    all_to_all x5, blocking collectives, exchange(): return lax.all_to_all(array, axis, split_axis=0, concat_axis=0, tiled=True)  58.2 us
    pallas_call x2, Pallas kernels, expert_step(): pl.pallas_call(functools.partial(expert_kernel, tick), out_shape=pltpu.VM...  17.8 us

profile of v12, /device:TPU:0, one launch (start us, length us, event | category | flops | bytes accessed | tf_op | source)
XLA Modules:
  0.0 80.2 jit_solution(16842622410048621759)
XLA Ops:
  0.6 0.0 copy-start
  0.6 0.0 copy-start.1
  0.7 0.0 copy-start.2
  0.7 1.3 %shard_map.122 = bf16[8,8,1792]{2,1,0:T(8,128)(2,1)S(1)} custom-call(s32[2,1,2,4]{3,2,1,0:T(2,128)} %bitcast.10, f32[2,1,2,4]{3,2,1,0:T(2,128)} %bitcast.14, s32[2,1,2,4]{3,2,1,0:T(2,128)} %bitcast.18, f32[2,1,2,4]{3,2,1,0:T(2,128)} %bitcast.22, bf16[1,4,3584]{2,1,0:T(4,128)(2,1)} %refs_5_.4, bf16[1,4,3584]{2,1,0:T(4,128)(2,1)} %refs_6_.3), custom_call_target="tpu_custom_call" | custom-call | flops 22020096000 | tf_op jit(solution)/shard_map/pallas_call | solution.py:119
  2.0 0.0 copy-start.5
  2.0 0.0 copy-start.6
  2.0 0.0 copy-start.7
  2.0 0.0 copy-start.8
  2.0 0.0 copy-start.9
  2.0 0.0 copy-start.10
  2.1 0.0 copy-start.3
  2.1 0.0 copy-start.4
  2.1 15.4 %all_to_all.25.rows_ref = bf16[8,8,1792]{2,1,0:T(8,128)(2,1)S(1)} all-to-all(bf16[8,8,1792]{2,1,0:T(8,128)(2,1)S(1)} %shard_map.122), channel_id=1, replica_groups=mesh['section'=4,'expert'=8] {'expert'}, dimensions={0} | all-to-all | bytes 458752 | tf_op jit(solution)/shard_map/all_to_all | solution.py:314
  17.5 0.0 copy-done
  17.5 8.9 %shard_map.123 = bf16[8,8,1792]{2,1,0:T(8,128)(2,1)S(1)} custom-call(bf16[8,8,1792]{2,1,0:T(8,128)(2,1)S(1)} %all_to_all.25.rows_ref, f32[2,1,1,16,2048]{4,3,2,1,0:T(8,128)S(1)} %copy-done.2, bf16[3584,2048]{1,0:T(8,128)(2,1)S(1)} %bitcast.6, bf16[1024,3584]{1,0:T(8,128)(2,1)S(1)} %bitcast.8), custom_call_target="tpu_custom_call" | custom-call | flops 704643072 | tf_op jit(solution)/shard_map/pallas_call | solution.py:299
  26.4 11.4 %all_to_all.26.refs_4_ = bf16[8,8,1792]{2,1,0:T(8,128)(2,1)S(1)} all-to-all(bf16[8,8,1792]{2,1,0:T(8,128)(2,1)S(1)} %shard_map.123), channel_id=1, replica_groups=mesh['section'=4,'expert'=8] {'expert'}, dimensions={0} | all-to-all | bytes 458752 | tf_op jit(solution)/shard_map/all_to_all | solution.py:314
  37.9 0.0 copy-done.6
  37.9 0.5 shard_map.124
  38.4 8.5 %all_to_all.27.refs_4_.refs_5_ = bf16[4,8,1792]{2,1,0:T(8,128)(2,1)S(1)} all-to-all(bf16[4,8,1792]{2,1,0:T(8,128)(2,1)S(1)} %get-tuple-element.5), channel_id=1, replica_groups=mesh['section'=4,'expert'=8] {'section'}, dimensions={0} | all-to-all | bytes 229376 | tf_op jit(solution)/shard_map/all_to_all | solution.py:314
  46.9 0.4 shard_map.125
  47.3 11.4 %all_to_all.28.rows_ref = bf16[8,8,1792]{2,1,0:T(8,128)(2,1)S(1)} all-to-all(bf16[8,8,1792]{2,1,0:T(8,128)(2,1)S(1)} %shard_map.125), channel_id=1, replica_groups=mesh['section'=4,'expert'=8] {'expert'}, dimensions={0} | all-to-all | bytes 458752 | tf_op jit(solution)/shard_map/all_to_all | solution.py:314
  58.7 8.9 %shard_map.126 = bf16[8,8,1792]{2,1,0:T(8,128)(2,1)S(1)} custom-call(bf16[8,8,1792]{2,1,0:T(8,128)(2,1)S(1)} %all_to_all.28.rows_ref, f32[2,1,1,16,2048]{4,3,2,1,0:T(8,128)S(1)} %copy-done.2, bf16[3584,2048]{1,0:T(8,128)(2,1)S(1)} %bitcast.7, bf16[1024,3584]{1,0:T(8,128)(2,1)S(1)} %bitcast.9), custom_call_target="tpu_custom_call" | custom-call | flops 704643072 | tf_op jit(solution)/shard_map/pallas_call | solution.py:299
  67.6 11.4 %all_to_all.29.refs_4_ = bf16[8,8,1792]{2,1,0:T(8,128)(2,1)S(1)} all-to-all(bf16[8,8,1792]{2,1,0:T(8,128)(2,1)S(1)} %shard_map.126), channel_id=1, replica_groups=mesh['section'=4,'expert'=8] {'expert'}, dimensions={0} | all-to-all | bytes 458752 | tf_op jit(solution)/shard_map/all_to_all | solution.py:314
  79.1 1.2 %shard_map.127 = (bf16[2,1,4,3584]{3,2,1,0:T(4,128)(2,1)}, bf16[2,1,4,3584]{3,2,1,0:T(4,128)(2,1)}) custom-call(s32[2,1,2,4]{3,2,1,0:T(2,128)S(1)} %bitcast.13, f32[2,1,2,4]{3,2,1,0:T(2,128)S(1)} %bitcast.17, s32[2,1,2,4]{3,2,1,0:T(2,128)S(1)} %bitcast.21, f32[2,1,2,4]{3,2,1,0:T(2,128)S(1)} %bitcast.25, bf16[8,8,1792]{2,1,0:T(8,128)(2,1)S(1)} %all_to_all.29.refs_4_, ...), custom_call_target="tpu_custom_call" | custom-call | tf_op jit(solution)/shard_map/pallas_call | solution.py:233
  (9 shorter events, 0.0 us)
Async XLA Ops:
  0.6 16.9 %copy-start = (bf16[1,1,3584,2048]{3,2,1,0:T(8,128)(2,1)S(1)}, bf16[1,1,3584,2048]{3,2,1,0:T(8,128)(2,1)}, u32[]{:S(2)}) copy-start(bf16[1,1,3584,2048]{3,2,1,0:T(8,128)(2,1)} %param.15) | copy-start | bytes 44040196
  0.6 16.9 %copy-start.1 = (bf16[1,1,1024,3584]{3,2,1,0:T(8,128)(2,1)S(1)}, bf16[1,1,1024,3584]{3,2,1,0:T(8,128)(2,1)}, u32[]{:S(2)}) copy-start(bf16[1,1,1024,3584]{3,2,1,0:T(8,128)(2,1)} %param.16) | copy-start | bytes 22020100
  0.7 16.9 %copy-start.2 = (f32[2,1,1,16,2048]{4,3,2,1,0:T(8,128)S(1)}, f32[2,1,1,16,2048]{4,3,2,1,0:T(8,128)}, u32[]{:S(2)}) copy-start(f32[2,1,1,16,2048]{4,3,2,1,0:T(8,128)} %saved_ref.3) | copy-start | bytes 786436
  2.0 35.9 %copy-start.5 = (bf16[1,4,3584]{2,1,0:T(4,128)(2,1)S(1)}, bf16[1,4,3584]{2,1,0:T(4,128)(2,1)}, u32[]{:S(2)}) copy-start(bf16[1,4,3584]{2,1,0:T(4,128)(2,1)} %refs_5_.4) | copy-start | bytes 86020
  2.0 35.9 %copy-start.6 = (bf16[1,4,3584]{2,1,0:T(4,128)(2,1)S(1)}, bf16[1,4,3584]{2,1,0:T(4,128)(2,1)}, u32[]{:S(2)}) copy-start(bf16[1,4,3584]{2,1,0:T(4,128)(2,1)} %refs_6_.3) | copy-start | bytes 86020
  2.0 35.9 %copy-start.7 = (s32[2,1,4,2]{2,3,1,0:T(2,128)S(1)}, s32[2,1,4,2]{2,3,1,0:T(2,128)}, u32[]{:S(2)}) copy-start(s32[2,1,4,2]{2,3,1,0:T(2,128)} %param.17) | copy-start | bytes 196
  2.0 35.9 %copy-start.8 = (f32[2,1,4,2]{2,3,1,0:T(2,128)S(1)}, f32[2,1,4,2]{2,3,1,0:T(2,128)}, u32[]{:S(2)}) copy-start(f32[2,1,4,2]{2,3,1,0:T(2,128)} %param.18) | copy-start | bytes 196
  2.0 35.9 %copy-start.9 = (s32[2,1,4,2]{2,3,1,0:T(2,128)S(1)}, s32[2,1,4,2]{2,3,1,0:T(2,128)}, u32[]{:S(2)}) copy-start(s32[2,1,4,2]{2,3,1,0:T(2,128)} %param.19) | copy-start | bytes 196
  2.0 35.8 %copy-start.10 = (f32[2,1,4,2]{2,3,1,0:T(2,128)S(1)}, f32[2,1,4,2]{2,3,1,0:T(2,128)}, u32[]{:S(2)}) copy-start(f32[2,1,4,2]{2,3,1,0:T(2,128)} %param.20) | copy-start | bytes 196
  2.1 44.9 %copy-start.3 = (bf16[4,3584]{1,0:T(4,128)(2,1)S(1)}, bf16[4,3584]{1,0:T(4,128)(2,1)}, u32[]{:S(2)}) copy-start(bf16[4,3584]{1,0:T(4,128)(2,1)} %refs_6_.5) | copy-start | bytes 86020
  2.1 44.9 %copy-start.4 = (bf16[4,3584]{1,0:T(4,128)(2,1)S(1)}, bf16[4,3584]{1,0:T(4,128)(2,1)}, u32[]{:S(2)}) copy-start(bf16[4,3584]{1,0:T(4,128)(2,1)} %refs_7_.1) | copy-start | bytes 86020
